TPU v7x, 32 devices: a whole 2x2x4 slice. The times are simulated.
32 devices in a mesh: groups: 2 (over y), tok: 4 (over x, core), voc: 4 (over z).
Axes of the slice: x: 2, y: 2, z: 4, core: 2. Of those that a mesh axis runs over, the one named last changes fastest.
Arguments:
- hidden: bfloat16 [4096, 2048], P(('groups', 'tok', 'voc')), parts along dimension 0, may hold values from -210 to 210
- head: bfloat16 [163840, 2048], P(('tok', 'voc')), may hold values from -0.125 to 0.125
- block_ids: int32 [4096, 8], P(('groups', 'tok', 'voc')), parts along dimension 0, may hold values from 0 to 1279, all different within a row; in each aligned block of 128 rows (0 to 127, 128 to 255, ...) at most 2 rows name the same one
- live_counts: int32 [4096], P(('groups', 'tok', 'voc')), parts along dimension 0, may hold values from 1 to 8, as said below
- teacher: bfloat16 [4096, 8, 128], P(('groups', 'tok', 'voc')), parts along dimension 0, may hold values from -15 to 215
Outputs:
- hidden_grad: bfloat16 [4096, 2048], P(('groups', 'tok', 'voc')), parts along dimension 0
- head_grad: bfloat16 [327680, 2048], P(('groups', 'tok', 'voc')), parts along dimension 0
- token_loss: float32 [4096], P(('groups', 'tok', 'voc')), parts along dimension 0
There are 2 independent parts, one for each index of `groups`. A program takes and returns all parts, laid end to end along the dimension named above; an argument that names none is the same for every part. Nothing has to cross between parts.
Inputs may be any that keep to these rules, and one draw needn't show every extreme that they name: `block_ids`: each token lists 8 different blocks. Among the list entries of one device's 128 tokens (aligned runs), no block is named more than 2 times, live or not, and some block is named exactly 2 times on some devices. Entries 0 to live_counts - 1 of a token's list are live; the others carry no weight. Some device has all of its tokens' entries live.
All inputs are finite; a program needn't handle non-finite values.
Results may differ from a plain program's by a relative error of at most 0.0059.
Values may be sent and summed in bfloat16 or wider, within the bound.
No kernel may reach another device: no remote copies, remote signals or barrier semaphores. Data moves between devices by JAX's collectives and lax.ppermute only.
A program may use at most 256 MiB of HBM per device.

v0:
```python
import jax
import jax.numpy as jnp
from jax import lax
from jax.sharding import PartitionSpec as P

BLOCK = 128
C = 2


def log_softmax_rows(values):
    top = jnp.max(values, axis=-1, keepdims=True)
    return values - top - jnp.log(jnp.sum(jnp.exp(values - top), axis=-1, keepdims=True))


def send_out(send_hidden, send_teacher, send_live, devices_all, bucket_rows):
    width = send_hidden.shape[-1]
    got_hidden, got_teacher, got_live = (
        lax.all_to_all(
            send_hidden.reshape(devices_all, bucket_rows, width),
            ("tok", "voc"),
            split_axis=0,
            concat_axis=0,
            tiled=True,
        ),
        lax.all_to_all(
            send_teacher.reshape(devices_all, bucket_rows, BLOCK),
            ("tok", "voc"),
            split_axis=0,
            concat_axis=0,
            tiled=True,
        ),
        lax.all_to_all(
            send_live.reshape(devices_all, bucket_rows),
            ("tok", "voc"),
            split_axis=0,
            concat_axis=0,
            tiled=True,
        ),
    )
    return (got_hidden, got_teacher, got_live)


def send_back(slot_grad, divergence, devices_all, bucket_rows):
    width = slot_grad.shape[-1]
    back_grad, back_loss = (
        lax.all_to_all(
            slot_grad.reshape(devices_all, bucket_rows, width),
            ("tok", "voc"),
            split_axis=0,
            concat_axis=0,
            tiled=True,
        ),
        lax.all_to_all(
            divergence.reshape(devices_all, bucket_rows),
            ("tok", "voc"),
            split_axis=0,
            concat_axis=0,
            tiled=True,
        ),
    )
    return (
        back_grad.reshape(devices_all * bucket_rows, width),
        back_loss.reshape(devices_all * bucket_rows),
    )


def on_device(hidden, head, block_ids, live_counts, teacher):
    devices_all = lax.axis_size(("tok", "voc"))
    tok_rows, list_width = block_ids.shape
    width = hidden.shape[1]
    local_blocks = head.shape[0] // BLOCK
    block_total = local_blocks * devices_all
    slot_total = tok_rows * list_width
    bucket_rows = local_blocks * C
    live_total = lax.psum(jnp.sum(live_counts), ("tok", "voc"))
    scale = jnp.float32(tok_rows * devices_all) / live_total.astype(jnp.float32)
    flat_ids = block_ids.reshape(slot_total)
    position = jnp.arange(slot_total, dtype=jnp.int32)
    earlier = (flat_ids[:, None] == flat_ids[None, :]) & (position[:, None] > position[None, :])
    ranks = jnp.sum(earlier, axis=1, dtype=jnp.int32)
    target_rows = flat_ids * C + ranks
    live = (jnp.arange(list_width, dtype=jnp.int32)[None, :] < live_counts[:, None]).reshape(
        slot_total
    )
    all_rows = block_total * C
    send_hidden = (
        jnp.zeros((all_rows, width), jnp.bfloat16)
        .at[target_rows]
        .set(jnp.repeat(hidden, list_width, axis=0))
    )
    send_teacher = (
        jnp.zeros((all_rows, BLOCK), jnp.bfloat16)
        .at[target_rows]
        .set(teacher.reshape(slot_total, BLOCK))
    )
    send_live = jnp.zeros((all_rows,), jnp.bfloat16).at[target_rows].set(live.astype(jnp.bfloat16))
    got_hidden, got_teacher, got_live = send_out(
        send_hidden, send_teacher, send_live, devices_all, bucket_rows
    )
    got_hidden = got_hidden.reshape(devices_all, local_blocks, C, width)
    block_weights = head.reshape(local_blocks, BLOCK, width)
    logits = jnp.einsum(
        "sbcd,bvd->sbcv", got_hidden, block_weights, preferred_element_type=jnp.float32
    )
    student_log = log_softmax_rows(logits)
    teacher_log = log_softmax_rows(
        got_teacher.reshape(devices_all, local_blocks, C, BLOCK).astype(jnp.float32)
    )
    teacher_prob = jnp.exp(teacher_log)
    weight = got_live.reshape(devices_all, local_blocks, C).astype(jnp.float32) * scale
    divergence = (weight * jnp.sum(teacher_prob * (teacher_log - student_log), axis=-1)).astype(
        jnp.bfloat16
    )
    grad_logits = (BLOCK * weight[..., None] * (jnp.exp(student_log) - teacher_prob)).astype(
        jnp.bfloat16
    )
    slot_grad = jnp.einsum(
        "sbcv,bvd->sbcd", grad_logits, block_weights, preferred_element_type=jnp.float32
    ).astype(jnp.bfloat16)
    summed = jnp.einsum(
        "sbcv,sbcd->bvd", grad_logits, got_hidden, preferred_element_type=jnp.float32
    )
    head_grad = summed.astype(jnp.bfloat16).reshape(local_blocks * BLOCK, width)
    back_grad, back_loss = send_back(slot_grad, divergence, devices_all, bucket_rows)
    token_terms = back_grad[target_rows].astype(jnp.float32).reshape(tok_rows, list_width, width)
    hidden_grad = jnp.sum(token_terms, axis=1).astype(jnp.bfloat16)
    token_loss = jnp.sum(
        back_loss[target_rows].astype(jnp.float32).reshape(tok_rows, list_width), axis=1
    )
    return (hidden_grad, head_grad, token_loss)


def solution(mesh):
    placed = (
        P(("groups", "tok", "voc"), None),
        P(("tok", "voc"), None),
        P(("groups", "tok", "voc"), None),
        P(("groups", "tok", "voc")),
        P(("groups", "tok", "voc"), None, None),
    )
    return jax.shard_map(
        on_device,
        mesh=mesh,
        in_specs=placed,
        out_specs=(
            P(("groups", "tok", "voc"), None),
            P(("groups", "tok", "voc"), None),
            P(("groups", "tok", "voc")),
        ),
        check_vma=False,
    )
```

profile of v0, /device:TPU:0, one launch (start us, length us, event | category | flops | bytes accessed | tf_op | source)
XLA Modules:
  0.0 623.9 jit_solution(11456917392340018109)
XLA Ops:
  0.6 0.7 broadcast_multiply_fusion
  1.4 0.8 copy.55
  2.2 0.7 fusion.14
  3.3 0.5 convert_reduce_fusion
  3.9 7.6 %scatter_custom_fusion = bf16[2560]{0:T(1024)(128)(2,1)S(1)} fusion(s32[1024]{0:T(1024)S(1)} %bitcast.56, bf16[1024]{0:T(1024)(128)(2,1)S(1)} %reshape.167, bf16[]{:T(256)} %constant.9.clone.1), kind=kCustom, calls=%fused_computation.36 | custom fusion | bytes 5122 | tf_op jit(solution)/shard_map/scatter | solution.py:96
  11.5 0.7 all_to_all.25
  12.2 7.4 %all-to-all-start = ((bf16[16,1,160]{2,1,0:T(2,128)(2,1)}), bf16[16,1,160]{2,1,0:T(2,128)(2,1)S(1)}, u32[]{:S(2)}, u32[]{:S(2)}) async-start(bf16[16,1,160]{2,1,0:T(2,128)(2,1)} %all_to_all.25), calls=%async_computation | async-start | bytes 32768 | tf_op jit(solution)/shard_map/all_to_all | solution.py:32
  19.5 4.4 scatter_custom_fusion.2
  23.9 2.0 all-to-all-done
  26.0 4.5 all-to-all-start.2
  30.5 12.6 %scatter_custom_fusion.1 = bf16[2560,2048]{1,0:T(8,128)(2,1)} fusion(s32[1024]{0:T(1024)S(1)} %bitcast.58, bf16[]{:T(256)} %constant.9.clone.1, bf16[128,2048]{1,0:T(8,128)(2,1)S(1)} %copy-done), kind=kCustom, calls=%fused_computation.9 | custom fusion | bytes 11010050 | tf_op jit(solution)/shard_map/scatter | solution.py:89
  43.1 5.9 all-to-all-done.2
  49.0 5.0 all-to-all-start.1
  54.0 0.6 reduce_sum.72
  54.6 232.2 %psum.7 = s32[]{:T(128)} all-reduce(s32[]{:T(128)} %reduce_sum.72), channel_id=1, replica_groups=mesh['groups'=2,'tok'=4,'voc'=4] {'tok','voc'}, use_global_device_ids=true, to_apply=%region_3.0 | all-reduce | flops 1 | bytes 8 | tf_op jit(solution)/shard_map/psum | solution.py:75
  287.6 0.5 reduce_max.28
  288.2 1.0 exponential_reduce_fusion
  289.4 1.3 copy.60
  290.6 13.8 %copy.59 = bf16[16,160,2048]{2,0,1:T(8,128)(2,1)} copy(bf16[16,160,2048]{2,1,0:T(8,128)(2,1)} %all-to-all-done.1) | data formatting | bytes 20971520 | tf_op jit(solution)/shard_map/all_to_all | solution.py:18
  304.4 20.9 %fusion.7 = f32[16,80,2,128]{3,0,2,1:T(8,128)S(1)} fusion(bf16[16,80,2,2048]{3,0,2,1:T(8,128)(2,1)} %bitcast.46, bf16[80,128,2048,1]{2,1,3,0:T(8,128)(2,1)} %bitcast.44), kind=kOutput, calls=%fused_computation.17 | convolution fusion | flops 1342507648 | bytes 53739520 | tf_op jit(solution)/shard_map/sub | solution.py:12
  325.3 5.8 multiply_reduce_fusion
  331.2 0.6 copy.65
  331.8 3.7 all-to-all-start.4
  335.5 18.6 %convolution_convert_fusion = bf16[80,16,2,2048]{3,1,2,0:T(8,128)(2,1)} fusion(bf16[16,80,2,128]{3,0,2,1:T(8,128)(2,1)S(1)} %get-tuple-element.4, bf16[80,128,2048,1]{2,1,3,0:T(8,128)(2,1)} %bitcast.45), kind=kOutput, calls=%fused_computation.8 | convolution fusion | flops 1347420160 | bytes 53084160 | tf_op jit(solution)/shard_map/sbcv,bvd->sbcd/dot_general | solution.py:117
  354.2 13.8 %copy.63 = bf16[16,160,2048]{2,1,0:T(8,128)(2,1)} copy(bf16[16,160,2048]{2,0,1:T(8,128)(2,1)} %bitcast.49) | data formatting | bytes 20971520 | tf_op jit(solution)/shard_map/reshape | solution.py:47
  367.9 6.4 %all-to-all-start.3 = ((bf16[16,160,2048]{2,1,0:T(8,128)(2,1)}), bf16[16,160,2048]{2,1,0:T(8,128)(2,1)}, u32[]{:S(2)}, u32[]{:S(2)}) async-start(bf16[16,160,2048]{2,1,0:T(8,128)(2,1)} %copy.63), calls=%async_computation.3 | async-start | bytes 20971520 | tf_op jit(solution)/shard_map/all_to_all | solution.py:46
  374.3 20.2 %bitcast_convert_fusion = bf16[80,128,2048]{2,1,0:T(8,128)(2,1)} fusion(bf16[16,80,2,128]{3,0,2,1:T(8,128)(2,1)S(1)} %get-tuple-element.4, bf16[16,80,2,2048]{3,0,2,1:T(8,128)(2,1)} %bitcast.47), kind=kOutput, calls=%fused_computation.7 | convolution fusion | flops 1363148800 | bytes 53084160 | tf_op jit(solution)/shard_map/sbcv,sbcd->bvd/dot_general | solution.py:120
  394.7 6.8 %gather_fusion.1 = bf16[1024]{0:T(1024)(128)(2,1)S(1)} fusion(bf16[2560]{0:T(1024)(128)(2,1)S(1)} %reshape.142, s32[1024]{0:T(1024)S(1)} %broadcast_clamp_fusion), kind=kCustom, calls=%fused_computation.1 | custom fusion | bytes 8192 | tf_op jit(solution)/shard_map/gather | solution.py:128
  401.5 0.6 reduce_sum.78
  402.2 201.4 %all-to-all-done.3 = bf16[16,160,2048]{2,1,0:T(8,128)(2,1)} async-done(((bf16[16,160,2048]{2,1,0:T(8,128)(2,1)}), bf16[16,160,2048]{2,1,0:T(8,128)(2,1)}, u32[]{:S(2)}, u32[]{:S(2)}) %all-to-all-start.3) | async-done | bytes 10485792 | tf_op jit(solution)/shard_map/all_to_all | solution.py:46
  603.5 14.2 %gather_fusion = bf16[1024,2048]{1,0:T(8,128)(2,1)} fusion(bf16[2560,2048]{1,0:T(8,128)(2,1)} %bitcast.17, s32[1024]{0:T(1024)S(1)} %broadcast_clamp_fusion), kind=kCustom, calls=%fused_computation | custom fusion | bytes 8392704 | tf_op jit(solution)/shard_map/gather | solution.py:125
  617.8 5.9 bitcast_reduce_fusion
  (25 shorter events, 1.1 us)
Async XLA Ops:
  0.6 29.8 %copy-start = (bf16[128,2048]{1,0:T(8,128)(2,1)S(1)}, bf16[128,2048]{1,0:T(8,128)(2,1)}, u32[]{:S(2)}) copy-start(bf16[128,2048]{1,0:T(8,128)(2,1)} %param.5) | copy-start | bytes 1572868
  12.2 13.8 %all-to-all-start = ((bf16[16,1,160]{2,1,0:T(2,128)(2,1)}), bf16[16,1,160]{2,1,0:T(2,128)(2,1)S(1)}, u32[]{:S(2)}, u32[]{:S(2)}) async-start(bf16[16,1,160]{2,1,0:T(2,128)(2,1)} %all_to_all.25), calls=%async_computation | async-start | bytes 32768 | tf_op jit(solution)/shard_map/all_to_all | solution.py:32
  26.0 23.0 %all-to-all-start.2 = ((bf16[16,160,128]{2,1,0:T(8,128)(2,1)}), bf16[16,160,128]{2,1,0:T(8,128)(2,1)S(1)}, u32[]{:S(2)}, u32[]{:S(2)}) async-start(bf16[16,160,128]{2,1,0:T(8,128)(2,1)} %bitcast.11), calls=%async_computation.2 | async-start | bytes 1310720 | tf_op jit(solution)/shard_map/all_to_all | solution.py:25
  49.0 5.0 copy-start.2
  49.0 241.7 %all-to-all-start.1 = ((bf16[16,160,2048]{2,1,0:T(8,128)(2,1)}), bf16[16,160,2048]{2,1,0:T(8,128)(2,1)}, u32[]{:S(2)}, u32[]{:S(2)}) async-start(bf16[16,160,2048]{2,1,0:T(8,128)(2,1)} %bitcast.50), calls=%async_computation.1 | async-start | bytes 20971520 | tf_op jit(solution)/shard_map/all_to_all | solution.py:18
  331.8 36.1 %all-to-all-start.4 = ((bf16[16,1,160]{2,1,0:T(2,128)(2,1)}), bf16[16,1,160]{2,1,0:T(2,128)(2,1)S(1)}, u32[]{:S(2)}, u32[]{:S(2)}) async-start(bf16[16,1,160]{2,1,0:T(2,128)(2,1)} %copy.65), calls=%async_computation.4 | async-start | bytes 32768 | tf_op jit(solution)/shard_map/all_to_all | solution.py:53
  367.9 235.6 %all-to-all-start.3 = ((bf16[16,160,2048]{2,1,0:T(8,128)(2,1)}), bf16[16,160,2048]{2,1,0:T(8,128)(2,1)}, u32[]{:S(2)}, u32[]{:S(2)}) async-start(bf16[16,160,2048]{2,1,0:T(8,128)(2,1)} %copy.63), calls=%async_computation.3 | async-start | bytes 20971520 | tf_op jit(solution)/shard_map/all_to_all | solution.py:46
  603.5 20.1 %copy-start.1 = (bf16[128,2048]{1,0:T(8,128)(2,1)S(1)}, bf16[128,2048]{1,0:T(8,128)(2,1)}, u32[]{:S(2)}) copy-start(bf16[128,2048]{1,0:T(8,128)(2,1)} %param.5) | copy-start | bytes 1572868
where the time goes:
time: 630 us; the launch traced here: 624 us
  blocking collectives  232 us (37%)
  waiting for transfers between devices  209 us (33%)
  local copies, waits for them, and re-layouts  77.5 us (12%)
  matrix products  59.7 us (9%)
  starting transfers between devices  26.9 us (4%)
  other arithmetic  16.5 us (3%)
    psum x1, blocking collectives, on_device(): live_total = lax.psum(jnp.sum(live_counts), ('tok', 'voc'))  232 us
    all_to_all x1, waiting for transfers between devices, send_back(): lax.all_to_all(slot_grad.reshape(devices_all, bucket_rows, width), ('tok'...  201 us
    sub x1, matrix products, log_softmax_rows(): values - top  20.9 us
    dot_general x1, matrix products, on_device(): jnp.einsum('sbcv,sbcd->bvd', grad_logits, got_hidden, preferred_element_t...  20.2 us
    dot_general x1, matrix products, on_device(): jnp.einsum('sbcv,bvd->sbcd', grad_logits, block_weights, preferred_elemen...  18.6 us
    gather x1, local copies, waits for them, and re-layouts, on_device(): back_grad[target_rows].astype(jnp.float32)  14.2 us
    all_to_all x1, local copies, waits for them, and re-layouts, send_out(): lax.all_to_all(send_hidden.reshape(devices_all, bucket_rows, width), ('to...  13.8 us
    reshape x1, local copies, waits for them, and re-layouts, send_back(): slot_grad.reshape(devices_all, bucket_rows, width)  13.8 us
  transfers between devices with their start and end apart: 5, of which 3 were waited for; matrix products, arithmetic and copies ran while one was open for 13% of the time, Pallas kernels for 0%

commit v1 on v0

v1 whole, which is shorter than its diff:
```python
import jax
import jax.numpy as jnp
from jax import lax
from jax.sharding import PartitionSpec as P

BLOCK = 128
C = 2
AXES = ("tok", "voc")


def log_softmax_rows(values):
    top = jnp.max(values, axis=-1, keepdims=True)
    return values - top - jnp.log(jnp.sum(jnp.exp(values - top), axis=-1, keepdims=True))


def on_device(hidden, head, block_ids, live_counts, teacher):
    devices = lax.axis_size(AXES)
    tokens, list_width = block_ids.shape
    width = hidden.shape[1]
    local_blocks = head.shape[0] // BLOCK
    entries = tokens * list_width
    bucket = local_blocks * C
    flat_ids = block_ids.reshape(entries)
    position = jnp.arange(entries, dtype=jnp.int32)
    earlier = (flat_ids[:, None] == flat_ids[None, :]) & (position[:, None] > position[None, :])
    ranks = jnp.sum(earlier, axis=1, dtype=jnp.int32)
    live = (jnp.arange(list_width, dtype=jnp.int32)[None, :] < live_counts[:, None]).reshape(entries)
    rows = jnp.where(live, flat_ids * C + ranks, -1)

    all_hidden = lax.all_gather(hidden, AXES, axis=0)
    all_rows = lax.all_gather(rows, AXES, axis=0)
    slots = jnp.arange(devices * bucket, dtype=jnp.int32)
    place = (slots[:, None] == rows[None, :]).astype(jnp.bfloat16)
    send_teacher = jnp.dot(
        place, teacher.reshape(entries, BLOCK), preferred_element_type=jnp.float32
    ).astype(jnp.bfloat16)
    got_teacher = lax.all_to_all(
        send_teacher.reshape(devices, bucket, BLOCK), AXES, split_axis=0, concat_axis=0, tiled=True
    )

    me = lax.axis_index(AXES)
    live_total = jnp.sum(all_rows >= 0, dtype=jnp.int32)
    scale = jnp.float32(tokens * devices) / live_total.astype(jnp.float32)
    own = (all_rows - me * bucket).reshape(devices, 1, tokens, list_width)
    here = jnp.arange(bucket, dtype=jnp.int32)[None, :, None, None]
    pick = jnp.any(own == here, axis=-1)
    weight = jnp.where(jnp.any(pick, axis=-1), scale, jnp.float32(0.0))
    pick = pick.astype(jnp.bfloat16)

    got_hidden = jnp.einsum("sgt,std->sgd", pick, all_hidden, preferred_element_type=jnp.float32)
    got_hidden = got_hidden.astype(jnp.bfloat16).reshape(devices, local_blocks, C, width)
    blocks = head.reshape(local_blocks, BLOCK, width)
    logits = jnp.einsum("sbcd,bvd->sbcv", got_hidden, blocks, preferred_element_type=jnp.float32)
    student_log = log_softmax_rows(logits)
    teacher_log = log_softmax_rows(
        got_teacher.reshape(devices, local_blocks, C, BLOCK).astype(jnp.float32)
    )
    teacher_prob = jnp.exp(teacher_log)
    weight = weight.reshape(devices, local_blocks, C)
    divergence = (weight * jnp.sum(teacher_prob * (teacher_log - student_log), axis=-1)).astype(
        jnp.bfloat16
    )
    grad_logits = (BLOCK * weight[..., None] * (jnp.exp(student_log) - teacher_prob)).astype(
        jnp.bfloat16
    )
    slot_grad = jnp.einsum(
        "sbcv,bvd->sbcd", grad_logits, blocks, preferred_element_type=jnp.float32
    ).astype(jnp.bfloat16)
    part = jnp.einsum(
        "sgt,sgd->std",
        pick,
        slot_grad.reshape(devices, bucket, width),
        preferred_element_type=jnp.float32,
    ).astype(jnp.bfloat16)
    hidden_grad = lax.psum_scatter(
        part.reshape(devices * tokens, width), AXES, scatter_dimension=0, tiled=True
    )
    summed = jnp.einsum(
        "sbcv,sbcd->bvd", grad_logits, got_hidden, preferred_element_type=jnp.float32
    )
    head_grad = summed.astype(jnp.bfloat16).reshape(local_blocks * BLOCK, width)
    loss_part = jnp.sum(
        pick.astype(jnp.float32) * divergence.astype(jnp.float32).reshape(devices, bucket, 1), axis=1
    )
    token_loss = lax.psum_scatter(
        loss_part.reshape(devices * tokens), AXES, scatter_dimension=0, tiled=True
    )
    return hidden_grad, head_grad, token_loss


def solution(mesh):
    tokens_on = ("groups", "tok", "voc")
    return jax.shard_map(
        on_device,
        mesh=mesh,
        in_specs=(
            P(tokens_on, None),
            P(AXES, None),
            P(tokens_on, None),
            P(tokens_on),
            P(tokens_on, None, None),
        ),
        out_specs=(P(tokens_on, None), P(tokens_on, None), P(tokens_on)),
        check_vma=False,
    )
```

time: 630 us -> 334 us (0.53)
  waiting for transfers between devices: 209 us -> 50.3 us
  blocking collectives: 232 us -> 87.7 us
  local copies, waits for them, and re-layouts: 77.5 us -> 18.9 us
  other arithmetic: 16.5 us -> 56.9 us
  matrix products: 59.7 us -> 93.6 us
  starting transfers between devices: 26.9 us -> 7.44 us
  between operations: 1.76 us -> 15.9 us
    psum x1 -> x0, blocking collectives: 232 us -> none  [on_device(): live_total = lax.psum(jnp.sum(live_counts), ('tok', 'voc'))]
    all_to_all x5 -> x1, waiting for transfers between devices: 209 us -> 0.01 us  [on_device(): lax.all_to_all(send_teacher.reshape(devices, bucket, BLOCK), AXES, split_...]
    all_gather x0 -> x1, blocking collectives: none -> 57.3 us  [on_device(): all_rows = lax.all_gather(rows, AXES, axis=0)]
    reduce_scatter x0 -> x1, waiting for transfers between devices: none -> 49.6 us  [on_device(): lax.psum_scatter(part.reshape(devices * tokens, width), AXES, scatter_dim...]
    reduce_or x0 -> x1, other arithmetic: none -> 47.1 us  [on_device(): weight = jnp.where(jnp.any(pick, axis=-1), scale, jnp.float32(0.0))]
    dot_general x1 -> x4, matrix products: 18.6 us -> 52.4 us  [the longest x1 20.3 us: on_device(): jnp.einsum('sgt,sgd->std', pick, slot_grad.reshape(devices, bucket, width...]
    unnamed x0 -> x1, blocking collectives: none -> 30.4 us
    scatter x3 -> x0, local copies, waits for them, and re-layouts: 24.6 us -> none  [the longest x1 12.6 us: on_device(): send_hidden = jnp.zeros((all_rows, width), jnp.bfloat16).at[target_rows]....]
  transfers between devices with their start and end apart: 5 -> 3, of which waited for: 3 -> 1; matrix products, arithmetic and copies ran while one was open for 13% -> 24% of each run, Pallas kernels for 0% -> 0%
where the time goes in v1:
time: 334 us; the launch traced here: 331 us
  matrix products  93.6 us (28%)
  blocking collectives  87.7 us (26%)
  other arithmetic  56.9 us (17%)
  waiting for transfers between devices  50.3 us (15%)
  local copies, waits for them, and re-layouts  18.9 us (6%)
  between operations  15.9 us (5%)
  starting transfers between devices  7.44 us (2%)
    all_gather x1, blocking collectives, on_device(): all_rows = lax.all_gather(rows, AXES, axis=0)  57.3 us
    reduce_scatter x1, waiting for transfers between devices, on_device(): lax.psum_scatter(part.reshape(devices * tokens, width), AXES, scatter_dim...  49.6 us
    reduce_or x1, other arithmetic, on_device(): weight = jnp.where(jnp.any(pick, axis=-1), scale, jnp.float32(0.0))  47.1 us
    unnamed x1, blocking collectives  30.4 us
    sub x1, matrix products, log_softmax_rows(): values - top  20.9 us
    dot_general x1, matrix products, on_device(): jnp.einsum('sgt,sgd->std', pick, slot_grad.reshape(devices, bucket, width...  20.3 us
    dot_general x1, matrix products, on_device(): jnp.einsum('sbcv,sbcd->bvd', grad_logits, got_hidden, preferred_element_t...  20.3 us
    dot_general x1, matrix products, on_device(): jnp.einsum('sbcv,bvd->sbcd', grad_logits, blocks, preferred_element_type=...  18.8 us
  transfers between devices with their start and end apart: 3, of which 1 were waited for; matrix products, arithmetic and copies ran while one was open for 24% of the time, Pallas kernels for 0%

profile of v1, /device:TPU:0, one launch (start us, length us, event | category | flops | bytes accessed | tf_op | source)
XLA Modules:
  0.0 330.7 jit_solution(17217871023615298428)
XLA Ops:
  7.2 0.7 all-gather.4.cloned.1.call-update
  7.9 0.7 iota_compare_fusion.6
  8.7 0.1 lt.32
  8.8 0.8 copy.87
  9.6 0.5 convert_reduce_fusion
  10.2 2.7 fusion.12
  12.9 7.4 %all-to-all-start = ((bf16[16,160,128]{2,1,0:T(8,128)(2,1)}), bf16[16,160,128]{2,1,0:T(8,128)(2,1)S(1)}, u32[]{:S(2)}, u32[]{:S(2)}) async-start(bf16[16,160,128]{2,1,0:T(8,128)(2,1)} %bitcast.10), calls=%async_computation | async-start | bytes 1310720 | tf_op jit(solution)/shard_map/all_to_all | solution.py:37
  20.4 0.1 lt.31
  20.5 0.1 copy.86
  20.7 57.3 %all-gather.1 = s32[16,1,1024]{2,1,0:T(1,128)S(1)} all-gather(s32[1,1,1024]{2,1,0:T(1,128)S(1)} %select_bitcast_fusion), channel_id=1, replica_groups=mesh['groups'=2,'tok'=4,'voc'=4] {'tok','voc'}, dimensions={0}, use_global_device_ids=true | all-gather | bytes 69632 | tf_op jit(solution)/shard_map/all_gather | solution.py:31
  78.0 0.8 fusion.18
  79.4 0.2 copy.89
  79.6 0.2 copy.90
  79.9 47.1 %fusion.4 = (pred[16,160]{1,0:T(8,128)(4,1)S(1)}, pred[16,160,128]{2,1,0:T(8,128)(4,1)S(1)}) fusion(s32[16,128,8]{1,2,0:T(8,128)S(1)} %copy.90), kind=kLoop, calls=%fused_computation.7 | loop fusion | flops 7534080 | bytes 395776 | tf_op jit(solution)/shard_map/reduce_or | solution.py:47
  127.0 0.1 copy.91
  127.1 0.5 reduce_max.28
  127.6 0.1 copy.94
  127.7 1.0 exponential_reduce_fusion
  128.8 1.3 copy.93
  130.1 10.5 %convolution_convert_fusion = bf16[16,160,2048]{2,1,0:T(8,128)(2,1)} fusion(pred[16,160,128]{2,1,0:T(8,128)(4,1)S(1)} %get-tuple-element.4, bf16[16,128,2048]{2,1,0:T(8,128)(2,1)} %bitcast.50), kind=kOutput, calls=%fused_computation.10 | convolution fusion | flops 1347420160 | bytes 19202048 | tf_op jit(solution)/shard_map/sgt,std->sgd/dot_general | solution.py:50
  140.6 13.8 %copy.101 = bf16[16,160,2048]{2,0,1:T(8,128)(2,1)} copy(bf16[16,160,2048]{2,1,0:T(8,128)(2,1)} %convolution_convert_fusion) | data formatting | bytes 20971520 | tf_op jit(solution)/shard_map/reshape | solution.py:51
  154.4 20.9 %fusion.13 = f32[16,80,2,128]{3,0,2,1:T(8,128)S(1)} fusion(bf16[16,80,2,2048]{3,0,2,1:T(8,128)(2,1)} %bitcast.45, bf16[80,128,2048,1]{2,1,3,0:T(8,128)(2,1)} %bitcast.43), kind=kOutput, calls=%fused_computation.18 | convolution fusion | flops 1342507648 | bytes 53739520 | tf_op jit(solution)/shard_map/sub | solution.py:13
  175.3 5.8 %multiply_reduce_fusion.1 = (f32[16,80,2]{0,2,1:T(2,128)S(1)}, bf16[16,80,2,128]{3,0,2,1:T(8,128)(2,1)S(1)}) fusion(f32[16,80,2,128]{3,0,2,1:T(8,128)} %bitcast.52, f32[16,80,2]{0,2,1:T(2,128)S(1)} %bitcast.56, f32[16,80,2]{0,2,1:T(2,128)S(1)} %bitcast.55, f32[16,80,2]{0,2,1:T(2,128)S(1)} %bitcast.54, f32[16,80,2,128]{3,0,2,1:T(8,128)S(1)} %fusion.13), kind=kOutput, calls=%fused_computation.23 | output fusion | flops 2949247 | bytes 3317760 | tf_op jit(solution)/shard_map/reduce_sum | solution.py:13
  181.1 18.8 %convolution_convert_fusion.1 = bf16[80,16,2,2048]{3,1,2,0:T(8,128)(2,1)} fusion(bf16[16,80,2,128]{3,0,2,1:T(8,128)(2,1)S(1)} %get-tuple-element.6, bf16[80,128,2048,1]{2,1,3,0:T(8,128)(2,1)} %bitcast.44), kind=kOutput, calls=%fused_computation.11 | convolution fusion | flops 1347420160 | bytes 53084160 | tf_op jit(solution)/shard_map/sbcv,bvd->sbcd/dot_general | solution.py:66
  199.9 20.3 %fusion.7 = bf16[16,128,2048]{2,1,0:T(8,128)(2,1)} fusion(pred[16,160,128]{2,1,0:T(8,128)(4,1)S(1)} %get-tuple-element.4, bf16[16,160,2048]{2,0,1:T(8,128)(2,1)} %bitcast.47), kind=kOutput, calls=%fused_computation.12 | convolution fusion | flops 1346371584 | bytes 19202048 | tf_op jit(solution)/shard_map/sgt,sgd->std/dot_general | solution.py:69
  220.3 0.6 copy-done.3
  220.9 0.6 dynamic-slice
  222.2 0.4 multiply_reduce_fusion
  222.7 30.4 %all-reduce = f32[2048]{0:T(1024)S(1)} all-reduce(f32[2048]{0:T(1024)S(1)} %bitcast.57), channel_id=4, replica_groups=mesh['groups'=2,'tok'=4,'voc'=4] {'tok','voc'}, use_global_device_ids=true, to_apply=%region_11.12.clone | all-reduce | flops 2048 | bytes 16384
  253.1 0.6 dynamic-slice.1
  253.7 20.3 %bitcast_convert_fusion = bf16[80,128,2048]{2,1,0:T(8,128)(2,1)} fusion(bf16[16,80,2,128]{3,0,2,1:T(8,128)(2,1)S(1)} %get-tuple-element.6, bf16[16,80,2,2048]{3,0,2,1:T(8,128)(2,1)} %bitcast.46), kind=kOutput, calls=%fused_computation.2 | convolution fusion | flops 1363148800 | bytes 53084160 | tf_op jit(solution)/shard_map/sbcv,sbcd->bvd/dot_general | solution.py:78
  274.0 49.6 %reduce-scatter.2.cloned.1.call-done = bf16[128,2048]{1,0:T(8,128)(2,1)} async-done(((bf16[2048,2048]{1,0:T(8,128)(2,1)}), bf16[128,2048]{1,0:T(8,128)(2,1)}) %reduce-scatter.2.cloned.1.call-update) | async-done | bytes 524304 | tf_op jit(solution)/shard_map/reduce_scatter | solution.py:75
  (24 shorter events, 0.5 us)
Async XLA Ops:
  7.2 3.0 copy-start
  7.2 122.9 %all-gather.4.cloned.1.call-start = ((), (), s32[]{:S(2)}) async-start(), calls=%async_computation.3 | async-start | bytes 8912896 | tf_op jit(solution)/shard_map/all_gather | solution.py:30
  10.2 10.2 %copy-start.2 = (s32[128,8]{0,1:T(8,128)S(1)}, s32[128,8]{0,1:T(8,128)}, u32[]{:S(2)}) copy-start(s32[128,8]{0,1:T(8,128)} %param.7) | copy-start | bytes 12292
  12.9 114.2 %all-to-all-start = ((bf16[16,160,128]{2,1,0:T(8,128)(2,1)}), bf16[16,160,128]{2,1,0:T(8,128)(2,1)S(1)}, u32[]{:S(2)}, u32[]{:S(2)}) async-start(bf16[16,160,128]{2,1,0:T(8,128)(2,1)} %bitcast.10), calls=%async_computation | async-start | bytes 1310720 | tf_op jit(solution)/shard_map/all_to_all | solution.py:37
  20.3 303.3 %reduce-scatter.2.cloned.1.call-start = ((), (), s32[]{:S(2)}) async-start(), calls=%async_computation.2 | async-start | bytes 8912896 | tf_op jit(solution)/shard_map/reduce_scatter | solution.py:75
  220.3 0.7 copy-start.3
  253.7 69.9 %copy-start.1 = (bf16[128,8,128]{2,1,0:T(8,128)(2,1)S(1)}, bf16[128,8,128]{2,1,0:T(8,128)(2,1)}, u32[]{:S(2)}) copy-start(bf16[128,8,128]{2,1,0:T(8,128)(2,1)} %param.9) | copy-start | bytes 786436
Sparse Core Ops, SparseCore 0:
  10.2 91.2 all-gather.3
  220.4 103.1 reduce-scatter.1

commit v2 on v1

v2 whole, which is shorter than its diff:
```python
import functools

import jax
import jax.numpy as jnp
import numpy as np
from jax import lax
from jax.experimental import pallas as pl
from jax.experimental.pallas import tpu as pltpu
from jax.sharding import Mesh
from jax.sharding import PartitionSpec as P

BLOCK = 128
LANES = 128
C = 2
QUAD = 4
ROWS = QUAD * C
COLS = 256
ALL = ("x", "core", "voc")
CHIPS = ("x", "voc")
RING_MOST = 8
VMEM_LIMIT = 52 * 1024 * 1024
NT = (((1,), (1,)), ((), ()))


def call(kernel, name, grid, ins, outs, shapes, flops, moved, scratch=(), aliases=None):
    return pl.pallas_call(
        kernel,
        grid=grid,
        in_specs=ins,
        out_specs=outs,
        out_shape=shapes,
        scratch_shapes=scratch,
        input_output_aliases=aliases or {},
        compiler_params=pltpu.CompilerParams(
            dimension_semantics=("arbitrary",) * len(grid), vmem_limit_bytes=VMEM_LIMIT
        ),
        cost_estimate=pl.CostEstimate(flops=flops, bytes_accessed=moved, transcendentals=0),
        name=name,
    )


def place_kernel(layout, pick_ref, *refs):
    *held, out_ref = refs
    width = out_ref.shape[1]
    blocks = out_ref.shape[0] // (2 * ROWS)
    for start in range(0, width, COLS):
        quads = []
        for quad in range(2):
            values = []
            for pieces in layout[quad * QUAD : (quad + 1) * QUAD]:
                at = start
                for number in pieces:
                    if at < held[number].shape[1]:
                        values.append(held[number][:, at : at + COLS])
                        break
                    at -= held[number].shape[1]
            rows = jnp.dot(
                pick_ref[quad], jnp.concatenate(values, axis=0), preferred_element_type=jnp.float32
            )
            quads.append(rows.reshape(blocks, ROWS, COLS))
        both = jnp.concatenate(quads, axis=1).reshape(blocks * 2 * ROWS, COLS)
        out_ref[:, start : start + COLS] = both.astype(jnp.bfloat16)


def in_block(shape, axis, pairs, joint):
    slot = lax.broadcasted_iota(jnp.int32, shape, axis)
    group = pairs * joint * 2 * ROWS
    return slot // group * joint + slot % (joint * 2 * ROWS) // (2 * ROWS)


def joint_rows(x_refs, first, joint, columns=slice(None)):
    rows = slice(first * 2 * ROWS, (first + joint) * 2 * ROWS)
    return [ref[rows, columns] for ref in x_refs]


def sum_quad(spread_ref, rows_ref, quad, columns):
    blocks = rows_ref.shape[0]
    rows = rows_ref[:, quad * ROWS : (quad + 1) * ROWS, columns]
    rows = rows.reshape(blocks * ROWS, rows.shape[-1]).astype(jnp.bfloat16)
    return jnp.dot(spread_ref[quad], rows, preferred_element_type=jnp.float32)


def main_kernel(turn, steps, pairs, sums, scale_ref, head_ref, teacher_ref, spread_ref, *refs):
    x_refs = refs[:pairs]
    grad_ref, *loss_ref = refs[pairs:-2]
    rows_ref, slot_loss_ref = refs[-2:]
    step = pl.program_id(0)
    origin = step * turn if sums else 0
    scale = scale_ref[0]
    joint = 2 if turn % 2 == 0 else 1
    group = pairs * joint * 2 * ROWS
    own_block = in_block((group, BLOCK), 0, pairs, joint)
    logits = []
    for first in range(0, turn, joint):
        product = lax.dot_general(
            jnp.concatenate(joint_rows(x_refs, first, joint), axis=0),
            head_ref[first * BLOCK : (first + joint) * BLOCK, :],
            NT,
            preferred_element_type=jnp.float32,
        )
        part = product[:, :BLOCK]
        for k in range(1, joint):
            part = jnp.where(own_block == k, product[:, k * BLOCK : (k + 1) * BLOCK], part)
        logits.append(part)
    logits = jnp.concatenate(logits, axis=0)

    def log_softmax(values):
        top = jnp.max(values, axis=-1, keepdims=True)
        return values - top - jnp.log(jnp.sum(jnp.exp(values - top), axis=-1, keepdims=True))

    student_log = log_softmax(logits)
    teacher_log = log_softmax(teacher_ref[...].astype(jnp.float32))
    teacher_prob = jnp.exp(teacher_log)
    loss = scale * jnp.sum(teacher_prob * (teacher_log - student_log), axis=-1, keepdims=True)
    loss = jnp.broadcast_to(loss, logits.shape)
    grad = BLOCK * scale * (jnp.exp(student_log) - teacher_prob)
    grad_ref[...] = grad.T.astype(jnp.bfloat16)
    grad = grad.astype(jnp.bfloat16)

    for first in range(0, turn, joint):
        here = slice(first * pairs * 2 * ROWS, (first + joint) * pairs * 2 * ROWS)
        lines = [
            jnp.where(own_block == k, grad[here], jnp.zeros_like(grad[here])) for k in range(joint)
        ]
        grads = jnp.dot(
            jnp.concatenate(lines, axis=1),
            head_ref[first * BLOCK : (first + joint) * BLOCK, :],
            preferred_element_type=jnp.float32,
        )
        for pair in range(pairs):
            to = slice(pair * 2 * ROWS, (pair + 1) * 2 * ROWS)
            for k in range(joint):
                start = (pair * joint + k) * 2 * ROWS
                rows_ref[origin + first + k, to, :] = grads[start : start + 2 * ROWS].astype(
                    rows_ref.dtype
                )
                start += here.start
                slot_loss_ref[origin + first + k, to, :] = loss[start : start + 2 * ROWS]

    if not sums:
        return
    loss_ref, *part_refs = loss_ref

    @pl.when(step == steps - 1)
    def _():
        half = spread_ref.shape[1] // 2
        for quad in range(2 * pairs):
            loss_ref[quad] = sum_quad(spread_ref, slot_loss_ref, quad, slice(0, BLOCK))
            for start in range(0, rows_ref.shape[-1], COLS):
                columns = slice(start, start + COLS)
                total = sum_quad(spread_ref, rows_ref, quad, columns).astype(jnp.bfloat16)
                part_refs[quad // 2][quad % 2, :, columns] = total[:half]
                part_refs[pairs + quad // 2][quad % 2, :, columns] = total[half:]


def head_kernel(turn, splits, pairs, grad_ref, *refs):
    x_refs, (out_ref, mark_ref) = refs[:pairs], refs[-2:]
    joint = 2 if turn % 2 == 0 else 1
    slots = grad_ref.shape[1]
    share = turn // splits
    place = in_block((1, slots), 1, pairs, joint) - pl.program_id(0) % splits * share
    grad = grad_ref[...]
    spaced = [grad * (place == index).astype(jnp.bfloat16) for index in range(share)]
    spaced = jnp.concatenate(spaced, axis=0)
    for start in range(0, out_ref.shape[1], COLS):
        columns = slice(start, start + COLS)
        rows = [
            piece
            for first in range(0, turn, joint)
            for piece in joint_rows(x_refs, first, joint, columns)
        ]
        out_ref[:, columns] = jnp.dot(
            spaced, jnp.concatenate(rows, axis=0), preferred_element_type=jnp.float32
        ).astype(jnp.bfloat16)
    mark_ref[...] = jnp.zeros_like(mark_ref)


def add_kernel(*refs):
    *terms, right_ref, left_ref = refs
    for way, out_ref in enumerate((right_ref, left_ref)):
        total = sum(ref[...].reshape(out_ref.shape).astype(jnp.float32) for ref in terms[way::2])
        out_ref[...] = total.astype(jnp.bfloat16)


def ring_order(rows, columns):
    order = []
    for r in range(rows):
        line = [r * columns + c for c in range(columns)]
        order += line if r % 2 == 0 else line[::-1]
    return order


def arrivals(chips):
    near = [0]
    for step in range(1, chips // 2):
        near += [-step, step]
    return near + [chips // 2]


def after(value, *others):
    return lax.optimization_barrier((value, *others))[0]


class Ring:
    def __init__(self, hidden, order):
        chips = len(order)
        self.chips = chips
        self.ways = [
            [(order[p], order[(p + way) % chips]) for p in range(chips)] for way in (1, -1)
        ]
        self.moving = [hidden, hidden]
        self.got = [self.both([hidden])]

    def both(self, pieces):
        return pieces, [lax.ppermute(piece, "core", [(0, 1), (1, 0)]) for piece in pieces]

    def step(self):
        self.moving = [lax.ppermute(m, CHIPS, way) for m, way in zip(self.moving, self.ways)]
        self.got += [self.both([m]) for m in self.moving]

    def last(self):
        half = self.moving[0].shape[1] // 2
        parts = [self.moving[0][:, :half], self.moving[1][:, half:]]
        self.moving = [lax.ppermute(p, CHIPS, way) for p, way in zip(parts, self.ways)]

    def finish(self, *behind):
        self.got += [self.both([after(m, *behind) for m in self.moving])]


def gather_whole(hidden):
    chips = lax.axis_size(CHIPS)
    own = lax.all_gather(hidden, CHIPS, axis=0)
    other = lax.ppermute(own, "core", [(0, 1), (1, 0)])
    return [([own[chip]], [other[chip]]) for chip in range(chips)]


def on_device(hidden, head, block_ids, live_counts, teacher):
    across, down = lax.axis_size("x"), lax.axis_size("voc")
    chips = across * down
    devices = 2 * chips
    pairs = chips // 4
    tokens, list_width = block_ids.shape
    width = hidden.shape[1]
    blocks = head.shape[0] // BLOCK
    even = [n for n in range(2, 9, 2) if blocks % n == 0]
    turn = max(even) if even else 1
    steps = blocks // turn
    entries = tokens * list_width
    bucket = blocks * C
    per_block = devices * C
    core = lax.axis_index("core")
    ring = chips <= RING_MOST
    order = ring_order(across, down)
    if ring:
        circle = Ring(hidden, order)
        for _ in range(chips // 2 - 1):
            circle.step()
        circle.last()
        held = circle.got
        offsets = np.array(arrivals(chips))
        places = np.argsort(np.array(order))
        spot = jnp.asarray(places, jnp.int32)[lax.axis_index(CHIPS)]
        chip_of = jnp.asarray(np.array(order), jnp.int32)[(spot + offsets) % chips]
    else:
        held = gather_whole(hidden)
        offsets = np.arange(chips)
        chip_of = jnp.arange(chips, dtype=jnp.int32)

    flat_ids = block_ids.reshape(entries)
    position = jnp.arange(entries, dtype=jnp.int32)
    earlier = (flat_ids[:, None] == flat_ids[None, :]) & (position[:, None] > position[None, :])
    ranks = jnp.sum(earlier, axis=1, dtype=jnp.int32)
    live = (jnp.arange(list_width, dtype=jnp.int32)[None, :] < live_counts[:, None]).reshape(entries)
    map_rows = -(-bucket // BLOCK)
    meta_at = -(-bucket // 16) * 16
    deep = meta_at + -(-(map_rows + 2) // 16) * 16
    rows = flat_ids // blocks * deep + ranks * blocks + flat_ids % blocks
    slots = jnp.arange(devices * deep, dtype=jnp.int32)
    place = (slots[:, None] == rows[None, :]).astype(jnp.bfloat16)
    send_teacher = jnp.dot(
        place, teacher.reshape(entries, BLOCK), preferred_element_type=jnp.float32
    ).astype(jnp.bfloat16)
    named = jnp.where(live, position // list_width + 1, 0)
    send_map = jnp.sum(jnp.where(rows[:, None] == slots[None, :], named[:, None], 0), axis=0)
    send_map = send_map.reshape(devices, deep)[:, :bucket]
    send_map = jnp.pad(send_map, ((0, 0), (0, map_rows * BLOCK - bucket)))
    live_sum = jnp.sum(live_counts)
    send_meta = jnp.concatenate(
        [
            send_map.reshape(devices, map_rows, BLOCK),
            jnp.broadcast_to(live_sum // 256, (devices, 1, BLOCK)),
            jnp.broadcast_to(live_sum % 256, (devices, 1, BLOCK)),
            jnp.zeros((devices, deep - meta_at - map_rows - 2, BLOCK), jnp.int32),
        ],
        axis=1,
    ).astype(jnp.bfloat16)
    sent = lax.dynamic_update_slice(
        send_teacher.reshape(devices, deep, BLOCK), send_meta, (0, meta_at, 0)
    )
    got = lax.all_to_all(sent, ALL, split_axis=0, concat_axis=0, tiled=True)

    lanes = jnp.stack([core, 1 - core])
    pair_of = chip_of.reshape(chips // 2, 1, 2)
    source_of = (pair_of // down * 2 + lanes[None, :, None]) * down + pair_of % down
    source_of = source_of.reshape(devices)
    got = jnp.take(got, source_of, axis=0)
    meta = got[:, meta_at:].astype(jnp.int32)
    live_total = jnp.sum(meta[:, map_rows, 0] * 256 + meta[:, map_rows + 1, 0])
    scale = jnp.float32(tokens * devices) / live_total.astype(jnp.float32)
    slot_map = meta[:, :map_rows].reshape(devices, map_rows * BLOCK)[:, :bucket]
    quads = devices // QUAD
    slot_map = slot_map.reshape(quads, QUAD, C, blocks)
    offset = jnp.arange(QUAD, dtype=jnp.int32)[None, :, None, None] * tokens - 1
    slot_map = jnp.where(slot_map > 0, slot_map + offset, -1)
    slot_map = slot_map.transpose(0, 3, 1, 2).reshape(quads, blocks * ROWS)
    token_of = jnp.arange(QUAD * tokens, dtype=jnp.int32)
    pick = (slot_map[:, :, None] == token_of[None, None, :]).astype(jnp.bfloat16)
    spread = (slot_map[:, None, :] == token_of[None, :, None]).astype(jnp.bfloat16)
    got_teacher = got[:, :bucket].reshape(devices, C, blocks, BLOCK)
    joint = 2 if turn % 2 == 0 else 1
    got_teacher = got_teacher.reshape(pairs, 2 * ROWS, blocks // joint, joint, BLOCK)
    got_teacher = got_teacher.transpose(2, 0, 3, 1, 4).reshape(blocks * per_block, BLOCK)

    once = pl.Buffered(1)
    x_rows = blocks * 2 * ROWS
    part = max(n for n in range(1, 17) if blocks % n == 0 and (n * ROWS) % 16 == 0)
    placed = []
    for pair in range(pairs):
        if ring and pair == pairs - 1:
            circle.finish(*placed)
        layout, operands = [], []
        for quad in range(2):
            two = held[pair * 4 + quad * 2 : pair * 4 + quad * 2 + 2]
            for pieces in [chip[lane] for lane in range(2) for chip in two]:
                layout.append(list(range(len(operands), len(operands) + len(pieces))))
                operands += pieces
        placed.append(
            call(
                functools.partial(place_kernel, layout),
                f"place_{pair}",
                (blocks // part,),
                [pl.BlockSpec((2, part * ROWS, QUAD * tokens), lambda s, p=pair: (p, s, 0))]
                + [pl.BlockSpec(o.shape, lambda s: (0, 0), pipeline_mode=once) for o in operands],
                pl.BlockSpec((part * 2 * ROWS, width), lambda s: (s, 0)),
                jax.ShapeDtypeStruct((x_rows, width), jnp.bfloat16),
                2 * x_rows * QUAD * tokens * width,
                2 * x_rows * width * 2,
            )(pick, *operands)
        )

    lane_slots = turn * per_block
    slot_spec = pl.BlockSpec((lane_slots, BLOCK), lambda s: (s, 0))
    flat_spec = pl.BlockSpec((BLOCK, lane_slots), lambda s: (0, s))
    x_spec = pl.BlockSpec((turn * 2 * ROWS, width), lambda s: (s, 0))
    flops = 2 * blocks * per_block * BLOCK * width
    if ring:
        part_spec = pl.BlockSpec((2, 2 * tokens, width), lambda s: (0, 0, 0), pipeline_mode=once)
        part_shape = jax.ShapeDtypeStruct((2, 2 * tokens, width), jnp.bfloat16)
        out_specs = [
            pl.BlockSpec((quads, QUAD * tokens, BLOCK), lambda s: (0, 0, 0), pipeline_mode=once)
        ] + [part_spec] * (2 * pairs)
        out_shapes = [
            jax.ShapeDtypeStruct((quads, QUAD * tokens, BLOCK), jnp.float32)
        ] + [part_shape] * (2 * pairs)
        scratch = [
            pltpu.VMEM((blocks, per_block, width), jnp.float32),
            pltpu.VMEM((blocks, per_block, BLOCK), jnp.float32),
        ]
    else:
        out_specs = [
            pl.BlockSpec((turn, per_block, columns), lambda s: (s, 0, 0))
            for columns in (width, BLOCK)
        ]
        out_shapes = [
            jax.ShapeDtypeStruct((blocks, per_block, width), jnp.bfloat16),
            jax.ShapeDtypeStruct((blocks, per_block, BLOCK), jnp.float32),
        ]
        scratch = []
    grad, *results = call(
        functools.partial(main_kernel, turn, steps, pairs, ring),
        "logits_and_back",
        (steps,),
        [
            pl.BlockSpec(memory_space=pltpu.SMEM),
            pl.BlockSpec((turn * BLOCK, width), lambda s: (s, 0)),
            slot_spec,
            pl.BlockSpec(
                spread.shape if ring else (1, 8, LANES), lambda s: (0, 0, 0), pipeline_mode=once
            ),
        ]
        + [x_spec] * pairs,
        [flat_spec] + out_specs,
        [jax.ShapeDtypeStruct((BLOCK, blocks * per_block), jnp.bfloat16)] + out_shapes,
        16 * flops,
        head.size * 2 + pairs * x_rows * width * 2,
        scratch,
    )(
        scale.reshape(1),
        head,
        got_teacher,
        spread if ring else jnp.zeros((1, 8, LANES), spread.dtype),
        *placed,
    )
    if ring:
        loss, *parts = results
    else:
        totals = []
        for value in results:
            value = value.astype(jnp.bfloat16).reshape(blocks, quads, ROWS, value.shape[-1])
            value = value.swapaxes(0, 1).reshape(quads, blocks * ROWS, value.shape[-1])
            totals.append(
                jnp.einsum("qts,qsd->qtd", spread, value, preferred_element_type=jnp.float32)
            )
        loss = totals[1]
        total = totals[0].astype(jnp.bfloat16).reshape(pairs, 2, 2, 2 * tokens, width)
        parts = [total[pair, :, lane] for lane in range(2) for pair in range(pairs)]
    own_parts, other_parts = [], []
    for pair in range(pairs):
        own_parts.append(parts[pair].reshape(4, tokens, width))
        swapped = lax.ppermute(parts[pairs + pair], "core", [(0, 1), (1, 0)])
        other_parts.append(swapped.reshape(4, tokens, width))

    lots = max(n for n in range(1, 6) if steps % n == 0)
    lot = steps // lots
    splits = 2 if turn % 4 == 0 else 1
    filled = []

    def fill(number, behind):
        shift = number * lot
        specs = [pl.BlockSpec((BLOCK, lane_slots), lambda s, d=shift: (0, s // splits + d))]
        specs += [
            pl.BlockSpec((turn * 2 * ROWS, width), lambda s, d=shift: (s // splits + d, 0))
        ] * pairs
        operands = [grad if behind is None else after(grad, behind), *placed]
        aliases = {}
        if filled:
            specs.append(pl.BlockSpec(memory_space=pl.ANY))
            aliases = {len(operands): 0}
            operands.append(filled[-1])
        out, mark = call(
            functools.partial(head_kernel, turn, splits, pairs),
            f"head_grad_{number}",
            (lot * splits,),
            specs,
            [
                pl.BlockSpec(
                    (turn // splits * BLOCK, width), lambda s, d=shift: (s + d * splits, 0)
                ),
                pl.BlockSpec((8, LANES), lambda s: (0, 0)),
            ],
            [
                jax.ShapeDtypeStruct(head.shape, jnp.bfloat16),
                jax.ShapeDtypeStruct((8, LANES), jnp.float32),
            ],
            turn * flops // lots,
            (head.size + pairs * x_rows * width) * 2 // lots,
            aliases=aliases,
        )(*operands)
        filled.append(out)
        return mark

    if ring:
        index_of = {int(o) % chips: n for n, o in enumerate(offsets)}
        half = width // 2
        sums, mark = [], None
        for step in range(1, chips + 1):
            operands, specs = [], []
            for source in (own_parts, other_parts):
                for way in range(2):
                    at = index_of[(-step, step)[way] % chips]
                    operands.append(source[at // 4])
                    specs.append(
                        pl.BlockSpec((1, tokens, half), lambda s, a=at % 4, w=way: (a, 0, w))
                    )
            for way in range(len(sums)):
                moved = lax.ppermute(sums[way], CHIPS, circle.ways[way])
                operands.append(moved if mark is None else after(moved, mark))
                specs.append(pl.BlockSpec((tokens, half), lambda s: (0, 0)))
            sums = call(
                add_kernel,
                f"ring_sum_{step}",
                (1,),
                specs,
                [pl.BlockSpec((tokens, half), lambda s: (0, 0))] * 2,
                [jax.ShapeDtypeStruct((tokens, half), jnp.bfloat16)] * 2,
                len(operands) * tokens * half,
                len(operands) * tokens * half * 2,
            )(*operands)
            mark = fill(step - 1, sums[1]) if step <= lots else None
            if step == chips - 2:
                loss = after(loss, sums[1])
        hidden_grad = jnp.concatenate(sums, axis=1)
        for number in range(min(lots, chips), lots):
            fill(number, None)
    else:
        total = [
            (own.astype(jnp.float32) + other.astype(jnp.float32)).astype(jnp.bfloat16)
            for own, other in zip(own_parts, other_parts)
        ]
        total = jnp.concatenate(total, axis=0).reshape(chips * tokens, width)
        hidden_grad = lax.psum_scatter(total, CHIPS, tiled=True)
        for number in range(lots):
            fill(number, None)
    head_grad = filled[-1]

    loss = loss[:, :, 0].reshape(devices, tokens)
    inverse = jnp.zeros((devices,), jnp.int32).at[source_of].set(jnp.arange(devices))
    loss = jnp.take(loss, inverse, axis=0)
    loss = lax.all_to_all(loss, ALL, split_axis=0, concat_axis=0, tiled=True)
    token_loss = jnp.sum(loss, axis=0)
    return hidden_grad, head_grad, token_loss


def solution(mesh):
    groups, tok, voc = (mesh.shape[name] for name in ("groups", "tok", "voc"))
    cores = Mesh(mesh.devices.reshape(groups, tok // 2, 2, voc), ("groups", "x", "core", "voc"))
    tokens_on = ("groups",) + ALL
    return jax.shard_map(
        on_device,
        mesh=cores,
        in_specs=(
            P(tokens_on, None),
            P(ALL, None),
            P(tokens_on, None),
            P(tokens_on),
            P(tokens_on, None, None),
        ),
        out_specs=(P(tokens_on, None), P(tokens_on, None), P(tokens_on)),
        check_vma=False,
    )
```

time: 334 us -> 226 us (0.68)
  Pallas kernels: 0 us -> 96.6 us
  matrix products: 93.6 us -> 2.92 us
  blocking collectives: 87.7 us -> 10.6 us
  other arithmetic: 56.9 us -> 16 us
  starting transfers between devices: 7.44 us -> 38 us
  waiting for transfers between devices: 50.3 us -> 38.3 us
  between operations: 15.9 us -> 4.26 us
    pallas_call x0 -> x16, Pallas kernels: none -> 96.6 us  [the longest x1 37.3 us: on_device(): call(functools.partial(main_kernel, turn, steps, pairs, ring), 'logits_an...]
    dot_general x4 -> x0, matrix products: 70 us -> none  [the longest x1 20.3 us: on_device(): jnp.einsum('sgt,sgd->std', pick, slot_grad.reshape(devices, bucket, width...]
    all_gather x1 -> x0, blocking collectives: 57.3 us -> none  [on_device(): all_rows = lax.all_gather(rows, AXES, axis=0)]
    reduce_scatter x1 -> x0, waiting for transfers between devices: 49.6 us -> none  [on_device(): lax.psum_scatter(part.reshape(devices * tokens, width), AXES, scatter_dim...]
    reduce_or x1 -> x0, other arithmetic: 47.1 us -> none  [on_device(): weight = jnp.where(jnp.any(pick, axis=-1), scale, jnp.float32(0.0))]
    ppermute x0 -> x33, waiting for transfers between devices: none -> 38.3 us  [the longest x6 27.7 us: step(): lax.ppermute(m, CHIPS, way)]
    ppermute x0 -> x33, starting transfers between devices: none -> 31.7 us  [the longest x14 14.7 us: on_device(): moved = lax.ppermute(sums[way], CHIPS, circle.ways[way])]
    unnamed x1 -> x0, blocking collectives: 30.4 us -> none
  transfers between devices with their start and end apart: 3 -> 34, of which waited for: 1 -> 7; matrix products, arithmetic and copies ran while one was open for 24% -> 14% of each run, Pallas kernels for 0% -> 19%
where the time goes in v2:
time: 226 us; the launch traced here: 225 us
  Pallas kernels  96.6 us (43%)
  waiting for transfers between devices  38.3 us (17%)
  starting transfers between devices  38 us (17%)
  local copies, waits for them, and re-layouts  17.9 us (8%)
  other arithmetic  16 us (7%)
  blocking collectives  10.6 us (5%)
  between operations  4.26 us (2%)
  matrix products  2.92 us (1%)
    pallas_call x1, Pallas kernels, on_device(): call(functools.partial(main_kernel, turn, steps, pairs, ring), 'logits_an...  37.3 us
    pallas_call x5, Pallas kernels, fill(): call(functools.partial(head_kernel, turn, splits, pairs), f'head_grad_{nu...  33.7 us
    ppermute x6, waiting for transfers between devices, step(): lax.ppermute(m, CHIPS, way)  27.7 us
    pallas_call x2, Pallas kernels, on_device(): call(functools.partial(place_kernel, layout), f'place_{pair}', (blocks //...  14.8 us
    ppermute x14, starting transfers between devices, on_device(): moved = lax.ppermute(sums[way], CHIPS, circle.ways[way])  14.7 us
    pallas_call x8, Pallas kernels, on_device(): call(add_kernel, f'ring_sum_{step}', (1,), specs, [pl.BlockSpec((tokens,...  11 us
    all_to_all x1, blocking collectives, on_device(): loss = lax.all_to_all(loss, ALL, split_axis=0, concat_axis=0, tiled=True)  10.6 us
    ppermute x6, starting transfers between devices, step(): lax.ppermute(m, CHIPS, way)  10.5 us
  transfers between devices with their start and end apart: 34, of which 7 were waited for; matrix products, arithmetic and copies ran while one was open for 14% of the time, Pallas kernels for 19%

profile of v2, /device:TPU:0, one launch (start us, length us, event | category | flops | bytes accessed | tf_op | source)
XLA Modules:
  0.0 224.6 jit_solution(15076451599898020690)
XLA Ops:
  0.6 3.1 %collective-permute-start = (bf16[128,2048]{1,0:T(8,128)(2,1)}, bf16[128,2048]{1,0:T(8,128)(2,1)S(1)}, u32[]{:S(2)}, u32[]{:S(2)}) collective-permute-start(bf16[128,2048]{1,0:T(8,128)(2,1)} %refs_0_.1), channel_id=1, source_target_pairs={{0,1},{1,2},{2,3},{3,11},{11,10},{10,9},{9,8},{8,0},{4,5},{5,6},{6... | collective-permute-start | bytes 1572872 | tf_op jit(solution)/shard_map/ppermute | solution.py:218
  10.0 2.9 %fusion.5 = bf16[2816,128]{1,0:T(8,128)(2,1)} fusion(s32[1024]{0:T(1024)S(1)} %get-tuple-element.105, bf16[128,8,128]{2,1,0:T(8,128)(2,1)S(1)} %copy-done), kind=kOutput, calls=%fused_computation.16 | convolution fusion | flops 741441536 | bytes 987136 | tf_op jit(solution)/shard_map/dot_general | solution.py:280
  12.9 4.1 %select_reduce_fusion = s32[2816]{0:T(1024)S(1)} fusion(s32[1024]{0:T(1024)S(1)} %get-tuple-element.106, s32[1024]{0:T(1024)S(1)} %get-tuple-element.105), kind=kLoop, calls=%fused_computation.4 | loop fusion | flops 8647936 | bytes 19456 | tf_op jit(solution)/shard_map/reduce_sum | solution.py:284
  18.1 6.3 %all-to-all-start = ((bf16[16,176,128]{2,1,0:T(8,128)(2,1)}), bf16[16,176,128]{2,1,0:T(8,128)(2,1)S(1)}, u32[]{:S(2)}, u32[]{:S(2)}) async-start(bf16[16,176,128]{2,1,0:T(8,128)(2,1)} %maximum_dynamic-update-slice_fusion), calls=%async_computation | async-start | bytes 1441792 | tf_op jit(solution)/shard_map/all_to_all | solution.py:300
  26.7 2.0 collective-permute-start.4
  28.9 19.5 %collective-permute-done.4.refs_5_ = bf16[128,2048]{1,0:T(8,128)(2,1)} collective-permute-done((bf16[128,2048]{1,0:T(8,128)(2,1)S(1)}, bf16[128,2048]{1,0:T(8,128)(2,1)}, u32[]{:S(2)}, u32[]{:S(2)}) %collective-permute-start.4) | collective-permute-done | bytes 524320 | tf_op jit(solution)/shard_map/ppermute | solution.py:218
  48.3 5.3 %collective-permute-start.8 = (bf16[128,2048]{1,0:T(8,128)(2,1)}, bf16[128,2048]{1,0:T(8,128)(2,1)}, u32[]{:S(2)}, u32[]{:S(2)}) collective-permute-start(bf16[128,2048]{1,0:T(8,128)(2,1)} %collective-permute-done.4.refs_5_), channel_id=1, source_target_pairs={{0,1},{1,2},{2,3},{3,11},{11,10},{10,9},{9,8},{8,0},{4,5},{5,6},{6... | collective-permute-start | bytes 1572872 | tf_op jit(solution)/shard_map/ppermute | solution.py:218
  54.2 1.5 gather_fusion.1
  57.1 8.3 %collective-permute-done.8.refs_1_ = bf16[128,2048]{1,0:T(8,128)(2,1)} collective-permute-done((bf16[128,2048]{1,0:T(8,128)(2,1)}, bf16[128,2048]{1,0:T(8,128)(2,1)}, u32[]{:S(2)}, u32[]{:S(2)}) %collective-permute-start.8) | collective-permute-done | bytes 524320 | tf_op jit(solution)/shard_map/ppermute | solution.py:218
  67.4 1.9 fusion.3.pick_ref
  69.3 1.7 slice.54
  71.0 2.6 %collective-permute-start.12 = (bf16[128,1024]{1,0:T(8,128)(2,1)}, bf16[128,1024]{1,0:T(8,128)(2,1)S(1)}, u32[]{:S(2)}, u32[]{:S(2)}) collective-permute-start(bf16[128,1024]{1,0:T(8,128)(2,1)} %slice.54), channel_id=1, source_target_pairs={{0,1},{1,2},{2,3},{3,11},{11,10},{10,9},{9,8},{8,0},{4,5},{5,6},{6... | collective-permute-start | bytes 786440 | tf_op jit(solution)/shard_map/ppermute | solution.py:224
  73.6 1.7 slice.55
  81.1 7.4 %place_0.1.refs_0_ = bf16[1280,2048]{1,0:T(8,128)(2,1)} custom-call(bf16[4,640,512]{2,1,0:T(8,128)(2,1)} %fusion.3.pick_ref, bf16[128,2048]{1,0:T(8,128)(2,1)S(1)} %copy-done.2, bf16[128,2048]{1,0:T(8,128)(2,1)S(1)} %collective-permute-done.refs_1_, bf16[128,2048]{1,0:T(8,128)(2,1)S(1)} %collective-permute-done.1.refs_2_, ...), custom_call_target="tpu_custom_call" | custom-call | flops 2684354560 | bytes 10485760 | tf_op jit(solution)/shard_map/place_0/pallas_call | solution.py:338
  89.0 2.4 %fusion.2.spread_ref = bf16[4,512,640]{2,1,0:T(8,128)(2,1)} fusion(s32[4,640]{1,0:T(4,128)S(1)} %copy.29), kind=kLoop, calls=%fused_computation.11 | loop fusion | flops 2621440 | bytes 2631680 | tf_op jit(solution)/shard_map/convert_element_type | solution.py:318
  93.2 7.4 %place_1.1.refs_1_ = bf16[1280,2048]{1,0:T(8,128)(2,1)} custom-call(bf16[4,640,512]{2,1,0:T(8,128)(2,1)} %fusion.3.pick_ref, bf16[128,2048]{1,0:T(8,128)(2,1)S(1)} %collective-permute-done.7.refs_0_, bf16[128,2048]{1,0:T(8,128)(2,1)} %collective-permute-done.8.refs_1_, bf16[128,2048]{1,0:T(8,128)(2,1)} %copy-done.7, bf16[128,2048]{1,0:T(8,128)(2,1)} %copy-done.8, ...), custom_call_target="tpu_custom_call" | custom-call | flops 2684354560 | bytes 10485760 | tf_op jit(solution)/shard_map/place_1/pallas_call | solution.py:338
  100.6 37.3 %logits_and_back.1 = (bf16[128,2560]{1,0:T(8,128)(2,1)S(1)}, f32[4,512,128]{2,1,0:T(8,128)}, bf16[2,256,2048]{2,1,0:T(8,128)(2,1)}, bf16[2,256,2048]{2,1,0:T(8,1...) custom-call(f32[1]{0:T(128)} %bitcast.6.scale_ref, bf16[10240,2048]{1,0:T(8,128)(2,1)} %head_ref.1, ...), custom_call_target="tpu_custom_call" | custom-call | flops 21474836480 | bytes 52428800 | tf_op jit(solution)/shard_map/logits_and_back/pallas_call | solution.py:379
  138.3 3.9 %collective-permute-done.17 = bf16[2,256,2048]{2,1,0:T(8,128)(2,1)S(1)} collective-permute-done((bf16[2,256,2048]{2,1,0:T(8,128)(2,1)}, bf16[2,256,2048]{2,1,0:T(8,128)(2,1)S(1)}, u32[]{:S(2)}, u32[]{:S(2)}) %collective-permute-start.17) | collective-permute-done | bytes 2097184 | tf_op jit(solution)/shard_map/ppermute | solution.py:420
  147.1 6.7 %head_grad_0.1 = (bf16[10240,2048]{1,0:T(8,128)(2,1)}, f32[8,128]{1,0:T(8,128)}) custom-call(bf16[128,2560]{1,0:T(8,128)(2,1)S(1)} %get-tuple-element.89.grad_ref, bf16[1280,2048]{1,0:T(8,128)(2,1)} %place_0.1.refs_0_, bf16[1280,2048]{1,0:T(8,128)(2,1)} %place_1.1.refs_1_), custom_call_target="tpu_custom_call" | custom-call | flops 2147483648 | bytes 10485760 | tf_op jit(solution)/shard_map/head_grad_0/pallas_call | solution.py:440
  157.2 1.8 collective-permute-start.21
  159.2 6.7 %head_grad_1.1 = (bf16[10240,2048]{1,0:T(8,128)(2,1)}, f32[8,128]{1,0:T(8,128)}) custom-call(bf16[128,2560]{1,0:T(8,128)(2,1)S(1)} %get-tuple-element.89.grad_ref, bf16[1280,2048]{1,0:T(8,128)(2,1)} %place_0.1.refs_0_, bf16[1280,2048]{1,0:T(8,128)(2,1)} %place_1.1.refs_1_, bf16[10240,2048]{1,0:T(8,128)(2,1)} %get-tuple-element.69.refs_2_), custom_call_target="tpu_custom_call", output_to_operand_aliasing={{0}: (3, {})} | custom-call | flops 2147483648 | bytes 10485760 | tf_op jit(solution)/shard_map/head_grad_1/pallas_call | solution.py:440
  167.5 1.7 collective-permute-start.23
  169.6 6.7 %head_grad_2.1 = (bf16[10240,2048]{1,0:T(8,128)(2,1)}, f32[8,128]{1,0:T(8,128)}) custom-call(bf16[128,2560]{1,0:T(8,128)(2,1)S(1)} %get-tuple-element.89.grad_ref, bf16[1280,2048]{1,0:T(8,128)(2,1)} %place_0.1.refs_0_, bf16[1280,2048]{1,0:T(8,128)(2,1)} %place_1.1.refs_1_, bf16[10240,2048]{1,0:T(8,128)(2,1)} %get-tuple-element.76.refs_2_), custom_call_target="tpu_custom_call", output_to_operand_aliasing={{0}: (3, {})} | custom-call | flops 2147483648 | bytes 10485760 | tf_op jit(solution)/shard_map/head_grad_2/pallas_call | solution.py:440
  177.7 1.7 collective-permute-start.25
  180.4 6.8 %head_grad_3.1 = (bf16[10240,2048]{1,0:T(8,128)(2,1)}, f32[8,128]{1,0:T(8,128)}) custom-call(bf16[128,2560]{1,0:T(8,128)(2,1)S(1)} %get-tuple-element.89.grad_ref, bf16[1280,2048]{1,0:T(8,128)(2,1)} %place_0.1.refs_0_, bf16[1280,2048]{1,0:T(8,128)(2,1)} %place_1.1.refs_1_, bf16[10240,2048]{1,0:T(8,128)(2,1)} %get-tuple-element.83.refs_2_), custom_call_target="tpu_custom_call", output_to_operand_aliasing={{0}: (3, {})} | custom-call | flops 2147483648 | bytes 10485760 | tf_op jit(solution)/shard_map/head_grad_3/pallas_call | solution.py:440
  188.6 1.7 collective-permute-start.27
  190.7 6.7 %head_grad_4.1 = (bf16[10240,2048]{1,0:T(8,128)(2,1)}, f32[8,128]{1,0:T(8,128)}) custom-call(bf16[128,2560]{1,0:T(8,128)(2,1)S(1)} %get-tuple-element.89.grad_ref, bf16[1280,2048]{1,0:T(8,128)(2,1)} %place_0.1.refs_0_, bf16[1280,2048]{1,0:T(8,128)(2,1)} %place_1.1.refs_1_, bf16[10240,2048]{1,0:T(8,128)(2,1)} %get-tuple-element.90.refs_2_), custom_call_target="tpu_custom_call", output_to_operand_aliasing={{0}: (3, {})} | custom-call | flops 2147483648 | bytes 10485760 | tf_op jit(solution)/shard_map/head_grad_4/pallas_call | solution.py:440
  198.8 1.6 collective-permute-start.29
  200.9 4.3 %collective-permute-done.29.refs_4_ = bf16[128,1024]{1,0:T(8,128)(2,1)S(1)} collective-permute-done((bf16[128,1024]{1,0:T(8,128)(2,1)S(1)}, bf16[128,1024]{1,0:T(8,128)(2,1)S(1)}, u32[]{:S(2)}, u32[]{:S(2)}) %collective-permute-start.29) | collective-permute-done | bytes 262176 | tf_op jit(solution)/shard_map/ppermute | solution.py:476
  205.2 1.6 collective-permute-done.30.refs_5_
  208.8 1.5 collective-permute-start.32
  211.3 10.6 %all_to_all.11 = f32[16,1,128]{2,1,0:T(1,128)S(1)} all-to-all(f32[16,1,128]{2,1,0:T(1,128)S(1)} %bitcast.70), channel_id=1, replica_groups=mesh['groups'=2,'x'=2,'core'=2,'voc'=4] {'x','core','voc'}, dimensions={0} | all-to-all | bytes 16384 | tf_op jit(solution)/shard_map/all_to_all | solution.py:509
  (134 shorter events, 41.3 us)
Async XLA Ops:
  0.6 26.0 %collective-permute-start = (bf16[128,2048]{1,0:T(8,128)(2,1)}, bf16[128,2048]{1,0:T(8,128)(2,1)S(1)}, u32[]{:S(2)}, u32[]{:S(2)}) collective-permute-start(bf16[128,2048]{1,0:T(8,128)(2,1)} %refs_0_.1), channel_id=1, source_target_pairs={{0,1},{1,2},{2,3},{3,11},{11,10},{10,9},{9,8},{8,0},{4,5},{5,6},{6... | collective-permute-start | bytes 1572872 | tf_op jit(solution)/shard_map/ppermute | solution.py:218
  3.7 71.6 %collective-permute-start.1 = (bf16[128,2048]{1,0:T(8,128)(2,1)}, bf16[128,2048]{1,0:T(8,128)(2,1)S(1)}, u32[]{:S(2)}, u32[]{:S(2)}) collective-permute-start(bf16[128,2048]{1,0:T(8,128)(2,1)} %refs_0_.1), channel_id=1, source_target_pairs={{0,4},{4,0},{1,5},{5,1},{2,6},{6,2},{3,7},{7,3},{8,12},{12,8},{9,1... | collective-permute-start | bytes 1572872 | tf_op jit(solution)/shard_map/ppermute | solution.py:215
  3.7 24.9 %collective-permute-start.3 = (bf16[128,2048]{1,0:T(8,128)(2,1)}, bf16[128,2048]{1,0:T(8,128)(2,1)}, u32[]{:S(2)}, u32[]{:S(2)}) collective-permute-start(bf16[128,2048]{1,0:T(8,128)(2,1)} %refs_0_.1), channel_id=1, source_target_pairs={{0,8},{1,0},{2,1},{3,2},{11,3},{10,11},{9,10},{8,9},{4,12},{5,4},{... | collective-permute-start | bytes 1572872 | tf_op jit(solution)/shard_map/ppermute | solution.py:218
  18.1 36.0 %all-to-all-start = ((bf16[16,176,128]{2,1,0:T(8,128)(2,1)}), bf16[16,176,128]{2,1,0:T(8,128)(2,1)S(1)}, u32[]{:S(2)}, u32[]{:S(2)}) async-start(bf16[16,176,128]{2,1,0:T(8,128)(2,1)} %maximum_dynamic-update-slice_fusion), calls=%async_computation | async-start | bytes 1441792 | tf_op jit(solution)/shard_map/all_to_all | solution.py:300
  26.7 21.6 %collective-permute-start.4 = (bf16[128,2048]{1,0:T(8,128)(2,1)S(1)}, bf16[128,2048]{1,0:T(8,128)(2,1)}, u32[]{:S(2)}, u32[]{:S(2)}) collective-permute-start(bf16[128,2048]{1,0:T(8,128)(2,1)S(1)} %collective-permute-done.refs_1_), channel_id=1, source_target_pairs={{0,1},{1,2},{2,3},{3,11},{11,10},{10,9},{9,8},{8,0},{4,5},{5,6},{6... | collective-permute-start | bytes 1572872 | tf_op jit(solution)/shard_map/ppermute | solution.py:218
  28.7 25.5 %collective-permute-start.7 = (bf16[128,2048]{1,0:T(8,128)(2,1)}, bf16[128,2048]{1,0:T(8,128)(2,1)S(1)}, u32[]{:S(2)}, u32[]{:S(2)}) collective-permute-start(bf16[128,2048]{1,0:T(8,128)(2,1)} %collective-permute-done.3.refs_4_), channel_id=1, source_target_pairs={{0,8},{1,0},{2,1},{3,2},{11,3},{10,11},{9,10},{8,9},{4,12},{5,4},{... | collective-permute-start | bytes 1572872 | tf_op jit(solution)/shard_map/ppermute | solution.py:218
  48.3 17.0 %collective-permute-start.8 = (bf16[128,2048]{1,0:T(8,128)(2,1)}, bf16[128,2048]{1,0:T(8,128)(2,1)}, u32[]{:S(2)}, u32[]{:S(2)}) collective-permute-start(bf16[128,2048]{1,0:T(8,128)(2,1)} %collective-permute-done.4.refs_5_), channel_id=1, source_target_pairs={{0,1},{1,2},{2,3},{3,11},{11,10},{10,9},{9,8},{8,0},{4,5},{5,6},{6... | collective-permute-start | bytes 1572872 | tf_op jit(solution)/shard_map/ppermute | solution.py:218
  53.6 26.6 %collective-permute-start.2 = (bf16[128,2048]{1,0:T(8,128)(2,1)S(1)}, bf16[128,2048]{1,0:T(8,128)(2,1)}, u32[]{:S(2)}, u32[]{:S(2)}) collective-permute-start(bf16[128,2048]{1,0:T(8,128)(2,1)S(1)} %collective-permute-done.refs_1_), channel_id=1, source_target_pairs={{0,4},{4,0},{1,5},{5,1},{2,6},{6,2},{3,7},{7,3},{8,12},{12,8},{9,1... | collective-permute-start | bytes 1572872 | tf_op jit(solution)/shard_map/ppermute | solution.py:215
  53.6 26.9 %collective-permute-start.5 = (bf16[128,2048]{1,0:T(8,128)(2,1)}, bf16[128,2048]{1,0:T(8,128)(2,1)}, u32[]{:S(2)}, u32[]{:S(2)}) collective-permute-start(bf16[128,2048]{1,0:T(8,128)(2,1)} %collective-permute-done.3.refs_4_), channel_id=1, source_target_pairs={{0,4},{4,0},{1,5},{5,1},{2,6},{6,2},{3,7},{7,3},{8,12},{12,8},{9,1... | collective-permute-start | bytes 1572872 | tf_op jit(solution)/shard_map/ppermute | solution.py:215
  54.2 16.9 %collective-permute-start.11 = (bf16[128,2048]{1,0:T(8,128)(2,1)S(1)}, bf16[128,2048]{1,0:T(8,128)(2,1)}, u32[]{:S(2)}, u32[]{:S(2)}) collective-permute-start(bf16[128,2048]{1,0:T(8,128)(2,1)S(1)} %collective-permute-done.7.refs_0_), channel_id=1, source_target_pairs={{0,8},{1,0},{2,1},{3,2},{11,3},{10,11},{9,10},{8,9},{4,12},{5,4},{... | collective-permute-start | bytes 1572872 | tf_op jit(solution)/shard_map/ppermute | solution.py:218
  65.3 15.5 %collective-permute-start.6 = (bf16[128,2048]{1,0:T(8,128)(2,1)}, bf16[128,2048]{1,0:T(8,128)(2,1)}, u32[]{:S(2)}, u32[]{:S(2)}) collective-permute-start(bf16[128,2048]{1,0:T(8,128)(2,1)} %collective-permute-done.4.refs_5_), channel_id=1, source_target_pairs={{0,4},{4,0},{1,5},{5,1},{2,6},{6,2},{3,7},{7,3},{8,12},{12,8},{9,1... | collective-permute-start | bytes 1572872 | tf_op jit(solution)/shard_map/ppermute | solution.py:215
  71.0 17.4 %collective-permute-start.12 = (bf16[128,1024]{1,0:T(8,128)(2,1)}, bf16[128,1024]{1,0:T(8,128)(2,1)S(1)}, u32[]{:S(2)}, u32[]{:S(2)}) collective-permute-start(bf16[128,1024]{1,0:T(8,128)(2,1)} %slice.54), channel_id=1, source_target_pairs={{0,1},{1,2},{2,3},{3,11},{11,10},{10,9},{9,8},{8,0},{4,5},{5,6},{6... | collective-permute-start | bytes 786440 | tf_op jit(solution)/shard_map/ppermute | solution.py:224
  75.3 13.1 %collective-permute-start.13 = (bf16[128,1024]{1,0:T(8,128)(2,1)}, bf16[128,1024]{1,0:T(8,128)(2,1)S(1)}, u32[]{:S(2)}, u32[]{:S(2)}) collective-permute-start(bf16[128,1024]{1,0:T(8,128)(2,1)} %slice.55), channel_id=1, source_target_pairs={{0,8},{1,0},{2,1},{3,2},{11,3},{10,11},{9,10},{8,9},{4,12},{5,4},{... | collective-permute-start | bytes 786440 | tf_op jit(solution)/shard_map/ppermute | solution.py:224
  80.2 11.2 %collective-permute-start.9 = (bf16[128,2048]{1,0:T(8,128)(2,1)S(1)}, bf16[128,2048]{1,0:T(8,128)(2,1)S(1)}, u32[]{:S(2)}, u32[]{:S(2)}) collective-permute-start(bf16[128,2048]{1,0:T(8,128)(2,1)S(1)} %collective-permute-done.7.refs_0_), channel_id=1, source_target_pairs={{0,4},{4,0},{1,5},{5,1},{2,6},{6,2},{3,7},{7,3},{8,12},{12,8},{9,1... | collective-permute-start | bytes 1572872 | tf_op jit(solution)/shard_map/ppermute | solution.py:215
  80.5 10.9 %collective-permute-start.10 = (bf16[128,2048]{1,0:T(8,128)(2,1)}, bf16[128,2048]{1,0:T(8,128)(2,1)S(1)}, u32[]{:S(2)}, u32[]{:S(2)}) collective-permute-start(bf16[128,2048]{1,0:T(8,128)(2,1)} %collective-permute-done.8.refs_1_), channel_id=1, source_target_pairs={{0,4},{4,0},{1,5},{5,1},{2,6},{6,2},{3,7},{7,3},{8,12},{12,8},{9,1... | collective-permute-start | bytes 1572872 | tf_op jit(solution)/shard_map/ppermute | solution.py:215
  80.8 10.6 %collective-permute-start.14 = (bf16[128,2048]{1,0:T(8,128)(2,1)}, bf16[128,2048]{1,0:T(8,128)(2,1)S(1)}, u32[]{:S(2)}, u32[]{:S(2)}) collective-permute-start(bf16[128,2048]{1,0:T(8,128)(2,1)} %collective-permute-done.11.refs_4_), channel_id=1, source_target_pairs={{0,4},{4,0},{1,5},{5,1},{2,6},{6,2},{3,7},{7,3},{8,12},{12,8},{9,1... | collective-permute-start | bytes 1572872 | tf_op jit(solution)/shard_map/ppermute | solution.py:215
  137.8 4.4 %collective-permute-start.17 = (bf16[2,256,2048]{2,1,0:T(8,128)(2,1)}, bf16[2,256,2048]{2,1,0:T(8,128)(2,1)S(1)}, u32[]{:S(2)}, u32[]{:S(2)}) collective-permute-start(bf16[2,256,2048]{2,1,0:T(8,128)(2,1)} %get-tuple-element.56), channel_id=1, source_target_pairs={{0,4},{4,0},{1,5},{5,1},{2,6},{6,2},{3,7},{7,3},{8,12},{12,8},{9,1... | collective-permute-start | bytes 6291464 | tf_op jit(solution)/shard_map/ppermute | solution.py:420
  138.1 16.3 %collective-permute-start.18 = (bf16[2,256,2048]{2,1,0:T(8,128)(2,1)}, bf16[2,256,2048]{2,1,0:T(8,128)(2,1)S(1)}, u32[]{:S(2)}, u32[]{:S(2)}) collective-permute-start(bf16[2,256,2048]{2,1,0:T(8,128)(2,1)} %get-tuple-element.58), channel_id=1, source_target_pairs={{0,4},{4,0},{1,5},{5,1},{2,6},{6,2},{3,7},{7,3},{8,12},{12,8},{9,1... | collective-permute-start | bytes 6291464 | tf_op jit(solution)/shard_map/ppermute | solution.py:420
  144.8 9.0 %collective-permute-start.19 = (bf16[128,1024]{1,0:T(8,128)(2,1)S(1)}, bf16[128,1024]{1,0:T(8,128)(2,1)S(1)}, u32[]{:S(2)}, u32[]{:S(2)}) collective-permute-start(bf16[128,1024]{1,0:T(8,128)(2,1)S(1)} %get-tuple-element.59), channel_id=1, source_target_pairs={{0,1},{1,2},{2,3},{3,11},{11,10},{10,9},{9,8},{8,0},{4,5},{5,6},{6... | collective-permute-start | bytes 786440 | tf_op jit(solution)/shard_map/ppermute | solution.py:476
  145.9 8.5 %collective-permute-start.20 = (bf16[128,1024]{1,0:T(8,128)(2,1)S(1)}, bf16[128,1024]{1,0:T(8,128)(2,1)S(1)}, u32[]{:S(2)}, u32[]{:S(2)}) collective-permute-start(bf16[128,1024]{1,0:T(8,128)(2,1)S(1)} %get-tuple-element.61), channel_id=1, source_target_pairs={{0,8},{1,0},{2,1},{3,2},{11,3},{10,11},{9,10},{8,9},{4,12},{5,4},{... | collective-permute-start | bytes 786440 | tf_op jit(solution)/shard_map/ppermute | solution.py:476
  157.2 8.8 %collective-permute-start.21 = (bf16[128,1024]{1,0:T(8,128)(2,1)S(1)}, bf16[128,1024]{1,0:T(8,128)(2,1)S(1)}, u32[]{:S(2)}, u32[]{:S(2)}) collective-permute-start(bf16[128,1024]{1,0:T(8,128)(2,1)S(1)} %get-tuple-element.66), channel_id=1, source_target_pairs={{0,1},{1,2},{2,3},{3,11},{11,10},{10,9},{9,8},{8,0},{4,5},{5,6},{6... | collective-permute-start | bytes 786440 | tf_op jit(solution)/shard_map/ppermute | solution.py:476
  159.0 7.2 %collective-permute-start.22 = (bf16[128,1024]{1,0:T(8,128)(2,1)S(1)}, bf16[128,1024]{1,0:T(8,128)(2,1)S(1)}, u32[]{:S(2)}, u32[]{:S(2)}) collective-permute-start(bf16[128,1024]{1,0:T(8,128)(2,1)S(1)} %get-tuple-element.67), channel_id=1, source_target_pairs={{0,8},{1,0},{2,1},{3,2},{11,3},{10,11},{9,10},{8,9},{4,12},{5,4},{... | collective-permute-start | bytes 786440 | tf_op jit(solution)/shard_map/ppermute | solution.py:476
  167.5 8.8 %collective-permute-start.23 = (bf16[128,1024]{1,0:T(8,128)(2,1)S(1)}, bf16[128,1024]{1,0:T(8,128)(2,1)S(1)}, u32[]{:S(2)}, u32[]{:S(2)}) collective-permute-start(bf16[128,1024]{1,0:T(8,128)(2,1)S(1)} %get-tuple-element.73), channel_id=1, source_target_pairs={{0,1},{1,2},{2,3},{3,11},{11,10},{10,9},{9,8},{8,0},{4,5},{5,6},{6... | collective-permute-start | bytes 786440 | tf_op jit(solution)/shard_map/ppermute | solution.py:476
  169.2 7.2 %collective-permute-start.24 = (bf16[128,1024]{1,0:T(8,128)(2,1)S(1)}, bf16[128,1024]{1,0:T(8,128)(2,1)S(1)}, u32[]{:S(2)}, u32[]{:S(2)}) collective-permute-start(bf16[128,1024]{1,0:T(8,128)(2,1)S(1)} %get-tuple-element.74), channel_id=1, source_target_pairs={{0,8},{1,0},{2,1},{3,2},{11,3},{10,11},{9,10},{8,9},{4,12},{5,4},{... | collective-permute-start | bytes 786440 | tf_op jit(solution)/shard_map/ppermute | solution.py:476
  177.7 9.5 %collective-permute-start.25 = (bf16[128,1024]{1,0:T(8,128)(2,1)S(1)}, bf16[128,1024]{1,0:T(8,128)(2,1)S(1)}, u32[]{:S(2)}, u32[]{:S(2)}) collective-permute-start(bf16[128,1024]{1,0:T(8,128)(2,1)S(1)} %get-tuple-element.80), channel_id=1, source_target_pairs={{0,1},{1,2},{2,3},{3,11},{11,10},{10,9},{9,8},{8,0},{4,5},{5,6},{6... | collective-permute-start | bytes 786440 | tf_op jit(solution)/shard_map/ppermute | solution.py:476
  179.4 7.8 %collective-permute-start.26 = (bf16[128,1024]{1,0:T(8,128)(2,1)S(1)}, bf16[128,1024]{1,0:T(8,128)(2,1)S(1)}, u32[]{:S(2)}, u32[]{:S(2)}) collective-permute-start(bf16[128,1024]{1,0:T(8,128)(2,1)S(1)} %get-tuple-element.81), channel_id=1, source_target_pairs={{0,8},{1,0},{2,1},{3,2},{11,3},{10,11},{9,10},{8,9},{4,12},{5,4},{... | collective-permute-start | bytes 786440 | tf_op jit(solution)/shard_map/ppermute | solution.py:476
  188.6 8.8 %collective-permute-start.27 = (bf16[128,1024]{1,0:T(8,128)(2,1)S(1)}, bf16[128,1024]{1,0:T(8,128)(2,1)S(1)}, u32[]{:S(2)}, u32[]{:S(2)}) collective-permute-start(bf16[128,1024]{1,0:T(8,128)(2,1)S(1)} %get-tuple-element.87), channel_id=1, source_target_pairs={{0,1},{1,2},{2,3},{3,11},{11,10},{10,9},{9,8},{8,0},{4,5},{5,6},{6... | collective-permute-start | bytes 786440 | tf_op jit(solution)/shard_map/ppermute | solution.py:476
  190.2 7.2 %collective-permute-start.28 = (bf16[128,1024]{1,0:T(8,128)(2,1)S(1)}, bf16[128,1024]{1,0:T(8,128)(2,1)S(1)}, u32[]{:S(2)}, u32[]{:S(2)}) collective-permute-start(bf16[128,1024]{1,0:T(8,128)(2,1)S(1)} %get-tuple-element.88), channel_id=1, source_target_pairs={{0,8},{1,0},{2,1},{3,2},{11,3},{10,11},{9,10},{8,9},{4,12},{5,4},{... | collective-permute-start | bytes 786440 | tf_op jit(solution)/shard_map/ppermute | solution.py:476
  198.8 6.4 %collective-permute-start.29 = (bf16[128,1024]{1,0:T(8,128)(2,1)S(1)}, bf16[128,1024]{1,0:T(8,128)(2,1)S(1)}, u32[]{:S(2)}, u32[]{:S(2)}) collective-permute-start(bf16[128,1024]{1,0:T(8,128)(2,1)S(1)} %get-tuple-element.94), channel_id=1, source_target_pairs={{0,1},{1,2},{2,3},{3,11},{11,10},{10,9},{9,8},{8,0},{4,5},{5,6},{6... | collective-permute-start | bytes 786440 | tf_op jit(solution)/shard_map/ppermute | solution.py:476
  200.4 6.4 %collective-permute-start.30 = (bf16[128,1024]{1,0:T(8,128)(2,1)S(1)}, bf16[128,1024]{1,0:T(8,128)(2,1)S(1)}, u32[]{:S(2)}, u32[]{:S(2)}) collective-permute-start(bf16[128,1024]{1,0:T(8,128)(2,1)S(1)} %get-tuple-element.95), channel_id=1, source_target_pairs={{0,8},{1,0},{2,1},{3,2},{11,3},{10,11},{9,10},{8,9},{4,12},{5,4},{... | collective-permute-start | bytes 786440 | tf_op jit(solution)/shard_map/ppermute | solution.py:476
  208.2 14.2 %collective-permute-start.31 = (bf16[128,1024]{1,0:T(8,128)(2,1)S(1)}, bf16[128,1024]{1,0:T(8,128)(2,1)S(1)}, u32[]{:S(2)}, u32[]{:S(2)}) collective-permute-start(bf16[128,1024]{1,0:T(8,128)(2,1)S(1)} %get-tuple-element.96), channel_id=1, source_target_pairs={{0,1},{1,2},{2,3},{3,11},{11,10},{10,9},{9,8},{8,0},{4,5},{5,6},{6... | collective-permute-start | bytes 786440 | tf_op jit(solution)/shard_map/ppermute | solution.py:476
  208.8 13.6 %collective-permute-start.32 = (bf16[128,1024]{1,0:T(8,128)(2,1)S(1)}, bf16[128,1024]{1,0:T(8,128)(2,1)S(1)}, u32[]{:S(2)}, u32[]{:S(2)}) collective-permute-start(bf16[128,1024]{1,0:T(8,128)(2,1)S(1)} %get-tuple-element.97), channel_id=1, source_target_pairs={{0,8},{1,0},{2,1},{3,2},{11,3},{10,11},{9,10},{8,9},{4,12},{5,4},{... | collective-permute-start | bytes 786440 | tf_op jit(solution)/shard_map/ppermute | solution.py:476
  (13 other events, 87.2 us)

commit v3 on v2

--- a/solution.py
+++ b/solution.py
@@ -73,14 +73,14 @@
     return [ref[rows, columns] for ref in x_refs]
 
 
-def sum_quad(spread_ref, rows_ref, quad, columns):
+def sum_quad(spread, rows_ref, quad, columns):
     blocks = rows_ref.shape[0]
     rows = rows_ref[:, quad * ROWS : (quad + 1) * ROWS, columns]
     rows = rows.reshape(blocks * ROWS, rows.shape[-1]).astype(jnp.bfloat16)
-    return jnp.dot(spread_ref[quad], rows, preferred_element_type=jnp.float32)
-
-
-def main_kernel(turn, steps, pairs, sums, scale_ref, head_ref, teacher_ref, spread_ref, *refs):
+    return jnp.dot(spread, rows, preferred_element_type=jnp.float32)
+
+
+def main_kernel(turn, steps, pairs, sums, scale_ref, head_ref, teacher_ref, map_ref, *refs):
     x_refs = refs[:pairs]
     grad_ref, *loss_ref = refs[pairs:-2]
     rows_ref, slot_loss_ref = refs[-2:]
@@ -143,12 +143,16 @@
 
     @pl.when(step == steps - 1)
     def _():
-        half = spread_ref.shape[1] // 2
+        quad_tokens = loss_ref.shape[1]
+        half = quad_tokens // 2
         for quad in range(2 * pairs):
-            loss_ref[quad] = sum_quad(spread_ref, slot_loss_ref, quad, slice(0, BLOCK))
+            slots = map_ref[quad : quad + 1, :]
+            token = lax.broadcasted_iota(jnp.int32, (quad_tokens, slots.shape[1]), 0)
+            spread = jnp.where(slots == token, 1.0, 0.0).astype(jnp.bfloat16)
+            loss_ref[quad] = sum_quad(spread, slot_loss_ref, quad, slice(0, BLOCK))
             for start in range(0, rows_ref.shape[-1], COLS):
                 columns = slice(start, start + COLS)
-                total = sum_quad(spread_ref, rows_ref, quad, columns).astype(jnp.bfloat16)
+                total = sum_quad(spread, rows_ref, quad, columns).astype(jnp.bfloat16)
                 part_refs[quad // 2][quad % 2, :, columns] = total[:half]
                 part_refs[pairs + quad // 2][quad % 2, :, columns] = total[half:]
 
@@ -204,27 +208,27 @@
 class Ring:
     def __init__(self, hidden, order):
         chips = len(order)
-        self.chips = chips
+        half = hidden.shape[1] // 2
         self.ways = [
             [(order[p], order[(p + way) % chips]) for p in range(chips)] for way in (1, -1)
         ]
-        self.moving = [hidden, hidden]
-        self.got = [self.both([hidden])]
+        halves = [hidden[:, :half], hidden[:, half:]]
+        self.moving = [halves, halves]
+        self.got = [self.both(halves)]
 
     def both(self, pieces):
         return pieces, [lax.ppermute(piece, "core", [(0, 1), (1, 0)]) for piece in pieces]
 
     def step(self):
-        self.moving = [lax.ppermute(m, CHIPS, way) for m, way in zip(self.moving, self.ways)]
-        self.got += [self.both([m]) for m in self.moving]
-
-    def last(self):
-        half = self.moving[0].shape[1] // 2
-        parts = [self.moving[0][:, :half], self.moving[1][:, half:]]
-        self.moving = [lax.ppermute(p, CHIPS, way) for p, way in zip(parts, self.ways)]
-
-    def finish(self, *behind):
-        self.got += [self.both([after(m, *behind) for m in self.moving])]
+        self.moving = [
+            [lax.ppermute(piece, CHIPS, way) for piece in pieces]
+            for pieces, way in zip(self.moving, self.ways)
+        ]
+        self.got += [self.both(pieces) for pieces in self.moving]
+
+    def last(self, *behind):
+        pieces = [after(self.moving[way][way], *behind) for way in range(2)]
+        self.got += [self.both([lax.ppermute(p, CHIPS, w) for p, w in zip(pieces, self.ways)])]
 
 
 def gather_whole(hidden):
@@ -255,7 +259,6 @@
         circle = Ring(hidden, order)
         for _ in range(chips // 2 - 1):
             circle.step()
-        circle.last()
         held = circle.got
         offsets = np.array(arrivals(chips))
         places = np.argsort(np.array(order))
@@ -281,8 +284,10 @@
         place, teacher.reshape(entries, BLOCK), preferred_element_type=jnp.float32
     ).astype(jnp.bfloat16)
     named = jnp.where(live, position // list_width + 1, 0)
-    send_map = jnp.sum(jnp.where(rows[:, None] == slots[None, :], named[:, None], 0), axis=0)
-    send_map = send_map.reshape(devices, deep)[:, :bucket]
+    tight = flat_ids // blocks * bucket + ranks * blocks + flat_ids % blocks
+    spots = jnp.arange(devices * bucket, dtype=jnp.int32)
+    send_map = jnp.sum(jnp.where(tight[:, None] == spots[None, :], named[:, None], 0), axis=0)
+    send_map = send_map.reshape(devices, bucket)
     send_map = jnp.pad(send_map, ((0, 0), (0, map_rows * BLOCK - bucket)))
     live_sum = jnp.sum(live_counts)
     send_meta = jnp.concatenate(
@@ -303,19 +308,18 @@
     pair_of = chip_of.reshape(chips // 2, 1, 2)
     source_of = (pair_of // down * 2 + lanes[None, :, None]) * down + pair_of % down
     source_of = source_of.reshape(devices)
-    got = jnp.take(got, source_of, axis=0)
+    got = got.at[source_of].get(mode="promise_in_bounds")
     meta = got[:, meta_at:].astype(jnp.int32)
     live_total = jnp.sum(meta[:, map_rows, 0] * 256 + meta[:, map_rows + 1, 0])
     scale = jnp.float32(tokens * devices) / live_total.astype(jnp.float32)
     slot_map = meta[:, :map_rows].reshape(devices, map_rows * BLOCK)[:, :bucket]
     quads = devices // QUAD
-    slot_map = slot_map.reshape(quads, QUAD, C, blocks)
-    offset = jnp.arange(QUAD, dtype=jnp.int32)[None, :, None, None] * tokens - 1
+    slot_map = slot_map.reshape(quads, ROWS, blocks)
+    offset = jnp.arange(ROWS, dtype=jnp.int32)[None, :, None] // C * tokens - 1
     slot_map = jnp.where(slot_map > 0, slot_map + offset, -1)
-    slot_map = slot_map.transpose(0, 3, 1, 2).reshape(quads, blocks * ROWS)
+    slot_map = slot_map.swapaxes(1, 2).reshape(quads, blocks * ROWS)
     token_of = jnp.arange(QUAD * tokens, dtype=jnp.int32)
     pick = (slot_map[:, :, None] == token_of[None, None, :]).astype(jnp.bfloat16)
-    spread = (slot_map[:, None, :] == token_of[None, :, None]).astype(jnp.bfloat16)
     got_teacher = got[:, :bucket].reshape(devices, C, blocks, BLOCK)
     joint = 2 if turn % 2 == 0 else 1
     got_teacher = got_teacher.reshape(pairs, 2 * ROWS, blocks // joint, joint, BLOCK)
@@ -327,7 +331,7 @@
     placed = []
     for pair in range(pairs):
         if ring and pair == pairs - 1:
-            circle.finish(*placed)
+            circle.last(*placed)
         layout, operands = [], []
         for quad in range(2):
             two = held[pair * 4 + quad * 2 : pair * 4 + quad * 2 + 2]
@@ -384,9 +388,7 @@
             pl.BlockSpec(memory_space=pltpu.SMEM),
             pl.BlockSpec((turn * BLOCK, width), lambda s: (s, 0)),
             slot_spec,
-            pl.BlockSpec(
-                spread.shape if ring else (1, 8, LANES), lambda s: (0, 0, 0), pipeline_mode=once
-            ),
+            pl.BlockSpec(slot_map.shape, lambda s: (0, 0), pipeline_mode=once),
         ]
         + [x_spec] * pairs,
         [flat_spec] + out_specs,
@@ -398,7 +400,7 @@
         scale.reshape(1),
         head,
         got_teacher,
-        spread if ring else jnp.zeros((1, 8, LANES), spread.dtype),
+        slot_map,
         *placed,
     )
     if ring:
@@ -409,7 +411,7 @@
             value = value.astype(jnp.bfloat16).reshape(blocks, quads, ROWS, value.shape[-1])
             value = value.swapaxes(0, 1).reshape(quads, blocks * ROWS, value.shape[-1])
             totals.append(
-                jnp.einsum("qts,qsd->qtd", spread, value, preferred_element_type=jnp.float32)
+                jnp.einsum("qst,qsd->qtd", pick, value, preferred_element_type=jnp.float32)
             )
         loss = totals[1]
         total = totals[0].astype(jnp.bfloat16).reshape(pairs, 2, 2, 2 * tokens, width)
@@ -419,6 +421,18 @@
         own_parts.append(parts[pair].reshape(4, tokens, width))
         swapped = lax.ppermute(parts[pairs + pair], "core", [(0, 1), (1, 0)])
         other_parts.append(swapped.reshape(4, tokens, width))
+
+    inverse = jnp.sum(
+        jnp.where(source_of[None, :] == jnp.arange(devices)[:, None], jnp.arange(devices)[None], 0),
+        axis=1,
+    )
+    loss = loss[:, :, 0].reshape(devices, tokens)
+    loss = loss.at[inverse].get(mode="promise_in_bounds")
+
+    def return_loss(behind=None):
+        sent = loss if behind is None else after(loss, behind)
+        back = lax.all_to_all(sent, ALL, split_axis=0, concat_axis=0, tiled=True)
+        return jnp.sum(back, axis=0)
 
     lots = max(n for n in range(1, 6) if steps % n == 0)
     lot = steps // lots
@@ -487,12 +501,11 @@
                 len(operands) * tokens * half * 2,
             )(*operands)
             mark = fill(step - 1, sums[1]) if step <= lots else None
-            if step == chips - 2:
-                loss = after(loss, sums[1])
+            if step == lots + 1:
+                mark = token_loss = return_loss(sums[1])
         hidden_grad = jnp.concatenate(sums, axis=1)
-        for number in range(min(lots, chips), lots):
-            fill(number, None)
     else:
+        token_loss = return_loss()
         total = [
             (own.astype(jnp.float32) + other.astype(jnp.float32)).astype(jnp.bfloat16)
             for own, other in zip(own_parts, other_parts)
@@ -503,11 +516,6 @@
             fill(number, None)
     head_grad = filled[-1]
 
-    loss = loss[:, :, 0].reshape(devices, tokens)
-    inverse = jnp.zeros((devices,), jnp.int32).at[source_of].set(jnp.arange(devices))
-    loss = jnp.take(loss, inverse, axis=0)
-    loss = lax.all_to_all(loss, ALL, split_axis=0, concat_axis=0, tiled=True)
-    token_loss = jnp.sum(loss, axis=0)
     return hidden_grad, head_grad, token_loss
 
 

time: 226 us -> 222 us (0.982)
  starting transfers between devices: 38 us -> 49.9 us
  local copies, waits for them, and re-layouts: 17.9 us -> 9.61 us
  other arithmetic: 16 us -> 11 us
    ppermute x8 -> x14, starting transfers between devices: 14.5 us -> 25.4 us  [the longest x12 23.4 us: step(): lax.ppermute(piece, CHIPS, way)]
    slice x2 -> x1, local copies, waits for them, and re-layouts: 3.39 us -> 0.04 us  [__init__(): halves = [hidden[:, :half], hidden[:, half:]]]
    convert_element_type x1 -> x0, other arithmetic: 2.38 us -> none  [on_device(): (slot_map[:, None, :] == token_of[None, :, None]).astype(jnp.bfloat16)]
    reduce_sum x2 -> x3, other arithmetic: 4.63 us -> 2.28 us  [the longest x1 1.63 us: on_device(): jnp.sum(jnp.where(tight[:, None] == spots[None, :], named[:, None], 0), a...]
    unnamed x24 -> x32, local copies, waits for them, and re-layouts: 5.22 us -> 3.5 us
    ppermute x8 -> x14, waiting for transfers between devices: 27.7 us -> 27.1 us  [the longest x12 19.4 us: step(): lax.ppermute(piece, CHIPS, way)]
  transfers between devices with their start and end apart: 34 -> 47, of which waited for: 7 -> 9; matrix products, arithmetic and copies ran while one was open for 14% -> 5% of each run, Pallas kernels for 19% -> 19%
where the time goes in v3:
time: 222 us; the launch traced here: 220 us
  Pallas kernels  95.6 us (43%)
  starting transfers between devices  49.9 us (22%)
  waiting for transfers between devices  37.5 us (17%)
  other arithmetic  11 us (5%)
  local copies, waits for them, and re-layouts  9.61 us (4%)
  blocking collectives  9.51 us (4%)
  between operations  4.38 us (2%)
  matrix products  2.92 us (1%)
    pallas_call x1, Pallas kernels, on_device(): call(functools.partial(main_kernel, turn, steps, pairs, ring), 'logits_an...  36.3 us
    pallas_call x5, Pallas kernels, fill(): call(functools.partial(head_kernel, turn, splits, pairs), f'head_grad_{nu...  33.7 us
    ppermute x12, starting transfers between devices, step(): lax.ppermute(piece, CHIPS, way)  23.4 us
    ppermute x12, waiting for transfers between devices, step(): lax.ppermute(piece, CHIPS, way)  19.4 us
    pallas_call x2, Pallas kernels, on_device(): call(functools.partial(place_kernel, layout), f'place_{pair}', (blocks //...  14.6 us
    ppermute x14, starting transfers between devices, on_device(): moved = lax.ppermute(sums[way], CHIPS, circle.ways[way])  14.6 us
    pallas_call x8, Pallas kernels, on_device(): call(add_kernel, f'ring_sum_{step}', (1,), specs, [pl.BlockSpec((tokens,...  11 us
    all_to_all x1, blocking collectives, return_loss(): back = lax.all_to_all(sent, ALL, split_axis=0, concat_axis=0, tiled=True)  9.51 us
  transfers between devices with their start and end apart: 47, of which 9 were waited for; matrix products, arithmetic and copies ran while one was open for 5% of the time, Pallas kernels for 19%

profile of v3, /device:TPU:0, one launch (start us, length us, event | category | flops | bytes accessed | tf_op | source)
XLA Modules:
  0.0 220.4 jit_solution(1271678639783356986)
XLA Ops:
  7.1 1.6 select_reduce_fusion
  8.9 2.9 %fusion.4 = bf16[2816,128]{1,0:T(8,128)(2,1)} fusion(s32[1024]{0:T(1024)S(1)} %get-tuple-element.110, bf16[128,8,128]{2,1,0:T(8,128)(2,1)S(1)} %copy-done), kind=kOutput, calls=%fused_computation.13 | convolution fusion | flops 741441536 | bytes 987136 | tf_op jit(solution)/shard_map/dot_general | solution.py:283
  12.6 7.4 %all-to-all-start = ((bf16[16,176,128]{2,1,0:T(8,128)(2,1)}), bf16[16,176,128]{2,1,0:T(8,128)(2,1)S(1)}, u32[]{:S(2)}, u32[]{:S(2)}) async-start(bf16[16,176,128]{2,1,0:T(8,128)(2,1)} %maximum_dynamic-update-slice_fusion), calls=%async_computation | async-start | bytes 1441792 | tf_op jit(solution)/shard_map/all_to_all | solution.py:305
  20.0 2.0 collective-permute-start.7
  22.2 1.8 collective-permute-start.6
  26.3 14.6 %collective-permute-done.7.refs_9_ = bf16[128,1024]{1,0:T(8,128)(2,1)} collective-permute-done((bf16[128,1024]{1,0:T(8,128)(2,1)S(1)}, bf16[128,1024]{1,0:T(8,128)(2,1)}, u32[]{:S(2)}, u32[]{:S(2)}) %collective-permute-start.7) | collective-permute-done | bytes 262176 | tf_op jit(solution)/shard_map/ppermute | solution.py:224
  40.8 5.4 %collective-permute-start = (bf16[128,1024]{1,0:T(8,128)(2,1)S(1)}, bf16[128,1024]{1,0:T(8,128)(2,1)S(1)}, u32[]{:S(2)}, u32[]{:S(2)}) collective-permute-start(bf16[128,1024]{1,0:T(8,128)(2,1)S(1)} %get-tuple-element.108.refs_0_), channel_id=1, source_target_pairs={{0,1},{1,2},{2,3},{3,11},{11,10},{10,9},{9,8},{8,0},{4,5},{5,6},{6... | collective-permute-start | bytes 786440 | tf_op jit(solution)/shard_map/ppermute | solution.py:224
  46.3 5.4 %collective-permute-start.9 = (bf16[128,1024]{1,0:T(8,128)(2,1)S(1)}, bf16[128,1024]{1,0:T(8,128)(2,1)}, u32[]{:S(2)}, u32[]{:S(2)}) collective-permute-start(bf16[128,1024]{1,0:T(8,128)(2,1)S(1)} %collective-permute-done.1.refs_3_), channel_id=1, source_target_pairs={{0,1},{1,2},{2,3},{3,11},{11,10},{10,9},{9,8},{8,0},{4,5},{5,6},{6... | collective-permute-start | bytes 786440 | tf_op jit(solution)/shard_map/ppermute | solution.py:224
  53.6 3.6 %collective-permute-start.8 = (bf16[128,1024]{1,0:T(8,128)(2,1)S(1)}, bf16[128,1024]{1,0:T(8,128)(2,1)}, u32[]{:S(2)}, u32[]{:S(2)}) collective-permute-start(bf16[128,1024]{1,0:T(8,128)(2,1)S(1)} %collective-permute-done.refs_2_), channel_id=1, source_target_pairs={{0,1},{1,2},{2,3},{3,11},{11,10},{10,9},{9,8},{8,0},{4,5},{5,6},{6... | collective-permute-start | bytes 786440 | tf_op jit(solution)/shard_map/ppermute | solution.py:224
  58.9 3.1 %collective-permute-done.14.refs_0_ = bf16[128,1024]{1,0:T(8,128)(2,1)S(1)} collective-permute-done((bf16[128,1024]{1,0:T(8,128)(2,1)}, bf16[128,1024]{1,0:T(8,128)(2,1)S(1)}, u32[]{:S(2)}, u32[]{:S(2)}) %collective-permute-start.14) | collective-permute-done | bytes 262176 | tf_op jit(solution)/shard_map/ppermute | solution.py:224
  63.5 2.6 %collective-permute-start.17 = (bf16[128,1024]{1,0:T(8,128)(2,1)}, bf16[128,1024]{1,0:T(8,128)(2,1)S(1)}, u32[]{:S(2)}, u32[]{:S(2)}) collective-permute-start(bf16[128,1024]{1,0:T(8,128)(2,1)} %collective-permute-done.9.refs_11_), channel_id=1, source_target_pairs={{0,1},{1,2},{2,3},{3,11},{11,10},{10,9},{9,8},{8,0},{4,5},{5,6},{6... | collective-permute-start | bytes 786440 | tf_op jit(solution)/shard_map/ppermute | solution.py:224
  66.4 1.8 fusion.2.pick_ref
  68.2 1.8 collective-permute-start.22
  69.9 7.3 %place_0.1.refs_0_ = bf16[1280,2048]{1,0:T(8,128)(2,1)} custom-call(bf16[4,640,512]{2,1,0:T(8,128)(2,1)} %fusion.2.pick_ref, bf16[128,1024]{1,0:T(8,128)(2,1)S(1)} %get-tuple-element.108.refs_0_, bf16[128,1024]{1,0:T(8,128)(2,1)S(1)} %get-tuple-element.107.refs_1_, bf16[128,1024]{1,0:T(8,128)(2,1)S(1)} %collective-permute-done.refs_2_, ...), custom_call_target="tpu_custom_call" | custom-call | flops 2684354560 | bytes 10485760 | tf_op jit(solution)/shard_map/place_0/pallas_call | solution.py:342
  77.8 2.0 collective-permute-start.24
  80.7 5.6 %collective-permute-done.24.refs_10_ = bf16[128,1024]{1,0:T(8,128)(2,1)S(1)} collective-permute-done((bf16[128,1024]{1,0:T(8,128)(2,1)S(1)}, bf16[128,1024]{1,0:T(8,128)(2,1)S(1)}, u32[]{:S(2)}, u32[]{:S(2)}) %collective-permute-start.24) | collective-permute-done | bytes 262176 | tf_op jit(solution)/shard_map/ppermute | solution.py:231
  86.3 2.1 collective-permute-done.25.refs_11_
  92.0 7.3 %place_1.1.refs_1_ = bf16[1280,2048]{1,0:T(8,128)(2,1)} custom-call(bf16[4,640,512]{2,1,0:T(8,128)(2,1)} %fusion.2.pick_ref, bf16[128,1024]{1,0:T(8,128)(2,1)S(1)} %collective-permute-done.14.refs_0_, bf16[128,1024]{1,0:T(8,128)(2,1)S(1)} %collective-permute-done.15.refs_1_, bf16[128,1024]{1,0:T(8,128)(2,1)S(1)} %collective-permute-done.16.refs_2_, ...), custom_call_target="tpu_custom_call" | custom-call | flops 2684354560 | bytes 10485760 | tf_op jit(solution)/shard_map/place_1/pallas_call | solution.py:342
  99.3 36.3 %logits_and_back.1 = (bf16[128,2560]{1,0:T(8,128)(2,1)S(1)}, f32[4,512,128]{2,1,0:T(8,128)}, bf16[2,256,2048]{2,1,0:T(8,128)(2,1)}, bf16[2,256,2048]{2,1,0:T(8,1...) custom-call(f32[1]{0:T(128)} %bitcast.6.scale_ref, bf16[10240,2048]{1,0:T(8,128)(2,1)} %head_ref.1, ...), custom_call_target="tpu_custom_call" | custom-call | flops 21474836480 | bytes 52428800 | tf_op jit(solution)/shard_map/logits_and_back/pallas_call | solution.py:383
  136.1 4.0 %collective-permute-done.30 = bf16[2,256,2048]{2,1,0:T(8,128)(2,1)S(1)} collective-permute-done((bf16[2,256,2048]{2,1,0:T(8,128)(2,1)}, bf16[2,256,2048]{2,1,0:T(8,128)(2,1)S(1)}, u32[]{:S(2)}, u32[]{:S(2)}) %collective-permute-start.30) | collective-permute-done | bytes 2097184 | tf_op jit(solution)/shard_map/ppermute | solution.py:422
  143.0 1.7 collective-permute-start.32
  144.8 6.7 %head_grad_0.1 = (bf16[10240,2048]{1,0:T(8,128)(2,1)}, f32[8,128]{1,0:T(8,128)}) custom-call(bf16[128,2560]{1,0:T(8,128)(2,1)S(1)} %get-tuple-element.91.grad_ref, bf16[1280,2048]{1,0:T(8,128)(2,1)} %place_0.1.refs_0_, bf16[1280,2048]{1,0:T(8,128)(2,1)} %place_1.1.refs_1_), custom_call_target="tpu_custom_call" | custom-call | flops 2147483648 | bytes 10485760 | tf_op jit(solution)/shard_map/head_grad_0/pallas_call | solution.py:454
  154.3 1.6 collective-permute-start.34
  156.3 6.7 %head_grad_1.1 = (bf16[10240,2048]{1,0:T(8,128)(2,1)}, f32[8,128]{1,0:T(8,128)}) custom-call(bf16[128,2560]{1,0:T(8,128)(2,1)S(1)} %get-tuple-element.91.grad_ref, bf16[1280,2048]{1,0:T(8,128)(2,1)} %place_0.1.refs_0_, bf16[1280,2048]{1,0:T(8,128)(2,1)} %place_1.1.refs_1_, bf16[10240,2048]{1,0:T(8,128)(2,1)} %get-tuple-element.71.refs_2_), custom_call_target="tpu_custom_call", output_to_operand_aliasing={{0}: (3, {})} | custom-call | flops 2147483648 | bytes 10485760 | tf_op jit(solution)/shard_map/head_grad_1/pallas_call | solution.py:454
  164.5 1.6 collective-permute-start.36
  166.6 6.8 %head_grad_2.1 = (bf16[10240,2048]{1,0:T(8,128)(2,1)}, f32[8,128]{1,0:T(8,128)}) custom-call(bf16[128,2560]{1,0:T(8,128)(2,1)S(1)} %get-tuple-element.91.grad_ref, bf16[1280,2048]{1,0:T(8,128)(2,1)} %place_0.1.refs_0_, bf16[1280,2048]{1,0:T(8,128)(2,1)} %place_1.1.refs_1_, bf16[10240,2048]{1,0:T(8,128)(2,1)} %get-tuple-element.78.refs_2_), custom_call_target="tpu_custom_call", output_to_operand_aliasing={{0}: (3, {})} | custom-call | flops 2147483648 | bytes 10485760 | tf_op jit(solution)/shard_map/head_grad_2/pallas_call | solution.py:454
  174.8 1.6 collective-permute-start.38
  177.0 6.8 %head_grad_3.1 = (bf16[10240,2048]{1,0:T(8,128)(2,1)}, f32[8,128]{1,0:T(8,128)}) custom-call(bf16[128,2560]{1,0:T(8,128)(2,1)S(1)} %get-tuple-element.91.grad_ref, bf16[1280,2048]{1,0:T(8,128)(2,1)} %place_0.1.refs_0_, bf16[1280,2048]{1,0:T(8,128)(2,1)} %place_1.1.refs_1_, bf16[10240,2048]{1,0:T(8,128)(2,1)} %get-tuple-element.85.refs_2_), custom_call_target="tpu_custom_call", output_to_operand_aliasing={{0}: (3, {})} | custom-call | flops 2147483648 | bytes 10485760 | tf_op jit(solution)/shard_map/head_grad_3/pallas_call | solution.py:454
  187.2 6.7 %head_grad_4.1 = (bf16[10240,2048]{1,0:T(8,128)(2,1)}, f32[8,128]{1,0:T(8,128)}) custom-call(bf16[128,2560]{1,0:T(8,128)(2,1)S(1)} %get-tuple-element.91.grad_ref, bf16[1280,2048]{1,0:T(8,128)(2,1)} %place_0.1.refs_0_, bf16[1280,2048]{1,0:T(8,128)(2,1)} %place_1.1.refs_1_, bf16[10240,2048]{1,0:T(8,128)(2,1)} %get-tuple-element.92.refs_2_), custom_call_target="tpu_custom_call", output_to_operand_aliasing={{0}: (3, {})} | custom-call | flops 2147483648 | bytes 10485760 | tf_op jit(solution)/shard_map/head_grad_4/pallas_call | solution.py:454
  195.4 1.6 collective-permute-start.42
  198.4 9.5 %all_to_all.14 = f32[16,1,128]{2,1,0:T(1,128)S(1)} all-to-all(f32[16,1,128]{2,1,0:T(1,128)S(1)} %bitcast.70), channel_id=1, replica_groups=mesh['groups'=2,'x'=2,'core'=2,'voc'=4] {'x','core','voc'}, dimensions={0} | all-to-all | bytes 16384 | tf_op jit(solution)/shard_map/all_to_all | solution.py:434
  212.0 6.0 %collective-permute-done.44.refs_4_ = bf16[128,1024]{1,0:T(8,128)(2,1)S(1)} collective-permute-done((bf16[128,1024]{1,0:T(8,128)(2,1)S(1)}, bf16[128,1024]{1,0:T(8,128)(2,1)S(1)}, u32[]{:S(2)}, u32[]{:S(2)}) %collective-permute-start.44) | collective-permute-done | bytes 262176 | tf_op jit(solution)/shard_map/ppermute | solution.py:490
  (161 shorter events, 40.2 us)
Async XLA Ops:
  12.6 39.7 %all-to-all-start = ((bf16[16,176,128]{2,1,0:T(8,128)(2,1)}), bf16[16,176,128]{2,1,0:T(8,128)(2,1)S(1)}, u32[]{:S(2)}, u32[]{:S(2)}) async-start(bf16[16,176,128]{2,1,0:T(8,128)(2,1)} %maximum_dynamic-update-slice_fusion), calls=%async_computation | async-start | bytes 1441792 | tf_op jit(solution)/shard_map/all_to_all | solution.py:305
  20.0 20.9 %collective-permute-start.7 = (bf16[128,1024]{1,0:T(8,128)(2,1)S(1)}, bf16[128,1024]{1,0:T(8,128)(2,1)}, u32[]{:S(2)}, u32[]{:S(2)}) collective-permute-start(bf16[128,1024]{1,0:T(8,128)(2,1)S(1)} %get-tuple-element.107.refs_1_), channel_id=1, source_target_pairs={{0,8},{1,0},{2,1},{3,2},{11,3},{10,11},{9,10},{8,9},{4,12},{5,4},{... | collective-permute-start | bytes 786440 | tf_op jit(solution)/shard_map/ppermute | solution.py:224
  22.0 24.3 %collective-permute-start.3 = (bf16[128,1024]{1,0:T(8,128)(2,1)S(1)}, bf16[128,1024]{1,0:T(8,128)(2,1)S(1)}, u32[]{:S(2)}, u32[]{:S(2)}) collective-permute-start(bf16[128,1024]{1,0:T(8,128)(2,1)S(1)} %get-tuple-element.107.refs_1_), channel_id=1, source_target_pairs={{0,4},{4,0},{1,5},{5,1},{2,6},{6,2},{3,7},{7,3},{8,12},{12,8},{9,1... | collective-permute-start | bytes 786440 | tf_op jit(solution)/shard_map/ppermute | solution.py:220
  22.0 24.3 %collective-permute-start.1 = (bf16[128,1024]{1,0:T(8,128)(2,1)S(1)}, bf16[128,1024]{1,0:T(8,128)(2,1)S(1)}, u32[]{:S(2)}, u32[]{:S(2)}) collective-permute-start(bf16[128,1024]{1,0:T(8,128)(2,1)S(1)} %get-tuple-element.107.refs_1_), channel_id=1, source_target_pairs={{0,1},{1,2},{2,3},{3,11},{11,10},{10,9},{9,8},{8,0},{4,5},{5,6},{6... | collective-permute-start | bytes 786440 | tf_op jit(solution)/shard_map/ppermute | solution.py:224
  22.2 24.1 %collective-permute-start.6 = (bf16[128,1024]{1,0:T(8,128)(2,1)S(1)}, bf16[128,1024]{1,0:T(8,128)(2,1)S(1)}, u32[]{:S(2)}, u32[]{:S(2)}) collective-permute-start(bf16[128,1024]{1,0:T(8,128)(2,1)S(1)} %get-tuple-element.108.refs_0_), channel_id=1, source_target_pairs={{0,8},{1,0},{2,1},{3,2},{11,3},{10,11},{9,10},{8,9},{4,12},{5,4},{... | collective-permute-start | bytes 786440 | tf_op jit(solution)/shard_map/ppermute | solution.py:224
  24.0 27.7 %collective-permute-start.2 = (bf16[128,1024]{1,0:T(8,128)(2,1)S(1)}, bf16[128,1024]{1,0:T(8,128)(2,1)S(1)}, u32[]{:S(2)}, u32[]{:S(2)}) collective-permute-start(bf16[128,1024]{1,0:T(8,128)(2,1)S(1)} %get-tuple-element.108.refs_0_), channel_id=1, source_target_pairs={{0,4},{4,0},{1,5},{5,1},{2,6},{6,2},{3,7},{7,3},{8,12},{12,8},{9,1... | collective-permute-start | bytes 786440 | tf_op jit(solution)/shard_map/ppermute | solution.py:220
  40.8 12.1 %collective-permute-start = (bf16[128,1024]{1,0:T(8,128)(2,1)S(1)}, bf16[128,1024]{1,0:T(8,128)(2,1)S(1)}, u32[]{:S(2)}, u32[]{:S(2)}) collective-permute-start(bf16[128,1024]{1,0:T(8,128)(2,1)S(1)} %get-tuple-element.108.refs_0_), channel_id=1, source_target_pairs={{0,1},{1,2},{2,3},{3,11},{11,10},{10,9},{9,8},{8,0},{4,5},{5,6},{6... | collective-permute-start | bytes 786440 | tf_op jit(solution)/shard_map/ppermute | solution.py:224
  46.3 10.9 %collective-permute-start.9 = (bf16[128,1024]{1,0:T(8,128)(2,1)S(1)}, bf16[128,1024]{1,0:T(8,128)(2,1)}, u32[]{:S(2)}, u32[]{:S(2)}) collective-permute-start(bf16[128,1024]{1,0:T(8,128)(2,1)S(1)} %collective-permute-done.1.refs_3_), channel_id=1, source_target_pairs={{0,1},{1,2},{2,3},{3,11},{11,10},{10,9},{9,8},{8,0},{4,5},{5,6},{6... | collective-permute-start | bytes 786440 | tf_op jit(solution)/shard_map/ppermute | solution.py:224
  53.0 9.0 %collective-permute-start.14 = (bf16[128,1024]{1,0:T(8,128)(2,1)}, bf16[128,1024]{1,0:T(8,128)(2,1)S(1)}, u32[]{:S(2)}, u32[]{:S(2)}) collective-permute-start(bf16[128,1024]{1,0:T(8,128)(2,1)} %copy-done.9), channel_id=1, source_target_pairs={{0,8},{1,0},{2,1},{3,2},{11,3},{10,11},{9,10},{8,9},{4,12},{5,4},{... | collective-permute-start | bytes 786440 | tf_op jit(solution)/shard_map/ppermute | solution.py:224
  53.5 8.7 %collective-permute-start.10 = (bf16[128,1024]{1,0:T(8,128)(2,1)}, bf16[128,1024]{1,0:T(8,128)(2,1)}, u32[]{:S(2)}, u32[]{:S(2)}) collective-permute-start(bf16[128,1024]{1,0:T(8,128)(2,1)} %copy-done.9), channel_id=1, source_target_pairs={{0,4},{4,0},{1,5},{5,1},{2,6},{6,2},{3,7},{7,3},{8,12},{12,8},{9,1... | collective-permute-start | bytes 786440 | tf_op jit(solution)/shard_map/ppermute | solution.py:220
  53.6 9.9 %collective-permute-start.8 = (bf16[128,1024]{1,0:T(8,128)(2,1)S(1)}, bf16[128,1024]{1,0:T(8,128)(2,1)}, u32[]{:S(2)}, u32[]{:S(2)}) collective-permute-start(bf16[128,1024]{1,0:T(8,128)(2,1)S(1)} %collective-permute-done.refs_2_), channel_id=1, source_target_pairs={{0,1},{1,2},{2,3},{3,11},{11,10},{10,9},{9,8},{8,0},{4,5},{5,6},{6... | collective-permute-start | bytes 786440 | tf_op jit(solution)/shard_map/ppermute | solution.py:224
  57.3 8.8 %collective-permute-start.4 = (bf16[128,1024]{1,0:T(8,128)(2,1)S(1)}, bf16[128,1024]{1,0:T(8,128)(2,1)S(1)}, u32[]{:S(2)}, u32[]{:S(2)}) collective-permute-start(bf16[128,1024]{1,0:T(8,128)(2,1)S(1)} %collective-permute-done.refs_2_), channel_id=1, source_target_pairs={{0,4},{4,0},{1,5},{5,1},{2,6},{6,2},{3,7},{7,3},{8,12},{12,8},{9,1... | collective-permute-start | bytes 786440 | tf_op jit(solution)/shard_map/ppermute | solution.py:220
  57.5 8.9 %collective-permute-start.13 = (bf16[128,1024]{1,0:T(8,128)(2,1)}, bf16[128,1024]{1,0:T(8,128)(2,1)}, u32[]{:S(2)}, u32[]{:S(2)}) collective-permute-start(bf16[128,1024]{1,0:T(8,128)(2,1)} %collective-permute-done.9.refs_11_), channel_id=1, source_target_pairs={{0,4},{4,0},{1,5},{5,1},{2,6},{6,2},{3,7},{7,3},{8,12},{12,8},{9,1... | collective-permute-start | bytes 786440 | tf_op jit(solution)/shard_map/ppermute | solution.py:220
  62.0 15.3 %collective-permute-start.23 = (bf16[128,1024]{1,0:T(8,128)(2,1)S(1)}, bf16[128,1024]{1,0:T(8,128)(2,1)S(1)}, u32[]{:S(2)}, u32[]{:S(2)}) collective-permute-start(bf16[128,1024]{1,0:T(8,128)(2,1)S(1)} %collective-permute-done.15.refs_1_), channel_id=1, source_target_pairs={{0,8},{1,0},{2,1},{3,2},{11,3},{10,11},{9,10},{8,9},{4,12},{5,4},{... | collective-permute-start | bytes 786440 | tf_op jit(solution)/shard_map/ppermute | solution.py:224
  62.3 15.6 %collective-permute-start.19 = (bf16[128,1024]{1,0:T(8,128)(2,1)S(1)}, bf16[128,1024]{1,0:T(8,128)(2,1)S(1)}, u32[]{:S(2)}, u32[]{:S(2)}) collective-permute-start(bf16[128,1024]{1,0:T(8,128)(2,1)S(1)} %collective-permute-done.15.refs_1_), channel_id=1, source_target_pairs={{0,4},{4,0},{1,5},{5,1},{2,6},{6,2},{3,7},{7,3},{8,12},{12,8},{9,1... | collective-permute-start | bytes 786440 | tf_op jit(solution)/shard_map/ppermute | solution.py:220
  63.5 16.4 %collective-permute-start.17 = (bf16[128,1024]{1,0:T(8,128)(2,1)}, bf16[128,1024]{1,0:T(8,128)(2,1)S(1)}, u32[]{:S(2)}, u32[]{:S(2)}) collective-permute-start(bf16[128,1024]{1,0:T(8,128)(2,1)} %collective-permute-done.9.refs_11_), channel_id=1, source_target_pairs={{0,1},{1,2},{2,3},{3,11},{11,10},{10,9},{9,8},{8,0},{4,5},{5,6},{6... | collective-permute-start | bytes 786440 | tf_op jit(solution)/shard_map/ppermute | solution.py:224
  66.1 11.5 %collective-permute-start.16 = (bf16[128,1024]{1,0:T(8,128)(2,1)}, bf16[128,1024]{1,0:T(8,128)(2,1)S(1)}, u32[]{:S(2)}, u32[]{:S(2)}) collective-permute-start(bf16[128,1024]{1,0:T(8,128)(2,1)} %collective-permute-done.8.refs_10_), channel_id=1, source_target_pairs={{0,1},{1,2},{2,3},{3,11},{11,10},{10,9},{9,8},{8,0},{4,5},{5,6},{6... | collective-permute-start | bytes 786440 | tf_op jit(solution)/shard_map/ppermute | solution.py:224
  68.2 11.7 %collective-permute-start.22 = (bf16[128,1024]{1,0:T(8,128)(2,1)S(1)}, bf16[128,1024]{1,0:T(8,128)(2,1)}, u32[]{:S(2)}, u32[]{:S(2)}) collective-permute-start(bf16[128,1024]{1,0:T(8,128)(2,1)S(1)} %collective-permute-done.14.refs_0_), channel_id=1, source_target_pairs={{0,8},{1,0},{2,1},{3,2},{11,3},{10,11},{9,10},{8,9},{4,12},{5,4},{... | collective-permute-start | bytes 786440 | tf_op jit(solution)/shard_map/ppermute | solution.py:224
  77.8 8.4 %collective-permute-start.24 = (bf16[128,1024]{1,0:T(8,128)(2,1)S(1)}, bf16[128,1024]{1,0:T(8,128)(2,1)S(1)}, u32[]{:S(2)}, u32[]{:S(2)}) collective-permute-start(bf16[128,1024]{1,0:T(8,128)(2,1)S(1)} %collective-permute-done.16.refs_2_), channel_id=1, source_target_pairs={{0,1},{1,2},{2,3},{3,11},{11,10},{10,9},{9,8},{8,0},{4,5},{5,6},{6... | collective-permute-start | bytes 786440 | tf_op jit(solution)/shard_map/ppermute | solution.py:231
  79.9 8.5 %collective-permute-start.25 = (bf16[128,1024]{1,0:T(8,128)(2,1)S(1)}, bf16[128,1024]{1,0:T(8,128)(2,1)}, u32[]{:S(2)}, u32[]{:S(2)}) collective-permute-start(bf16[128,1024]{1,0:T(8,128)(2,1)S(1)} %collective-permute-done.23.refs_9_), channel_id=1, source_target_pairs={{0,8},{1,0},{2,1},{3,2},{11,3},{10,11},{9,10},{8,9},{4,12},{5,4},{... | collective-permute-start | bytes 786440 | tf_op jit(solution)/shard_map/ppermute | solution.py:231
  79.9 12.0 %collective-permute-start.20 = (bf16[128,1024]{1,0:T(8,128)(2,1)S(1)}, bf16[128,1024]{1,0:T(8,128)(2,1)S(1)}, u32[]{:S(2)}, u32[]{:S(2)}) collective-permute-start(bf16[128,1024]{1,0:T(8,128)(2,1)S(1)} %collective-permute-done.16.refs_2_), channel_id=1, source_target_pairs={{0,4},{4,0},{1,5},{5,1},{2,6},{6,2},{3,7},{7,3},{8,12},{12,8},{9,1... | collective-permute-start | bytes 786440 | tf_op jit(solution)/shard_map/ppermute | solution.py:220
  80.2 11.7 %collective-permute-start.21 = (bf16[128,1024]{1,0:T(8,128)(2,1)S(1)}, bf16[128,1024]{1,0:T(8,128)(2,1)}, u32[]{:S(2)}, u32[]{:S(2)}) collective-permute-start(bf16[128,1024]{1,0:T(8,128)(2,1)S(1)} %collective-permute-done.17.refs_3_), channel_id=1, source_target_pairs={{0,4},{4,0},{1,5},{5,1},{2,6},{6,2},{3,7},{7,3},{8,12},{12,8},{9,1... | collective-permute-start | bytes 786440 | tf_op jit(solution)/shard_map/ppermute | solution.py:220
  80.5 11.5 %collective-permute-start.26 = (bf16[128,1024]{1,0:T(8,128)(2,1)}, bf16[128,1024]{1,0:T(8,128)(2,1)}, u32[]{:S(2)}, u32[]{:S(2)}) collective-permute-start(bf16[128,1024]{1,0:T(8,128)(2,1)} %collective-permute-done.22.refs_8_), channel_id=1, source_target_pairs={{0,4},{4,0},{1,5},{5,1},{2,6},{6,2},{3,7},{7,3},{8,12},{12,8},{9,1... | collective-permute-start | bytes 786440 | tf_op jit(solution)/shard_map/ppermute | solution.py:220
  136.1 15.4 %collective-permute-start.31 = (bf16[2,256,2048]{2,1,0:T(8,128)(2,1)}, bf16[2,256,2048]{2,1,0:T(8,128)(2,1)S(1)}, u32[]{:S(2)}, u32[]{:S(2)}) collective-permute-start(bf16[2,256,2048]{2,1,0:T(8,128)(2,1)} %get-tuple-element.60), channel_id=1, source_target_pairs={{0,4},{4,0},{1,5},{5,1},{2,6},{6,2},{3,7},{7,3},{8,12},{12,8},{9,1... | collective-permute-start | bytes 6291464 | tf_op jit(solution)/shard_map/ppermute | solution.py:422
  142.7 8.8 %collective-permute-start.33 = (bf16[128,1024]{1,0:T(8,128)(2,1)S(1)}, bf16[128,1024]{1,0:T(8,128)(2,1)S(1)}, u32[]{:S(2)}, u32[]{:S(2)}) collective-permute-start(bf16[128,1024]{1,0:T(8,128)(2,1)S(1)} %get-tuple-element.63), channel_id=1, source_target_pairs={{0,8},{1,0},{2,1},{3,2},{11,3},{10,11},{9,10},{8,9},{4,12},{5,4},{... | collective-permute-start | bytes 786440 | tf_op jit(solution)/shard_map/ppermute | solution.py:490
  143.0 8.5 %collective-permute-start.32 = (bf16[128,1024]{1,0:T(8,128)(2,1)S(1)}, bf16[128,1024]{1,0:T(8,128)(2,1)S(1)}, u32[]{:S(2)}, u32[]{:S(2)}) collective-permute-start(bf16[128,1024]{1,0:T(8,128)(2,1)S(1)} %get-tuple-element.61), channel_id=1, source_target_pairs={{0,1},{1,2},{2,3},{3,11},{11,10},{10,9},{9,8},{8,0},{4,5},{5,6},{6... | collective-permute-start | bytes 786440 | tf_op jit(solution)/shard_map/ppermute | solution.py:490
  154.3 8.8 %collective-permute-start.34 = (bf16[128,1024]{1,0:T(8,128)(2,1)S(1)}, bf16[128,1024]{1,0:T(8,128)(2,1)S(1)}, u32[]{:S(2)}, u32[]{:S(2)}) collective-permute-start(bf16[128,1024]{1,0:T(8,128)(2,1)S(1)} %get-tuple-element.68), channel_id=1, source_target_pairs={{0,1},{1,2},{2,3},{3,11},{11,10},{10,9},{9,8},{8,0},{4,5},{5,6},{6... | collective-permute-start | bytes 786440 | tf_op jit(solution)/shard_map/ppermute | solution.py:490
  164.5 8.9 %collective-permute-start.36 = (bf16[128,1024]{1,0:T(8,128)(2,1)S(1)}, bf16[128,1024]{1,0:T(8,128)(2,1)S(1)}, u32[]{:S(2)}, u32[]{:S(2)}) collective-permute-start(bf16[128,1024]{1,0:T(8,128)(2,1)S(1)} %get-tuple-element.75), channel_id=1, source_target_pairs={{0,1},{1,2},{2,3},{3,11},{11,10},{10,9},{9,8},{8,0},{4,5},{5,6},{6... | collective-permute-start | bytes 786440 | tf_op jit(solution)/shard_map/ppermute | solution.py:490
  174.8 9.0 %collective-permute-start.38 = (bf16[128,1024]{1,0:T(8,128)(2,1)S(1)}, bf16[128,1024]{1,0:T(8,128)(2,1)S(1)}, u32[]{:S(2)}, u32[]{:S(2)}) collective-permute-start(bf16[128,1024]{1,0:T(8,128)(2,1)S(1)} %get-tuple-element.82), channel_id=1, source_target_pairs={{0,1},{1,2},{2,3},{3,11},{11,10},{10,9},{9,8},{8,0},{4,5},{5,6},{6... | collective-permute-start | bytes 786440 | tf_op jit(solution)/shard_map/ppermute | solution.py:490
  185.1 8.8 %collective-permute-start.40 = (bf16[128,1024]{1,0:T(8,128)(2,1)S(1)}, bf16[128,1024]{1,0:T(8,128)(2,1)S(1)}, u32[]{:S(2)}, u32[]{:S(2)}) collective-permute-start(bf16[128,1024]{1,0:T(8,128)(2,1)S(1)} %get-tuple-element.89), channel_id=1, source_target_pairs={{0,1},{1,2},{2,3},{3,11},{11,10},{10,9},{9,8},{8,0},{4,5},{5,6},{6... | collective-permute-start | bytes 786440 | tf_op jit(solution)/shard_map/ppermute | solution.py:490
  195.4 13.1 %collective-permute-start.42 = (bf16[128,1024]{1,0:T(8,128)(2,1)S(1)}, bf16[128,1024]{1,0:T(8,128)(2,1)S(1)}, u32[]{:S(2)}, u32[]{:S(2)}) collective-permute-start(bf16[128,1024]{1,0:T(8,128)(2,1)S(1)} %get-tuple-element.96), channel_id=1, source_target_pairs={{0,1},{1,2},{2,3},{3,11},{11,10},{10,9},{9,8},{8,0},{4,5},{5,6},{6... | collective-permute-start | bytes 786440 | tf_op jit(solution)/shard_map/ppermute | solution.py:490
  197.0 11.5 %collective-permute-start.43 = (bf16[128,1024]{1,0:T(8,128)(2,1)S(1)}, bf16[128,1024]{1,0:T(8,128)(2,1)S(1)}, u32[]{:S(2)}, u32[]{:S(2)}) collective-permute-start(bf16[128,1024]{1,0:T(8,128)(2,1)S(1)} %get-tuple-element.98), channel_id=1, source_target_pairs={{0,8},{1,0},{2,1},{3,2},{11,3},{10,11},{9,10},{8,9},{4,12},{5,4},{... | collective-permute-start | bytes 786440 | tf_op jit(solution)/shard_map/ppermute | solution.py:490
  (30 other events, 222.9 us)

commit v4 on v3

--- a/solution.py
+++ b/solution.py
@@ -18,11 +18,11 @@
 ALL = ("x", "core", "voc")
 CHIPS = ("x", "voc")
 RING_MOST = 8
-VMEM_LIMIT = 52 * 1024 * 1024
+MIB = 1024 * 1024
 NT = (((1,), (1,)), ((), ()))
 
 
-def call(kernel, name, grid, ins, outs, shapes, flops, moved, scratch=(), aliases=None):
+def call(kernel, name, grid, ins, outs, shapes, flops, moved, vmem, scratch=(), aliases=None):
     return pl.pallas_call(
         kernel,
         grid=grid,
@@ -32,7 +32,7 @@
         scratch_shapes=scratch,
         input_output_aliases=aliases or {},
         compiler_params=pltpu.CompilerParams(
-            dimension_semantics=("arbitrary",) * len(grid), vmem_limit_bytes=VMEM_LIMIT
+            dimension_semantics=("arbitrary",) * len(grid), vmem_limit_bytes=vmem * MIB
         ),
         cost_estimate=pl.CostEstimate(flops=flops, bytes_accessed=moved, transcendentals=0),
         name=name,
@@ -78,6 +78,20 @@
     rows = rows_ref[:, quad * ROWS : (quad + 1) * ROWS, columns]
     rows = rows.reshape(blocks * ROWS, rows.shape[-1]).astype(jnp.bfloat16)
     return jnp.dot(spread, rows, preferred_element_type=jnp.float32)
+
+
+def two_parts(values):
+    high = values.astype(jnp.bfloat16)
+    low = (values - high.astype(jnp.float32)).astype(jnp.bfloat16)
+    lane = lax.broadcasted_iota(jnp.int32, values.shape, 1)
+    return jnp.where(lane < LANES // 2, high.astype(jnp.float32), low.astype(jnp.float32)).astype(
+        jnp.bfloat16
+    )
+
+
+def joined(values):
+    values = values.astype(jnp.float32)
+    return values + pltpu.roll(values, LANES // 2, 1)
 
 
 def main_kernel(turn, steps, pairs, sums, scale_ref, head_ref, teacher_ref, map_ref, *refs):
@@ -139,30 +153,34 @@
 
     if not sums:
         return
-    loss_ref, *part_refs = loss_ref
+    part_refs = loss_ref
 
     @pl.when(step == steps - 1)
     def _():
-        quad_tokens = loss_ref.shape[1]
-        half = quad_tokens // 2
+        half = part_refs[0].shape[1]
+        width = rows_ref.shape[-1]
         for quad in range(2 * pairs):
             slots = map_ref[quad : quad + 1, :]
-            token = lax.broadcasted_iota(jnp.int32, (quad_tokens, slots.shape[1]), 0)
+            token = lax.broadcasted_iota(jnp.int32, (2 * half, slots.shape[1]), 0)
             spread = jnp.where(slots == token, 1.0, 0.0).astype(jnp.bfloat16)
-            loss_ref[quad] = sum_quad(spread, slot_loss_ref, quad, slice(0, BLOCK))
-            for start in range(0, rows_ref.shape[-1], COLS):
-                columns = slice(start, start + COLS)
-                total = sum_quad(spread, rows_ref, quad, columns).astype(jnp.bfloat16)
+
+            def put(columns, total):
                 part_refs[quad // 2][quad % 2, :, columns] = total[:half]
                 part_refs[pairs + quad // 2][quad % 2, :, columns] = total[half:]
 
-
-def head_kernel(turn, splits, pairs, grad_ref, *refs):
+            loss = sum_quad(spread, slot_loss_ref, quad, slice(0, LANES))
+            put(slice(width, width + LANES), two_parts(loss))
+            for start in range(0, width, COLS):
+                columns = slice(start, start + COLS)
+                put(columns, sum_quad(spread, rows_ref, quad, columns).astype(jnp.bfloat16))
+
+
+def head_kernel(turn, splits, shift, pairs, grad_ref, *refs):
     x_refs, (out_ref, mark_ref) = refs[:pairs], refs[-2:]
     joint = 2 if turn % 2 == 0 else 1
     slots = grad_ref.shape[1]
     share = turn // splits
-    place = in_block((1, slots), 1, pairs, joint) - pl.program_id(0) % splits * share
+    place = in_block((1, slots), 1, pairs, joint) - (pl.program_id(0) + shift) % splits * share
     grad = grad_ref[...]
     spaced = [grad * (place == index).astype(jnp.bfloat16) for index in range(share)]
     spaced = jnp.concatenate(spaced, axis=0)
@@ -179,11 +197,30 @@
     mark_ref[...] = jnp.zeros_like(mark_ref)
 
 
-def add_kernel(*refs):
-    *terms, right_ref, left_ref = refs
-    for way, out_ref in enumerate((right_ref, left_ref)):
-        total = sum(ref[...].reshape(out_ref.shape).astype(jnp.float32) for ref in terms[way::2])
-        out_ref[...] = total.astype(jnp.bfloat16)
+def add_kernel(last, *refs):
+    own_right, own_left, own_loss, other_right, other_left, other_loss = refs[:6]
+    half = own_right.shape[-1]
+    moved, outs = (refs[6:], ()) if len(refs) == 8 else (refs[6:8], refs[8:])
+    moved, outs = (moved, outs) if outs else ((), moved)
+
+    def whole(ref):
+        return ref[...].reshape(ref.shape[-2:]).astype(jnp.float32)
+
+    right = whole(own_right) + whole(other_right)
+    left = whole(own_left) + whole(other_left)
+    loss = joined(whole(own_loss)) + joined(whole(other_loss))
+    if moved:
+        right += moved[0][:, :half].astype(jnp.float32)
+        left += moved[1][...].astype(jnp.float32)
+        loss += joined(moved[0][:, half:])
+    if last:
+        outs[0][:, :half] = right.astype(jnp.bfloat16)
+        outs[0][:, half:] = left.astype(jnp.bfloat16)
+        outs[1][...] = loss
+    else:
+        outs[0][:, :half] = right.astype(jnp.bfloat16)
+        outs[0][:, half:] = two_parts(loss)
+        outs[1][...] = left.astype(jnp.bfloat16)
 
 
 def ring_order(rows, columns):
@@ -302,6 +339,8 @@
     sent = lax.dynamic_update_slice(
         send_teacher.reshape(devices, deep, BLOCK), send_meta, (0, meta_at, 0)
     )
+    if ring:
+        sent = after(sent, *held[1][0], *held[2][0])
     got = lax.all_to_all(sent, ALL, split_axis=0, concat_axis=0, tiled=True)
 
     lanes = jnp.stack([core, 1 - core])
@@ -349,6 +388,7 @@
                 jax.ShapeDtypeStruct((x_rows, width), jnp.bfloat16),
                 2 * x_rows * QUAD * tokens * width,
                 2 * x_rows * width * 2,
+                28,
             )(pick, *operands)
         )
 
@@ -358,14 +398,9 @@
     x_spec = pl.BlockSpec((turn * 2 * ROWS, width), lambda s: (s, 0))
     flops = 2 * blocks * per_block * BLOCK * width
     if ring:
-        part_spec = pl.BlockSpec((2, 2 * tokens, width), lambda s: (0, 0, 0), pipeline_mode=once)
-        part_shape = jax.ShapeDtypeStruct((2, 2 * tokens, width), jnp.bfloat16)
-        out_specs = [
-            pl.BlockSpec((quads, QUAD * tokens, BLOCK), lambda s: (0, 0, 0), pipeline_mode=once)
-        ] + [part_spec] * (2 * pairs)
-        out_shapes = [
-            jax.ShapeDtypeStruct((quads, QUAD * tokens, BLOCK), jnp.float32)
-        ] + [part_shape] * (2 * pairs)
+        part = (2, 2 * tokens, width + LANES)
+        out_specs = [pl.BlockSpec(part, lambda s: (0, 0, 0), pipeline_mode=once)] * (2 * pairs)
+        out_shapes = [jax.ShapeDtypeStruct(part, jnp.bfloat16)] * (2 * pairs)
         scratch = [
             pltpu.VMEM((blocks, per_block, width), jnp.float32),
             pltpu.VMEM((blocks, per_block, BLOCK), jnp.float32),
@@ -395,6 +430,7 @@
         [jax.ShapeDtypeStruct((BLOCK, blocks * per_block), jnp.bfloat16)] + out_shapes,
         16 * flops,
         head.size * 2 + pairs * x_rows * width * 2,
+        52,
         scratch,
     )(
         scale.reshape(1),
@@ -404,7 +440,7 @@
         *placed,
     )
     if ring:
-        loss, *parts = results
+        parts = results
     else:
         totals = []
         for value in results:
@@ -418,32 +454,21 @@
         parts = [total[pair, :, lane] for lane in range(2) for pair in range(pairs)]
     own_parts, other_parts = [], []
     for pair in range(pairs):
-        own_parts.append(parts[pair].reshape(4, tokens, width))
+        own_parts.append(parts[pair].reshape(4, tokens, -1))
         swapped = lax.ppermute(parts[pairs + pair], "core", [(0, 1), (1, 0)])
-        other_parts.append(swapped.reshape(4, tokens, width))
-
-    inverse = jnp.sum(
-        jnp.where(source_of[None, :] == jnp.arange(devices)[:, None], jnp.arange(devices)[None], 0),
-        axis=1,
-    )
-    loss = loss[:, :, 0].reshape(devices, tokens)
-    loss = loss.at[inverse].get(mode="promise_in_bounds")
-
-    def return_loss(behind=None):
-        sent = loss if behind is None else after(loss, behind)
-        back = lax.all_to_all(sent, ALL, split_axis=0, concat_axis=0, tiled=True)
-        return jnp.sum(back, axis=0)
-
-    lots = max(n for n in range(1, 6) if steps % n == 0)
-    lot = steps // lots
+        other_parts.append(swapped.reshape(4, tokens, -1))
+
     splits = 2 if turn % 4 == 0 else 1
+    lots = min(steps * splits, chips - 1)
+    cuts = [steps * splits * n // lots for n in range(lots + 1)]
     filled = []
 
     def fill(number, behind):
-        shift = number * lot
-        specs = [pl.BlockSpec((BLOCK, lane_slots), lambda s, d=shift: (0, s // splits + d))]
+        shift = cuts[number]
+        count = cuts[number + 1] - shift
+        specs = [pl.BlockSpec((BLOCK, lane_slots), lambda s, d=shift: (0, (s + d) // splits))]
         specs += [
-            pl.BlockSpec((turn * 2 * ROWS, width), lambda s, d=shift: (s // splits + d, 0))
+            pl.BlockSpec((turn * 2 * ROWS, width), lambda s, d=shift: ((s + d) // splits, 0))
         ] * pairs
         operands = [grad if behind is None else after(grad, behind), *placed]
         aliases = {}
@@ -452,14 +477,12 @@
             aliases = {len(operands): 0}
             operands.append(filled[-1])
         out, mark = call(
-            functools.partial(head_kernel, turn, splits, pairs),
+            functools.partial(head_kernel, turn, splits, shift, pairs),
             f"head_grad_{number}",
-            (lot * splits,),
+            (count,),
             specs,
             [
-                pl.BlockSpec(
-                    (turn // splits * BLOCK, width), lambda s, d=shift: (s + d * splits, 0)
-                ),
+                pl.BlockSpec((turn // splits * BLOCK, width), lambda s, d=shift: (s + d, 0)),
                 pl.BlockSpec((8, LANES), lambda s: (0, 0)),
             ],
             [
@@ -468,6 +491,7 @@
             ],
             turn * flops // lots,
             (head.size + pairs * x_rows * width) * 2 // lots,
+            28,
             aliases=aliases,
         )(*operands)
         filled.append(out)
@@ -479,33 +503,47 @@
         sums, mark = [], None
         for step in range(1, chips + 1):
             operands, specs = [], []
+            ends = [index_of[-step % chips], index_of[step % chips]]
+            places = [(ends[0], half, 0), (ends[1], half, 1), (ends[0], LANES, width // LANES)]
             for source in (own_parts, other_parts):
-                for way in range(2):
-                    at = index_of[(-step, step)[way] % chips]
+                for at, columns, where in places:
                     operands.append(source[at // 4])
                     specs.append(
-                        pl.BlockSpec((1, tokens, half), lambda s, a=at % 4, w=way: (a, 0, w))
+                        pl.BlockSpec(
+                            (1, tokens, columns), lambda s, a=at % 4, w=where: (a, 0, w)
+                        )
                     )
             for way in range(len(sums)):
                 moved = lax.ppermute(sums[way], CHIPS, circle.ways[way])
                 operands.append(moved if mark is None else after(moved, mark))
-                specs.append(pl.BlockSpec((tokens, half), lambda s: (0, 0)))
+                specs.append(pl.BlockSpec(moved.shape, lambda s: (0, 0)))
+            last = step == chips
+            out_types = [(width, jnp.bfloat16), (LANES, jnp.float32)]
+            if not last:
+                out_types = [(half + LANES, jnp.bfloat16), (half, jnp.bfloat16)]
             sums = call(
-                add_kernel,
+                functools.partial(add_kernel, last),
                 f"ring_sum_{step}",
                 (1,),
                 specs,
-                [pl.BlockSpec((tokens, half), lambda s: (0, 0))] * 2,
-                [jax.ShapeDtypeStruct((tokens, half), jnp.bfloat16)] * 2,
+                [pl.BlockSpec((tokens, columns), lambda s: (0, 0)) for columns, _ in out_types],
+                [jax.ShapeDtypeStruct((tokens, columns), kind) for columns, kind in out_types],
                 len(operands) * tokens * half,
                 len(operands) * tokens * half * 2,
+                16,
             )(*operands)
             mark = fill(step - 1, sums[1]) if step <= lots else None
-            if step == lots + 1:
-                mark = token_loss = return_loss(sums[1])
-        hidden_grad = jnp.concatenate(sums, axis=1)
+        hidden_grad, loss = sums
+        token_loss = loss[:, 0]
     else:
-        token_loss = return_loss()
+        inverse = jnp.sum(
+            jnp.where(source_of[None, :] == jnp.arange(devices)[:, None], jnp.arange(devices)[None], 0),
+            axis=1,
+        )
+        loss = loss[:, :, 0].reshape(devices, tokens)
+        loss = loss.at[inverse].get(mode="promise_in_bounds")
+        loss = lax.all_to_all(loss, ALL, split_axis=0, concat_axis=0, tiled=True)
+        token_loss = jnp.sum(loss, axis=0)
         total = [
             (own.astype(jnp.float32) + other.astype(jnp.float32)).astype(jnp.bfloat16)
             for own, other in zip(own_parts, other_parts)

time: 222 us -> 215 us (0.968)
  local copies, waits for them, and re-layouts: 9.61 us -> 32 us
  Pallas kernels: 95.6 us -> 78.2 us
  blocking collectives: 9.51 us -> 0 us
  waiting for transfers between devices: 37.5 us -> 43.6 us
  starting transfers between devices: 49.9 us -> 44.3 us
  other arithmetic: 11 us -> 8.18 us
    unnamed x32 -> x84, local copies, waits for them, and re-layouts: 3.5 us -> 24.4 us
    ppermute x12, waiting for transfers between devices: 19.4 us -> 1.24 us  [step(): lax.ppermute(piece, CHIPS, way)]
    all_to_all x1, waiting for transfers between devices: 0.01 us -> 14.7 us  [on_device(): got = lax.all_to_all(sent, ALL, split_axis=0, concat_axis=0, tiled=True)]
    pallas_call x13 -> x15, Pallas kernels: 44.7 us -> 31.2 us  [the longest x7 27.5 us: fill(): call(functools.partial(head_kernel, turn, splits, shift, pairs), f'head_g...]
    ppermute x14, waiting for transfers between devices: 6.3 us -> 17.2 us  [on_device(): moved = lax.ppermute(sums[way], CHIPS, circle.ways[way])]
    all_to_all x1 -> x0, blocking collectives: 9.51 us -> none  [return_loss(): back = lax.all_to_all(sent, ALL, split_axis=0, concat_axis=0, tiled=True)]
    ppermute x12, starting transfers between devices: 23.4 us -> 17.5 us  [step(): lax.ppermute(piece, CHIPS, way)]
    pallas_call x2, Pallas kernels: 14.6 us -> 10.9 us  [on_device(): call(functools.partial(place_kernel, layout), f'place_{pair}', (blocks //...]
  transfers between devices with their start and end apart: 47 -> 47, of which waited for: 9 -> 16; matrix products, arithmetic and copies ran while one was open for 5% -> 8% of each run, Pallas kernels for 19% -> 15%
where the time goes in v4:
time: 215 us; the launch traced here: 214 us
  Pallas kernels  78.2 us (36%)
  starting transfers between devices  44.3 us (21%)
  waiting for transfers between devices  43.6 us (20%)
  local copies, waits for them, and re-layouts  32 us (15%)
  other arithmetic  8.18 us (4%)
  between operations  4.38 us (2%)
  matrix products  2.92 us (1%)
    pallas_call x1, Pallas kernels, on_device(): call(functools.partial(main_kernel, turn, steps, pairs, ring), 'logits_an...  36.2 us
    pallas_call x7, Pallas kernels, fill(): call(functools.partial(head_kernel, turn, splits, shift, pairs), f'head_g...  27.5 us
    unnamed x84, local copies, waits for them, and re-layouts  24.4 us
    ppermute x12, starting transfers between devices, step(): lax.ppermute(piece, CHIPS, way)  17.5 us
    ppermute x14, waiting for transfers between devices, on_device(): moved = lax.ppermute(sums[way], CHIPS, circle.ways[way])  17.2 us
    all_to_all x1, waiting for transfers between devices, on_device(): got = lax.all_to_all(sent, ALL, split_axis=0, concat_axis=0, tiled=True)  14.7 us
    ppermute x14, starting transfers between devices, on_device(): moved = lax.ppermute(sums[way], CHIPS, circle.ways[way])  14.5 us
    pallas_call x2, Pallas kernels, on_device(): call(functools.partial(place_kernel, layout), f'place_{pair}', (blocks //...  10.9 us
  transfers between devices with their start and end apart: 47, of which 16 were waited for; matrix products, arithmetic and copies ran while one was open for 8% of the time, Pallas kernels for 15%

profile of v4, /device:TPU:0, one launch (start us, length us, event | category | flops | bytes accessed | tf_op | source)
XLA Modules:
  0.0 213.7 jit_solution(16163229987615747764)
XLA Ops:
  1.8 3.0 %collective-permute-start.3 = (bf16[128,1024]{1,0:T(8,128)(2,1)S(1)}, bf16[128,1024]{1,0:T(8,128)(2,1)S(1)}, u32[]{:S(2)}, u32[]{:S(2)}) collective-permute-start(bf16[128,1024]{1,0:T(8,128)(2,1)S(1)} %get-tuple-element.121.refs_1_), channel_id=1, source_target_pairs={{0,8},{1,0},{2,1},{3,2},{11,3},{10,11},{9,10},{8,9},{4,12},{5,4},{... | collective-permute-start | bytes 786440 | tf_op jit(solution)/shard_map/ppermute | solution.py:261
  4.9 1.9 collective-permute-start.2
  10.9 2.9 %fusion.4 = bf16[2816,128]{1,0:T(8,128)(2,1)} fusion(s32[1024]{0:T(1024)S(1)} %get-tuple-element.124, bf16[128,8,128]{2,1,0:T(8,128)(2,1)S(1)} %copy-done), kind=kOutput, calls=%fused_computation.12 | convolution fusion | flops 741441536 | bytes 987136 | tf_op jit(solution)/shard_map/dot_general | solution.py:320
  18.2 6.3 %all-to-all-start = ((bf16[16,176,128]{2,1,0:T(8,128)(2,1)}), bf16[16,176,128]{2,1,0:T(8,128)(2,1)S(1)}, u32[]{:S(2)}, u32[]{:S(2)}) async-start(bf16[16,176,128]{2,1,0:T(8,128)(2,1)} %maximum_dynamic-update-slice_fusion), calls=%async_computation | async-start | bytes 1441792 | tf_op jit(solution)/shard_map/all_to_all | solution.py:344
  27.3 1.9 collective-permute-start.15
  29.8 14.7 %all-to-all-done = bf16[16,176,128]{2,1,0:T(8,128)(2,1)S(1)} async-done(((bf16[16,176,128]{2,1,0:T(8,128)(2,1)}), bf16[16,176,128]{2,1,0:T(8,128)(2,1)S(1)}, u32[]{:S(2)}, u32[]{:S(2)}) %all-to-all-start) | async-done | bytes 720928 | tf_op jit(solution)/shard_map/all_to_all | solution.py:344
  47.0 3.8 %collective-permute-start.8 = (bf16[128,1024]{1,0:T(8,128)(2,1)S(1)}, bf16[128,1024]{1,0:T(8,128)(2,1)}, u32[]{:S(2)}, u32[]{:S(2)}) collective-permute-start(bf16[128,1024]{1,0:T(8,128)(2,1)S(1)} %collective-permute-done.refs_2_), channel_id=1, source_target_pairs={{0,1},{1,2},{2,3},{3,11},{11,10},{10,9},{9,8},{8,0},{4,5},{5,6},{6... | collective-permute-start | bytes 786440 | tf_op jit(solution)/shard_map/ppermute | solution.py:261
  57.0 2.6 %collective-permute-start.17 = (bf16[128,1024]{1,0:T(8,128)(2,1)}, bf16[128,1024]{1,0:T(8,128)(2,1)}, u32[]{:S(2)}, u32[]{:S(2)}) collective-permute-start(bf16[128,1024]{1,0:T(8,128)(2,1)} %collective-permute-done.9.refs_11_), channel_id=1, source_target_pairs={{0,1},{1,2},{2,3},{3,11},{11,10},{10,9},{9,8},{8,0},{4,5},{5,6},{6... | collective-permute-start | bytes 786440 | tf_op jit(solution)/shard_map/ppermute | solution.py:261
  63.1 1.7 collective-permute-start.22
  74.4 4.9 %place_0.1.refs_0_ = bf16[1280,2048]{1,0:T(8,128)(2,1)S(1)} custom-call(bf16[4,640,512]{2,1,0:T(8,128)(2,1)S(1)} %fusion.2.pick_ref, bf16[128,1024]{1,0:T(8,128)(2,1)S(1)} %get-tuple-element.122.refs_0_, bf16[128,1024]{1,0:T(8,128)(2,1)S(1)} %get-tuple-element.121.refs_1_, bf16[128,1024]{1,0:T(8,128)(2,1)S(1)} %copy-done.13, ...), custom_call_target="tpu_custom_call" | custom-call | flops 2684354560 | bytes 10485760 | tf_op jit(solution)/shard_map/place_0/pallas_call | solution.py:381
  79.3 2.3 %copy-done.2 = bf16[1280,2048]{1,0:T(8,128)(2,1)} copy-done((bf16[1280,2048]{1,0:T(8,128)(2,1)}, bf16[1280,2048]{1,0:T(8,128)(2,1)S(1)}, u32[]{:S(2)}) %copy-start.2) | copy-done | bytes 5242904
  83.2 1.7 collective-permute-start.25
  86.2 5.3 %collective-permute-done.24.refs_10_ = bf16[128,1024]{1,0:T(8,128)(2,1)} collective-permute-done((bf16[128,1024]{1,0:T(8,128)(2,1)}, bf16[128,1024]{1,0:T(8,128)(2,1)}, u32[]{:S(2)}, u32[]{:S(2)}) %collective-permute-start.24) | collective-permute-done | bytes 262176 | tf_op jit(solution)/shard_map/ppermute | solution.py:268
  99.3 6.0 %place_1.1.refs_1_ = bf16[1280,2048]{1,0:T(8,128)(2,1)S(1)} custom-call(bf16[4,640,512]{2,1,0:T(8,128)(2,1)S(1)} %fusion.2.pick_ref, bf16[128,1024]{1,0:T(8,128)(2,1)} %collective-permute-done.14.refs_0_, bf16[128,1024]{1,0:T(8,128)(2,1)} %collective-permute-done.15.refs_1_, bf16[128,1024]{1,0:T(8,128)(2,1)} %collective-permute-done.16.refs_2_, ...), custom_call_target="tpu_custom_call" | custom-call | flops 2684354560 | bytes 10485760 | tf_op jit(solution)/shard_map/place_1/pallas_call | solution.py:381
  105.3 2.3 %copy-done.3 = bf16[1280,2048]{1,0:T(8,128)(2,1)} copy-done((bf16[1280,2048]{1,0:T(8,128)(2,1)}, bf16[1280,2048]{1,0:T(8,128)(2,1)S(1)}, u32[]{:S(2)}) %copy-start.3) | copy-done | bytes 5242904
  107.7 36.2 %logits_and_back.1 = (bf16[128,2560]{1,0:T(8,128)(2,1)S(1)}, bf16[2,256,2176]{2,1,0:T(8,128)(2,1)}, bf16[2,256,2176]{2,1,0:T(8,128)(2,1)}, bf16[2,256,2176]{2,1,0:T(8,128)(2,1)}, bf16[2,256,2176]{2,1,0:T(8,128)(2,1)}) custom-call(f32[1]{0:T(128)} %bitcast.6.scale_ref, bf16[10240,2048]{1,0:T(8,128)(2,1)} %head_ref.1, bf16[2560,128]{1,0:T(8,128)(2,1)S(1)} %bitcast.77, ...), custom_call_target="tpu_custom_call" | custom-call | flops 21474836480 | bytes 52428800 | tf_op jit(solution)/shard_map/logits_and_back/pallas_call | solution.py:418
  144.3 4.0 %collective-permute-done.30 = bf16[2,256,2176]{2,1,0:T(8,128)(2,1)S(1)} collective-permute-done((bf16[2,256,2176]{2,1,0:T(8,128)(2,1)}, bf16[2,256,2176]{2,1,0:T(8,128)(2,1)S(1)}, u32[]{:S(2)}, u32[]{:S(2)}) %collective-permute-start.30) | collective-permute-done | bytes 2228256 | tf_op jit(solution)/shard_map/ppermute | solution.py:458
  148.4 1.6 copy-done.5
  150.6 1.7 collective-permute-start.33
  152.5 2.8 %head_grad_0.1 = (bf16[10240,2048]{1,0:T(8,128)(2,1)}, f32[8,128]{1,0:T(8,128)}) custom-call(bf16[128,2560]{1,0:T(8,128)(2,1)S(1)} %get-tuple-element.113.grad_ref, bf16[1280,2048]{1,0:T(8,128)(2,1)S(1)} %bitcast.28, bf16[1280,2048]{1,0:T(8,128)(2,1)S(1)} %copy-done.4), custom_call_target="tpu_custom_call" | custom-call | flops 1533916928 | bytes 7489828 | tf_op jit(solution)/shard_map/head_grad_0/pallas_call | solution.py:479
  155.3 3.4 %collective-permute-done.33.refs_7_ = bf16[128,1024]{1,0:T(8,128)(2,1)S(1)} collective-permute-done((bf16[128,1024]{1,0:T(8,128)(2,1)S(1)}, bf16[128,1024]{1,0:T(8,128)(2,1)S(1)}, u32[]{:S(2)}, u32[]{:S(2)}) %collective-permute-start.33) | collective-permute-done | bytes 262176 | tf_op jit(solution)/shard_map/ppermute | solution.py:517
  160.1 1.7 collective-permute-start.35
  161.8 4.1 %head_grad_1.1 = (bf16[10240,2048]{1,0:T(8,128)(2,1)}, f32[8,128]{1,0:T(8,128)}) custom-call(bf16[128,2560]{1,0:T(8,128)(2,1)S(1)} %get-tuple-element.113.grad_ref, bf16[1280,2048]{1,0:T(8,128)(2,1)S(1)} %bitcast.28, bf16[1280,2048]{1,0:T(8,128)(2,1)S(1)} %copy-done.4, bf16[10240,2048]{1,0:T(8,128)(2,1)} %get-tuple-element.79.refs_2_), custom_call_target="tpu_custom_call", output_to_operand_aliasing={{0}: (3, {})} | custom-call | flops 1533916928 | bytes 7489828 | tf_op jit(solution)/shard_map/head_grad_1/pallas_call | solution.py:479
  165.9 1.7 collective-permute-done.35.refs_7_
  170.5 4.1 %head_grad_2.1 = (bf16[10240,2048]{1,0:T(8,128)(2,1)}, f32[8,128]{1,0:T(8,128)}) custom-call(bf16[128,2560]{1,0:T(8,128)(2,1)S(1)} %get-tuple-element.113.grad_ref, bf16[1280,2048]{1,0:T(8,128)(2,1)S(1)} %bitcast.28, bf16[1280,2048]{1,0:T(8,128)(2,1)S(1)} %copy-done.4, bf16[10240,2048]{1,0:T(8,128)(2,1)} %get-tuple-element.86.refs_2_), custom_call_target="tpu_custom_call", output_to_operand_aliasing={{0}: (3, {})} | custom-call | flops 1533916928 | bytes 7489828 | tf_op jit(solution)/shard_map/head_grad_2/pallas_call | solution.py:479
  178.4 4.1 %head_grad_3.1 = (bf16[10240,2048]{1,0:T(8,128)(2,1)}, f32[8,128]{1,0:T(8,128)}) custom-call(bf16[128,2560]{1,0:T(8,128)(2,1)S(1)} %get-tuple-element.113.grad_ref, bf16[1280,2048]{1,0:T(8,128)(2,1)S(1)} %bitcast.28, bf16[1280,2048]{1,0:T(8,128)(2,1)S(1)} %copy-done.4, bf16[10240,2048]{1,0:T(8,128)(2,1)} %get-tuple-element.93.refs_2_), custom_call_target="tpu_custom_call", output_to_operand_aliasing={{0}: (3, {})} | custom-call | flops 1533916928 | bytes 7489828 | tf_op jit(solution)/shard_map/head_grad_3/pallas_call | solution.py:479
  186.4 4.1 %head_grad_4.1 = (bf16[10240,2048]{1,0:T(8,128)(2,1)}, f32[8,128]{1,0:T(8,128)}) custom-call(bf16[128,2560]{1,0:T(8,128)(2,1)S(1)} %get-tuple-element.113.grad_ref, bf16[1280,2048]{1,0:T(8,128)(2,1)S(1)} %bitcast.28, bf16[1280,2048]{1,0:T(8,128)(2,1)S(1)} %copy-done.4, bf16[10240,2048]{1,0:T(8,128)(2,1)} %get-tuple-element.100.refs_2_), custom_call_target="tpu_custom_call", output_to_operand_aliasing={{0}: (3, {})} | custom-call | flops 1533916928 | bytes 7489828 | tf_op jit(solution)/shard_map/head_grad_4/pallas_call | solution.py:479
  190.5 2.5 %collective-permute-done.41.refs_7_ = bf16[128,1024]{1,0:T(8,128)(2,1)S(1)} collective-permute-done((bf16[128,1024]{1,0:T(8,128)(2,1)S(1)}, bf16[128,1024]{1,0:T(8,128)(2,1)S(1)}, u32[]{:S(2)}, u32[]{:S(2)}) %collective-permute-start.41) | collective-permute-done | bytes 262176 | tf_op jit(solution)/shard_map/ppermute | solution.py:517
  193.4 1.9 collective-permute-start.42
  195.5 4.1 %head_grad_5.1 = (bf16[10240,2048]{1,0:T(8,128)(2,1)}, f32[8,128]{1,0:T(8,128)}) custom-call(bf16[128,2560]{1,0:T(8,128)(2,1)S(1)} %get-tuple-element.113.grad_ref, bf16[1280,2048]{1,0:T(8,128)(2,1)S(1)} %bitcast.28, bf16[1280,2048]{1,0:T(8,128)(2,1)S(1)} %copy-done.4, bf16[10240,2048]{1,0:T(8,128)(2,1)} %get-tuple-element.107.refs_2_), custom_call_target="tpu_custom_call", output_to_operand_aliasing={{0}: (3, {})} | custom-call | flops 1533916928 | bytes 7489828 | tf_op jit(solution)/shard_map/head_grad_5/pallas_call | solution.py:479
  199.6 4.6 %collective-permute-done.43.refs_7_ = bf16[128,1024]{1,0:T(8,128)(2,1)S(1)} collective-permute-done((bf16[128,1024]{1,0:T(8,128)(2,1)S(1)}, bf16[128,1024]{1,0:T(8,128)(2,1)S(1)}, u32[]{:S(2)}, u32[]{:S(2)}) %collective-permute-start.43) | collective-permute-done | bytes 262176 | tf_op jit(solution)/shard_map/ppermute | solution.py:517
  206.6 4.1 %head_grad_6.1 = (bf16[10240,2048]{1,0:T(8,128)(2,1)}, f32[8,128]{1,0:T(8,128)}) custom-call(bf16[128,2560]{1,0:T(8,128)(2,1)S(1)} %get-tuple-element.113.grad_ref, bf16[1280,2048]{1,0:T(8,128)(2,1)S(1)} %bitcast.28, bf16[1280,2048]{1,0:T(8,128)(2,1)S(1)} %copy-done.4, bf16[10240,2048]{1,0:T(8,128)(2,1)} %get-tuple-element.114.refs_2_), custom_call_target="tpu_custom_call", output_to_operand_aliasing={{0}: (3, {})} | custom-call | flops 1533916928 | bytes 7489828 | tf_op jit(solution)/shard_map/head_grad_6/pallas_call | solution.py:479
  (207 shorter events, 61.1 us)
Async XLA Ops:
  1.8 16.3 %collective-permute-start.3 = (bf16[128,1024]{1,0:T(8,128)(2,1)S(1)}, bf16[128,1024]{1,0:T(8,128)(2,1)S(1)}, u32[]{:S(2)}, u32[]{:S(2)}) collective-permute-start(bf16[128,1024]{1,0:T(8,128)(2,1)S(1)} %get-tuple-element.121.refs_1_), channel_id=1, source_target_pairs={{0,8},{1,0},{2,1},{3,2},{11,3},{10,11},{9,10},{8,9},{4,12},{5,4},{... | collective-permute-start | bytes 786440 | tf_op jit(solution)/shard_map/ppermute | solution.py:261
  4.8 13.3 %collective-permute-start.1 = (bf16[128,1024]{1,0:T(8,128)(2,1)S(1)}, bf16[128,1024]{1,0:T(8,128)(2,1)S(1)}, u32[]{:S(2)}, u32[]{:S(2)}) collective-permute-start(bf16[128,1024]{1,0:T(8,128)(2,1)S(1)} %get-tuple-element.121.refs_1_), channel_id=1, source_target_pairs={{0,1},{1,2},{2,3},{3,11},{11,10},{10,9},{9,8},{8,0},{4,5},{5,6},{6... | collective-permute-start | bytes 786440 | tf_op jit(solution)/shard_map/ppermute | solution.py:261
  4.9 13.2 %collective-permute-start.2 = (bf16[128,1024]{1,0:T(8,128)(2,1)S(1)}, bf16[128,1024]{1,0:T(8,128)(2,1)S(1)}, u32[]{:S(2)}, u32[]{:S(2)}) collective-permute-start(bf16[128,1024]{1,0:T(8,128)(2,1)S(1)} %get-tuple-element.122.refs_0_), channel_id=1, source_target_pairs={{0,8},{1,0},{2,1},{3,2},{11,3},{10,11},{9,10},{8,9},{4,12},{5,4},{... | collective-permute-start | bytes 786440 | tf_op jit(solution)/shard_map/ppermute | solution.py:261
  6.8 11.4 %collective-permute-start = (bf16[128,1024]{1,0:T(8,128)(2,1)S(1)}, bf16[128,1024]{1,0:T(8,128)(2,1)S(1)}, u32[]{:S(2)}, u32[]{:S(2)}) collective-permute-start(bf16[128,1024]{1,0:T(8,128)(2,1)S(1)} %get-tuple-element.122.refs_0_), channel_id=1, source_target_pairs={{0,1},{1,2},{2,3},{3,11},{11,10},{10,9},{9,8},{8,0},{4,5},{5,6},{6... | collective-permute-start | bytes 786440 | tf_op jit(solution)/shard_map/ppermute | solution.py:261
  18.2 26.4 %all-to-all-start = ((bf16[16,176,128]{2,1,0:T(8,128)(2,1)}), bf16[16,176,128]{2,1,0:T(8,128)(2,1)S(1)}, u32[]{:S(2)}, u32[]{:S(2)}) async-start(bf16[16,176,128]{2,1,0:T(8,128)(2,1)} %maximum_dynamic-update-slice_fusion), calls=%async_computation | async-start | bytes 1441792 | tf_op jit(solution)/shard_map/all_to_all | solution.py:344
  24.9 21.1 %collective-permute-start.4 = (bf16[128,1024]{1,0:T(8,128)(2,1)S(1)}, bf16[128,1024]{1,0:T(8,128)(2,1)S(1)}, u32[]{:S(2)}, u32[]{:S(2)}) collective-permute-start(bf16[128,1024]{1,0:T(8,128)(2,1)S(1)} %get-tuple-element.122.refs_0_), channel_id=1, source_target_pairs={{0,4},{4,0},{1,5},{5,1},{2,6},{6,2},{3,7},{7,3},{8,12},{12,8},{9,1... | collective-permute-start | bytes 786440 | tf_op jit(solution)/shard_map/ppermute | solution.py:257
  27.3 19.3 %collective-permute-start.15 = (bf16[128,1024]{1,0:T(8,128)(2,1)S(1)}, bf16[128,1024]{1,0:T(8,128)(2,1)}, u32[]{:S(2)}, u32[]{:S(2)}) collective-permute-start(bf16[128,1024]{1,0:T(8,128)(2,1)S(1)} %collective-permute-done.3.refs_9_), channel_id=1, source_target_pairs={{0,8},{1,0},{2,1},{3,2},{11,3},{10,11},{9,10},{8,9},{4,12},{5,4},{... | collective-permute-start | bytes 786440 | tf_op jit(solution)/shard_map/ppermute | solution.py:261
  29.2 17.8 %collective-permute-start.11 = (bf16[128,1024]{1,0:T(8,128)(2,1)S(1)}, bf16[128,1024]{1,0:T(8,128)(2,1)S(1)}, u32[]{:S(2)}, u32[]{:S(2)}) collective-permute-start(bf16[128,1024]{1,0:T(8,128)(2,1)S(1)} %collective-permute-done.3.refs_9_), channel_id=1, source_target_pairs={{0,4},{4,0},{1,5},{5,1},{2,6},{6,2},{3,7},{7,3},{8,12},{12,8},{9,1... | collective-permute-start | bytes 786440 | tf_op jit(solution)/shard_map/ppermute | solution.py:257
  29.2 21.6 %collective-permute-start.9 = (bf16[128,1024]{1,0:T(8,128)(2,1)S(1)}, bf16[128,1024]{1,0:T(8,128)(2,1)}, u32[]{:S(2)}, u32[]{:S(2)}) collective-permute-start(bf16[128,1024]{1,0:T(8,128)(2,1)S(1)} %collective-permute-done.1.refs_3_), channel_id=1, source_target_pairs={{0,1},{1,2},{2,3},{3,11},{11,10},{10,9},{9,8},{8,0},{4,5},{5,6},{6... | collective-permute-start | bytes 786440 | tf_op jit(solution)/shard_map/ppermute | solution.py:261
  29.4 21.6 %collective-permute-start.7 = (bf16[128,1024]{1,0:T(8,128)(2,1)S(1)}, bf16[128,1024]{1,0:T(8,128)(2,1)S(1)}, u32[]{:S(2)}, u32[]{:S(2)}) collective-permute-start(bf16[128,1024]{1,0:T(8,128)(2,1)S(1)} %collective-permute-done.1.refs_3_), channel_id=1, source_target_pairs={{0,4},{4,0},{1,5},{5,1},{2,6},{6,2},{3,7},{7,3},{8,12},{12,8},{9,1... | collective-permute-start | bytes 786440 | tf_op jit(solution)/shard_map/ppermute | solution.py:257
  46.0 8.3 %collective-permute-start.14 = (bf16[128,1024]{1,0:T(8,128)(2,1)S(1)}, bf16[128,1024]{1,0:T(8,128)(2,1)}, u32[]{:S(2)}, u32[]{:S(2)}) collective-permute-start(bf16[128,1024]{1,0:T(8,128)(2,1)S(1)} %collective-permute-done.2.refs_8_), channel_id=1, source_target_pairs={{0,8},{1,0},{2,1},{3,2},{11,3},{10,11},{9,10},{8,9},{4,12},{5,4},{... | collective-permute-start | bytes 786440 | tf_op jit(solution)/shard_map/ppermute | solution.py:261
  46.6 9.0 %collective-permute-start.10 = (bf16[128,1024]{1,0:T(8,128)(2,1)S(1)}, bf16[128,1024]{1,0:T(8,128)(2,1)S(1)}, u32[]{:S(2)}, u32[]{:S(2)}) collective-permute-start(bf16[128,1024]{1,0:T(8,128)(2,1)S(1)} %collective-permute-done.2.refs_8_), channel_id=1, source_target_pairs={{0,4},{4,0},{1,5},{5,1},{2,6},{6,2},{3,7},{7,3},{8,12},{12,8},{9,1... | collective-permute-start | bytes 786440 | tf_op jit(solution)/shard_map/ppermute | solution.py:257
  47.0 10.0 %collective-permute-start.8 = (bf16[128,1024]{1,0:T(8,128)(2,1)S(1)}, bf16[128,1024]{1,0:T(8,128)(2,1)}, u32[]{:S(2)}, u32[]{:S(2)}) collective-permute-start(bf16[128,1024]{1,0:T(8,128)(2,1)S(1)} %collective-permute-done.refs_2_), channel_id=1, source_target_pairs={{0,1},{1,2},{2,3},{3,11},{11,10},{10,9},{9,8},{8,0},{4,5},{5,6},{6... | collective-permute-start | bytes 786440 | tf_op jit(solution)/shard_map/ppermute | solution.py:261
  50.8 8.8 %collective-permute-start.6 = (bf16[128,1024]{1,0:T(8,128)(2,1)S(1)}, bf16[128,1024]{1,0:T(8,128)(2,1)S(1)}, u32[]{:S(2)}, u32[]{:S(2)}) collective-permute-start(bf16[128,1024]{1,0:T(8,128)(2,1)S(1)} %collective-permute-done.refs_2_), channel_id=1, source_target_pairs={{0,4},{4,0},{1,5},{5,1},{2,6},{6,2},{3,7},{7,3},{8,12},{12,8},{9,1... | collective-permute-start | bytes 786440 | tf_op jit(solution)/shard_map/ppermute | solution.py:257
  51.7 8.9 %collective-permute-start.13 = (bf16[128,1024]{1,0:T(8,128)(2,1)}, bf16[128,1024]{1,0:T(8,128)(2,1)S(1)}, u32[]{:S(2)}, u32[]{:S(2)}) collective-permute-start(bf16[128,1024]{1,0:T(8,128)(2,1)} %collective-permute-done.9.refs_11_), channel_id=1, source_target_pairs={{0,4},{4,0},{1,5},{5,1},{2,6},{6,2},{3,7},{7,3},{8,12},{12,8},{9,1... | collective-permute-start | bytes 786440 | tf_op jit(solution)/shard_map/ppermute | solution.py:257
  54.4 27.3 %collective-permute-start.23 = (bf16[128,1024]{1,0:T(8,128)(2,1)}, bf16[128,1024]{1,0:T(8,128)(2,1)S(1)}, u32[]{:S(2)}, u32[]{:S(2)}) collective-permute-start(bf16[128,1024]{1,0:T(8,128)(2,1)} %collective-permute-done.15.refs_1_), channel_id=1, source_target_pairs={{0,8},{1,0},{2,1},{3,2},{11,3},{10,11},{9,10},{8,9},{4,12},{5,4},{... | collective-permute-start | bytes 786440 | tf_op jit(solution)/shard_map/ppermute | solution.py:261
  56.3 25.9 %collective-permute-start.19 = (bf16[128,1024]{1,0:T(8,128)(2,1)}, bf16[128,1024]{1,0:T(8,128)(2,1)S(1)}, u32[]{:S(2)}, u32[]{:S(2)}) collective-permute-start(bf16[128,1024]{1,0:T(8,128)(2,1)} %collective-permute-done.15.refs_1_), channel_id=1, source_target_pairs={{0,4},{4,0},{1,5},{5,1},{2,6},{6,2},{3,7},{7,3},{8,12},{12,8},{9,1... | collective-permute-start | bytes 786440 | tf_op jit(solution)/shard_map/ppermute | solution.py:257
  57.0 26.2 %collective-permute-start.17 = (bf16[128,1024]{1,0:T(8,128)(2,1)}, bf16[128,1024]{1,0:T(8,128)(2,1)}, u32[]{:S(2)}, u32[]{:S(2)}) collective-permute-start(bf16[128,1024]{1,0:T(8,128)(2,1)} %collective-permute-done.9.refs_11_), channel_id=1, source_target_pairs={{0,1},{1,2},{2,3},{3,11},{11,10},{10,9},{9,8},{8,0},{4,5},{5,6},{6... | collective-permute-start | bytes 786440 | tf_op jit(solution)/shard_map/ppermute | solution.py:261
  60.3 21.4 %collective-permute-start.16 = (bf16[128,1024]{1,0:T(8,128)(2,1)}, bf16[128,1024]{1,0:T(8,128)(2,1)}, u32[]{:S(2)}, u32[]{:S(2)}) collective-permute-start(bf16[128,1024]{1,0:T(8,128)(2,1)} %collective-permute-done.8.refs_10_), channel_id=1, source_target_pairs={{0,1},{1,2},{2,3},{3,11},{11,10},{10,9},{9,8},{8,0},{4,5},{5,6},{6... | collective-permute-start | bytes 786440 | tf_op jit(solution)/shard_map/ppermute | solution.py:261
  63.1 22.5 %collective-permute-start.22 = (bf16[128,1024]{1,0:T(8,128)(2,1)}, bf16[128,1024]{1,0:T(8,128)(2,1)}, u32[]{:S(2)}, u32[]{:S(2)}) collective-permute-start(bf16[128,1024]{1,0:T(8,128)(2,1)} %collective-permute-done.14.refs_0_), channel_id=1, source_target_pairs={{0,8},{1,0},{2,1},{3,2},{11,3},{10,11},{9,10},{8,9},{4,12},{5,4},{... | collective-permute-start | bytes 786440 | tf_op jit(solution)/shard_map/ppermute | solution.py:261
  82.9 8.6 %collective-permute-start.24 = (bf16[128,1024]{1,0:T(8,128)(2,1)}, bf16[128,1024]{1,0:T(8,128)(2,1)}, u32[]{:S(2)}, u32[]{:S(2)}) collective-permute-start(bf16[128,1024]{1,0:T(8,128)(2,1)} %collective-permute-done.16.refs_2_), channel_id=1, source_target_pairs={{0,1},{1,2},{2,3},{3,11},{11,10},{10,9},{9,8},{8,0},{4,5},{5,6},{6... | collective-permute-start | bytes 786440 | tf_op jit(solution)/shard_map/ppermute | solution.py:268
  83.2 8.3 %collective-permute-start.25 = (bf16[128,1024]{1,0:T(8,128)(2,1)S(1)}, bf16[128,1024]{1,0:T(8,128)(2,1)}, u32[]{:S(2)}, u32[]{:S(2)}) collective-permute-start(bf16[128,1024]{1,0:T(8,128)(2,1)S(1)} %collective-permute-done.23.refs_9_), channel_id=1, source_target_pairs={{0,8},{1,0},{2,1},{3,2},{11,3},{10,11},{9,10},{8,9},{4,12},{5,4},{... | collective-permute-start | bytes 786440 | tf_op jit(solution)/shard_map/ppermute | solution.py:268
  85.6 10.8 %collective-permute-start.20 = (bf16[128,1024]{1,0:T(8,128)(2,1)}, bf16[128,1024]{1,0:T(8,128)(2,1)}, u32[]{:S(2)}, u32[]{:S(2)}) collective-permute-start(bf16[128,1024]{1,0:T(8,128)(2,1)} %collective-permute-done.16.refs_2_), channel_id=1, source_target_pairs={{0,4},{4,0},{1,5},{5,1},{2,6},{6,2},{3,7},{7,3},{8,12},{12,8},{9,1... | collective-permute-start | bytes 786440 | tf_op jit(solution)/shard_map/ppermute | solution.py:257
  85.6 10.8 %collective-permute-start.21 = (bf16[128,1024]{1,0:T(8,128)(2,1)}, bf16[128,1024]{1,0:T(8,128)(2,1)}, u32[]{:S(2)}, u32[]{:S(2)}) collective-permute-start(bf16[128,1024]{1,0:T(8,128)(2,1)} %collective-permute-done.17.refs_3_), channel_id=1, source_target_pairs={{0,4},{4,0},{1,5},{5,1},{2,6},{6,2},{3,7},{7,3},{8,12},{12,8},{9,1... | collective-permute-start | bytes 786440 | tf_op jit(solution)/shard_map/ppermute | solution.py:257
  86.2 10.3 %collective-permute-start.26 = (bf16[128,1024]{1,0:T(8,128)(2,1)}, bf16[128,1024]{1,0:T(8,128)(2,1)}, u32[]{:S(2)}, u32[]{:S(2)}) collective-permute-start(bf16[128,1024]{1,0:T(8,128)(2,1)} %collective-permute-done.22.refs_8_), channel_id=1, source_target_pairs={{0,4},{4,0},{1,5},{5,1},{2,6},{6,2},{3,7},{7,3},{8,12},{12,8},{9,1... | collective-permute-start | bytes 786440 | tf_op jit(solution)/shard_map/ppermute | solution.py:257
  143.8 15.6 %collective-permute-start.31 = (bf16[2,256,2176]{2,1,0:T(8,128)(2,1)}, bf16[2,256,2176]{2,1,0:T(8,128)(2,1)S(1)}, u32[]{:S(2)}, u32[]{:S(2)}) collective-permute-start(bf16[2,256,2176]{2,1,0:T(8,128)(2,1)} %get-tuple-element.68), channel_id=1, source_target_pairs={{0,4},{4,0},{1,5},{5,1},{2,6},{6,2},{3,7},{7,3},{8,12},{12,8},{9,1... | collective-permute-start | bytes 6684680 | tf_op jit(solution)/shard_map/ppermute | solution.py:458
  150.3 9.1 %collective-permute-start.32 = (bf16[128,1152]{1,0:T(8,128)(2,1)S(1)}, bf16[128,1152]{1,0:T(8,128)(2,1)S(1)}, u32[]{:S(2)}, u32[]{:S(2)}) collective-permute-start(bf16[128,1152]{1,0:T(8,128)(2,1)S(1)} %get-tuple-element.69), channel_id=1, source_target_pairs={{0,1},{1,2},{2,3},{3,11},{11,10},{10,9},{9,8},{8,0},{4,5},{5,6},{6... | collective-permute-start | bytes 884744 | tf_op jit(solution)/shard_map/ppermute | solution.py:517
  150.6 8.1 %collective-permute-start.33 = (bf16[128,1024]{1,0:T(8,128)(2,1)S(1)}, bf16[128,1024]{1,0:T(8,128)(2,1)S(1)}, u32[]{:S(2)}, u32[]{:S(2)}) collective-permute-start(bf16[128,1024]{1,0:T(8,128)(2,1)S(1)} %get-tuple-element.71), channel_id=1, source_target_pairs={{0,8},{1,0},{2,1},{3,2},{11,3},{10,11},{9,10},{8,9},{4,12},{5,4},{... | collective-permute-start | bytes 786440 | tf_op jit(solution)/shard_map/ppermute | solution.py:517
  159.8 8.3 %collective-permute-start.34 = (bf16[128,1152]{1,0:T(8,128)(2,1)S(1)}, bf16[128,1152]{1,0:T(8,128)(2,1)S(1)}, u32[]{:S(2)}, u32[]{:S(2)}) collective-permute-start(bf16[128,1152]{1,0:T(8,128)(2,1)S(1)} %get-tuple-element.76), channel_id=1, source_target_pairs={{0,1},{1,2},{2,3},{3,11},{11,10},{10,9},{9,8},{8,0},{4,5},{5,6},{6... | collective-permute-start | bytes 884744 | tf_op jit(solution)/shard_map/ppermute | solution.py:517
  184.3 8.7 %collective-permute-start.40 = (bf16[128,1152]{1,0:T(8,128)(2,1)S(1)}, bf16[128,1152]{1,0:T(8,128)(2,1)S(1)}, u32[]{:S(2)}, u32[]{:S(2)}) collective-permute-start(bf16[128,1152]{1,0:T(8,128)(2,1)S(1)} %get-tuple-element.97), channel_id=1, source_target_pairs={{0,1},{1,2},{2,3},{3,11},{11,10},{10,9},{9,8},{8,0},{4,5},{5,6},{6... | collective-permute-start | bytes 884744 | tf_op jit(solution)/shard_map/ppermute | solution.py:517
  193.4 10.8 %collective-permute-start.42 = (bf16[128,1152]{1,0:T(8,128)(2,1)S(1)}, bf16[128,1152]{1,0:T(8,128)(2,1)S(1)}, u32[]{:S(2)}, u32[]{:S(2)}) collective-permute-start(bf16[128,1152]{1,0:T(8,128)(2,1)S(1)} %get-tuple-element.104), channel_id=1, source_target_pairs={{0,1},{1,2},{2,3},{3,11},{11,10},{10,9},{9,8},{8,0},{4,5},{5,6},{6... | collective-permute-start | bytes 884744 | tf_op jit(solution)/shard_map/ppermute | solution.py:517
  195.3 8.9 %collective-permute-start.43 = (bf16[128,1024]{1,0:T(8,128)(2,1)S(1)}, bf16[128,1024]{1,0:T(8,128)(2,1)S(1)}, u32[]{:S(2)}, u32[]{:S(2)}) collective-permute-start(bf16[128,1024]{1,0:T(8,128)(2,1)S(1)} %get-tuple-element.105), channel_id=1, source_target_pairs={{0,8},{1,0},{2,1},{3,2},{11,3},{10,11},{9,10},{8,9},{4,12},{5,4},{... | collective-permute-start | bytes 786440 | tf_op jit(solution)/shard_map/ppermute | solution.py:517
  (56 other events, 530.0 us)

commit v5 on v4

--- a/solution.py
+++ b/solution.py
@@ -39,21 +39,16 @@
     )
 
 
-def place_kernel(layout, pick_ref, *refs):
+def place_kernel(pick_ref, *refs):
     *held, out_ref = refs
     width = out_ref.shape[1]
     blocks = out_ref.shape[0] // (2 * ROWS)
     for start in range(0, width, COLS):
         quads = []
         for quad in range(2):
-            values = []
-            for pieces in layout[quad * QUAD : (quad + 1) * QUAD]:
-                at = start
-                for number in pieces:
-                    if at < held[number].shape[1]:
-                        values.append(held[number][:, at : at + COLS])
-                        break
-                    at -= held[number].shape[1]
+            values = [
+                ref[:, start : start + COLS] for ref in held[quad * QUAD : (quad + 1) * QUAD]
+            ]
             rows = jnp.dot(
                 pick_ref[quad], jnp.concatenate(values, axis=0), preferred_element_type=jnp.float32
             )
@@ -157,7 +152,7 @@
 
     @pl.when(step == steps - 1)
     def _():
-        half = part_refs[0].shape[1]
+        half = part_refs[0].shape[0]
         width = rows_ref.shape[-1]
         for quad in range(2 * pairs):
             slots = map_ref[quad : quad + 1, :]
@@ -165,8 +160,8 @@
             spread = jnp.where(slots == token, 1.0, 0.0).astype(jnp.bfloat16)
 
             def put(columns, total):
-                part_refs[quad // 2][quad % 2, :, columns] = total[:half]
-                part_refs[pairs + quad // 2][quad % 2, :, columns] = total[half:]
+                part_refs[quad][:, columns] = total[:half]
+                part_refs[2 * pairs + quad][:, columns] = total[half:]
 
             loss = sum_quad(spread, slot_loss_ref, quad, slice(0, LANES))
             put(slice(width, width + LANES), two_parts(loss))
@@ -232,8 +227,8 @@
 
 
 def arrivals(chips):
-    near = [0]
-    for step in range(1, chips // 2):
+    near = [-1, 1, 0]
+    for step in range(2, chips // 2):
         near += [-step, step]
     return near + [chips // 2]
 
@@ -245,34 +240,42 @@
 class Ring:
     def __init__(self, hidden, order):
         chips = len(order)
-        half = hidden.shape[1] // 2
+        self.order = order
         self.ways = [
             [(order[p], order[(p + way) % chips]) for p in range(chips)] for way in (1, -1)
         ]
-        halves = [hidden[:, :half], hidden[:, half:]]
-        self.moving = [halves, halves]
-        self.got = [self.both(halves)]
-
-    def both(self, pieces):
-        return pieces, [lax.ppermute(piece, "core", [(0, 1), (1, 0)]) for piece in pieces]
-
-    def step(self):
-        self.moving = [
-            [lax.ppermute(piece, CHIPS, way) for piece in pieces]
-            for pieces, way in zip(self.moving, self.ways)
-        ]
-        self.got += [self.both(pieces) for pieces in self.moving]
+        self.moving = [hidden, hidden]
+        self.got = {0: self.both(hidden)}
+
+    def both(self, shard):
+        return shard, lax.ppermute(shard, "core", [(0, 1), (1, 0)])
+
+    def step(self, number, *behind):
+        if behind:
+            self.moving = [after(shard, *behind) for shard in self.moving]
+        self.moving = [lax.ppermute(shard, CHIPS, way) for shard, way in zip(self.moving, self.ways)]
+        self.got[-number], self.got[number] = (self.both(shard) for shard in self.moving)
 
     def last(self, *behind):
-        pieces = [after(self.moving[way][way], *behind) for way in range(2)]
-        self.got += [self.both([lax.ppermute(p, CHIPS, w) for p, w in zip(pieces, self.ways)])]
+        shard = jnp.where(lax.axis_index("core") == 0, *self.moving)
+        down = lax.axis_size("voc")
+
+        def place(chip, core):
+            return (chip // down * 2 + core) * down + chip % down
+
+        links = [
+            (place(source, core), place(target, core))
+            for core in range(2)
+            for source, target in self.ways[core]
+        ]
+        self.got[len(self.order) // 2] = self.both(lax.ppermute(after(shard, *behind), ALL, links))
 
 
 def gather_whole(hidden):
     chips = lax.axis_size(CHIPS)
     own = lax.all_gather(hidden, CHIPS, axis=0)
     other = lax.ppermute(own, "core", [(0, 1), (1, 0)])
-    return [([own[chip]], [other[chip]]) for chip in range(chips)]
+    return [(own[chip], other[chip]) for chip in range(chips)]
 
 
 def on_device(hidden, head, block_ids, live_counts, teacher):
@@ -294,9 +297,7 @@
     order = ring_order(across, down)
     if ring:
         circle = Ring(hidden, order)
-        for _ in range(chips // 2 - 1):
-            circle.step()
-        held = circle.got
+        circle.step(1)
         offsets = np.array(arrivals(chips))
         places = np.argsort(np.array(order))
         spot = jnp.asarray(places, jnp.int32)[lax.axis_index(CHIPS)]
@@ -313,7 +314,8 @@
     live = (jnp.arange(list_width, dtype=jnp.int32)[None, :] < live_counts[:, None]).reshape(entries)
     map_rows = -(-bucket // BLOCK)
     meta_at = -(-bucket // 16) * 16
-    deep = meta_at + -(-(map_rows + 2) // 16) * 16
+    live_rows = tokens // BLOCK
+    deep = meta_at + -(-(map_rows + live_rows) // 16) * 16
     rows = flat_ids // blocks * deep + ranks * blocks + flat_ids % blocks
     slots = jnp.arange(devices * deep, dtype=jnp.int32)
     place = (slots[:, None] == rows[None, :]).astype(jnp.bfloat16)
@@ -326,13 +328,11 @@
     send_map = jnp.sum(jnp.where(tight[:, None] == spots[None, :], named[:, None], 0), axis=0)
     send_map = send_map.reshape(devices, bucket)
     send_map = jnp.pad(send_map, ((0, 0), (0, map_rows * BLOCK - bucket)))
-    live_sum = jnp.sum(live_counts)
     send_meta = jnp.concatenate(
         [
             send_map.reshape(devices, map_rows, BLOCK),
-            jnp.broadcast_to(live_sum // 256, (devices, 1, BLOCK)),
-            jnp.broadcast_to(live_sum % 256, (devices, 1, BLOCK)),
-            jnp.zeros((devices, deep - meta_at - map_rows - 2, BLOCK), jnp.int32),
+            jnp.broadcast_to(live_counts.reshape(1, live_rows, BLOCK), (devices, live_rows, BLOCK)),
+            jnp.zeros((devices, deep - meta_at - map_rows - live_rows, BLOCK), jnp.int32),
         ],
         axis=1,
     ).astype(jnp.bfloat16)
@@ -340,7 +340,9 @@
         send_teacher.reshape(devices, deep, BLOCK), send_meta, (0, meta_at, 0)
     )
     if ring:
-        sent = after(sent, *held[1][0], *held[2][0])
+        sent = after(sent, *circle.moving)
+        for number in range(2, chips // 2 - 1):
+            circle.step(number)
     got = lax.all_to_all(sent, ALL, split_axis=0, concat_axis=0, tiled=True)
 
     lanes = jnp.stack([core, 1 - core])
@@ -349,7 +351,7 @@
     source_of = source_of.reshape(devices)
     got = got.at[source_of].get(mode="promise_in_bounds")
     meta = got[:, meta_at:].astype(jnp.int32)
-    live_total = jnp.sum(meta[:, map_rows, 0] * 256 + meta[:, map_rows + 1, 0])
+    live_total = jnp.sum(meta[:, map_rows : map_rows + live_rows])
     scale = jnp.float32(tokens * devices) / live_total.astype(jnp.float32)
     slot_map = meta[:, :map_rows].reshape(devices, map_rows * BLOCK)[:, :bucket]
     quads = devices // QUAD
@@ -359,6 +361,9 @@
     slot_map = slot_map.swapaxes(1, 2).reshape(quads, blocks * ROWS)
     token_of = jnp.arange(QUAD * tokens, dtype=jnp.int32)
     pick = (slot_map[:, :, None] == token_of[None, None, :]).astype(jnp.bfloat16)
+    if ring:
+        circle.step(chips // 2 - 1, pick)
+        held = [circle.got[int(offset)] for offset in offsets[:-1]]
     got_teacher = got[:, :bucket].reshape(devices, C, blocks, BLOCK)
     joint = 2 if turn % 2 == 0 else 1
     got_teacher = got_teacher.reshape(pairs, 2 * ROWS, blocks // joint, joint, BLOCK)
@@ -371,15 +376,14 @@
     for pair in range(pairs):
         if ring and pair == pairs - 1:
             circle.last(*placed)
-        layout, operands = [], []
+            held += [circle.got[int(offset)] for offset in offsets[len(held) :]]
+        operands = []
         for quad in range(2):
             two = held[pair * 4 + quad * 2 : pair * 4 + quad * 2 + 2]
-            for pieces in [chip[lane] for lane in range(2) for chip in two]:
-                layout.append(list(range(len(operands), len(operands) + len(pieces))))
-                operands += pieces
+            operands += [chip[lane] for lane in range(2) for chip in two]
         placed.append(
             call(
-                functools.partial(place_kernel, layout),
+                place_kernel,
                 f"place_{pair}",
                 (blocks // part,),
                 [pl.BlockSpec((2, part * ROWS, QUAD * tokens), lambda s, p=pair: (p, s, 0))]
@@ -388,7 +392,7 @@
                 jax.ShapeDtypeStruct((x_rows, width), jnp.bfloat16),
                 2 * x_rows * QUAD * tokens * width,
                 2 * x_rows * width * 2,
-                28,
+                52,
             )(pick, *operands)
         )
 
@@ -398,9 +402,9 @@
     x_spec = pl.BlockSpec((turn * 2 * ROWS, width), lambda s: (s, 0))
     flops = 2 * blocks * per_block * BLOCK * width
     if ring:
-        part = (2, 2 * tokens, width + LANES)
-        out_specs = [pl.BlockSpec(part, lambda s: (0, 0, 0), pipeline_mode=once)] * (2 * pairs)
-        out_shapes = [jax.ShapeDtypeStruct(part, jnp.bfloat16)] * (2 * pairs)
+        part = (2 * tokens, width + LANES)
+        out_specs = [pl.BlockSpec(part, lambda s: (0, 0), pipeline_mode=once)] * (2 * quads)
+        out_shapes = [jax.ShapeDtypeStruct(part, jnp.bfloat16)] * (2 * quads)
         scratch = [
             pltpu.VMEM((blocks, per_block, width), jnp.float32),
             pltpu.VMEM((blocks, per_block, BLOCK), jnp.float32),
@@ -450,13 +454,13 @@
                 jnp.einsum("qst,qsd->qtd", pick, value, preferred_element_type=jnp.float32)
             )
         loss = totals[1]
-        total = totals[0].astype(jnp.bfloat16).reshape(pairs, 2, 2, 2 * tokens, width)
-        parts = [total[pair, :, lane] for lane in range(2) for pair in range(pairs)]
+        total = totals[0].astype(jnp.bfloat16).reshape(quads, 2, 2 * tokens, width)
+        parts = [total[quad, lane] for lane in range(2) for quad in range(quads)]
     own_parts, other_parts = [], []
-    for pair in range(pairs):
-        own_parts.append(parts[pair].reshape(4, tokens, -1))
-        swapped = lax.ppermute(parts[pairs + pair], "core", [(0, 1), (1, 0)])
-        other_parts.append(swapped.reshape(4, tokens, -1))
+    for quad in range(quads):
+        own_parts.append(parts[quad].reshape(2, tokens, -1))
+        swapped = lax.ppermute(parts[quads + quad], "core", [(0, 1), (1, 0)])
+        other_parts.append(swapped.reshape(2, tokens, -1))
 
     splits = 2 if turn % 4 == 0 else 1
     lots = min(steps * splits, chips - 1)
@@ -507,10 +511,10 @@
             places = [(ends[0], half, 0), (ends[1], half, 1), (ends[0], LANES, width // LANES)]
             for source in (own_parts, other_parts):
                 for at, columns, where in places:
-                    operands.append(source[at // 4])
+                    operands.append(source[at // 2])
                     specs.append(
                         pl.BlockSpec(
-                            (1, tokens, columns), lambda s, a=at % 4, w=where: (a, 0, w)
+                            (1, tokens, columns), lambda s, a=at % 2, w=where: (a, 0, w)
                         )
                     )
             for way in range(len(sums)):

time: 215 us -> 199 us (0.926)
  local copies, waits for them, and re-layouts: 32 us -> 8.57 us
  waiting for transfers between devices: 43.6 us -> 58 us
  starting transfers between devices: 44.3 us -> 35 us
  Pallas kernels: 78.2 us -> 83.2 us
  between operations: 4.38 us -> 1.67 us
    ppermute x32 -> x19, waiting for transfers between devices: 11.7 us -> 39.6 us  [the longest x6 31.1 us: step(): lax.ppermute(shard, CHIPS, way)]
    unnamed x84 -> x36, local copies, waits for them, and re-layouts: 24.4 us -> 2.11 us
    all_to_all x1, waiting for transfers between devices: 14.7 us -> 0.01 us  [on_device(): got = lax.all_to_all(sent, ALL, split_axis=0, concat_axis=0, tiled=True)]
    ppermute x32 -> x19, starting transfers between devices: 23.5 us -> 15.5 us  [the longest x6 10.6 us: step(): lax.ppermute(shard, CHIPS, way)]
    pallas_call x2, Pallas kernels: 10.9 us -> 14.9 us  [on_device(): call(place_kernel, f'place_{pair}', (blocks // part,), [pl.BlockSpec((2,...]
  transfers between devices with their start and end apart: 47 -> 34, of which waited for: 16 -> 14; matrix products, arithmetic and copies ran while one was open for 8% -> 9% of each run, Pallas kernels for 15% -> 18%
where the time goes in v5:
time: 199 us; the launch traced here: 198 us
  Pallas kernels  83.2 us (42%)
  waiting for transfers between devices  58 us (29%)
  starting transfers between devices  35 us (18%)
  other arithmetic  8.6 us (4%)
  local copies, waits for them, and re-layouts  8.57 us (4%)
  matrix products  2.92 us (1%)
    pallas_call x1, Pallas kernels, on_device(): call(functools.partial(main_kernel, turn, steps, pairs, ring), 'logits_an...  37.1 us
    ppermute x6, waiting for transfers between devices, step(): lax.ppermute(shard, CHIPS, way)  31.1 us
    pallas_call x7, Pallas kernels, fill(): call(functools.partial(head_kernel, turn, splits, shift, pairs), f'head_g...  27.6 us
    ppermute x14, waiting for transfers between devices, on_device(): moved = lax.ppermute(sums[way], CHIPS, circle.ways[way])  18.4 us
    pallas_call x2, Pallas kernels, on_device(): call(place_kernel, f'place_{pair}', (blocks // part,), [pl.BlockSpec((2,...  14.9 us
    ppermute x14, starting transfers between devices, on_device(): moved = lax.ppermute(sums[way], CHIPS, circle.ways[way])  14.6 us
    ppermute x6, starting transfers between devices, step(): lax.ppermute(shard, CHIPS, way)  10.6 us
    ppermute x1, waiting for transfers between devices, last(): lax.ppermute(after(shard, *behind), ALL, links)  6.49 us
  transfers between devices with their start and end apart: 34, of which 14 were waited for; matrix products, arithmetic and copies ran while one was open for 9% of the time, Pallas kernels for 18%

profile of v5, /device:TPU:0, one launch (start us, length us, event | category | flops | bytes accessed | tf_op | source)
XLA Modules:
  0.0 198.0 jit_solution(14166787836839143238)
XLA Ops:
  0.6 3.0 %collective-permute-start.1 = (bf16[128,2048]{1,0:T(8,128)(2,1)}, bf16[128,2048]{1,0:T(8,128)(2,1)S(1)}, u32[]{:S(2)}, u32[]{:S(2)}) collective-permute-start(bf16[128,2048]{1,0:T(8,128)(2,1)} %refs_4_.1), channel_id=1, source_target_pairs={{0,8},{1,0},{2,1},{3,2},{11,3},{10,11},{9,10},{8,9},{4,12},{5,4},{... | collective-permute-start | bytes 1572872 | tf_op jit(solution)/shard_map/ppermute | solution.py:256
  6.1 1.6 select_reduce_fusion
  8.6 2.9 %fusion.4 = bf16[2816,128]{1,0:T(8,128)(2,1)} fusion(s32[1024]{0:T(1024)S(1)} %get-tuple-element.132, bf16[128,8,128]{2,1,0:T(8,128)(2,1)S(1)} %copy-done), kind=kOutput, calls=%fused_computation.12 | convolution fusion | flops 741441536 | bytes 987136 | tf_op jit(solution)/shard_map/dot_general | solution.py:322
  12.2 3.6 %collective-permute-done.1.refs_1_ = bf16[128,2048]{1,0:T(8,128)(2,1)S(1)} collective-permute-done((bf16[128,2048]{1,0:T(8,128)(2,1)}, bf16[128,2048]{1,0:T(8,128)(2,1)S(1)}, u32[]{:S(2)}, u32[]{:S(2)}) %collective-permute-start.1) | collective-permute-done | bytes 524320 | tf_op jit(solution)/shard_map/ppermute | solution.py:256
  17.2 5.0 %all-to-all-start = ((bf16[16,176,128]{2,1,0:T(8,128)(2,1)}), bf16[16,176,128]{2,1,0:T(8,128)(2,1)S(1)}, u32[]{:S(2)}, u32[]{:S(2)}) async-start(bf16[16,176,128]{2,1,0:T(8,128)(2,1)} %maximum_dynamic-update-slice_fusion), calls=%async_computation | async-start | bytes 1441792 | tf_op jit(solution)/shard_map/all_to_all | solution.py:346
  24.7 1.7 collective-permute-start.4
  27.6 18.6 %collective-permute-done.4.refs_5_ = bf16[128,2048]{1,0:T(8,128)(2,1)} collective-permute-done((bf16[128,2048]{1,0:T(8,128)(2,1)S(1)}, bf16[128,2048]{1,0:T(8,128)(2,1)}, u32[]{:S(2)}, u32[]{:S(2)}) %collective-permute-start.4) | collective-permute-done | bytes 524320 | tf_op jit(solution)/shard_map/ppermute | solution.py:256
  46.1 1.5 gather_fusion.1
  48.9 1.9 fusion.2.pick_ref
  50.8 5.3 %collective-permute-start.8 = (bf16[128,2048]{1,0:T(8,128)(2,1)}, bf16[128,2048]{1,0:T(8,128)(2,1)S(1)}, u32[]{:S(2)}, u32[]{:S(2)}) collective-permute-start(bf16[128,2048]{1,0:T(8,128)(2,1)} %collective-permute-done.4.refs_5_), channel_id=1, source_target_pairs={{0,1},{1,2},{2,3},{3,11},{11,10},{10,9},{9,8},{8,0},{4,5},{5,6},{6... | collective-permute-start | bytes 1572872 | tf_op jit(solution)/shard_map/ppermute | solution.py:256
  56.2 7.4 %place_0.1.refs_0_ = bf16[1280,2048]{1,0:T(8,128)(2,1)} custom-call(bf16[4,640,512]{2,1,0:T(8,128)(2,1)} %fusion.2.pick_ref, bf16[128,2048]{1,0:T(8,128)(2,1)S(1)} %collective-permute-done.refs_0_, bf16[128,2048]{1,0:T(8,128)(2,1)S(1)} %collective-permute-done.1.refs_1_, bf16[128,2048]{1,0:T(8,128)(2,1)S(1)} %collective-permute-done.2.refs_2_, ...), custom_call_target="tpu_custom_call" | custom-call | flops 2684354560 | bytes 10485760 | tf_op jit(solution)/shard_map/place_0/pallas_call | solution.py:385
  63.6 4.6 %collective-permute-done.8.refs_1_ = bf16[128,2048]{1,0:T(8,128)(2,1)S(1)} collective-permute-done((bf16[128,2048]{1,0:T(8,128)(2,1)}, bf16[128,2048]{1,0:T(8,128)(2,1)S(1)}, u32[]{:S(2)}, u32[]{:S(2)}) %collective-permute-start.8) | collective-permute-done | bytes 524320 | tf_op jit(solution)/shard_map/ppermute | solution.py:256
  68.3 2.8 %collective-permute-done.11.refs_4_ = bf16[128,2048]{1,0:T(8,128)(2,1)} collective-permute-done((bf16[128,2048]{1,0:T(8,128)(2,1)S(1)}, bf16[128,2048]{1,0:T(8,128)(2,1)}, u32[]{:S(2)}, u32[]{:S(2)}) %collective-permute-start.11) | collective-permute-done | bytes 524320 | tf_op jit(solution)/shard_map/ppermute | solution.py:256
  71.2 2.0 collective-permute-start.12
  74.1 6.5 %collective-permute-done.12.refs_5_ = bf16[128,2048]{1,0:T(8,128)(2,1)S(1)} collective-permute-done((bf16[128,2048]{1,0:T(8,128)(2,1)S(1)}, bf16[128,2048]{1,0:T(8,128)(2,1)S(1)}, u32[]{:S(2)}, u32[]{:S(2)}) %collective-permute-start.12) | collective-permute-done | bytes 524320 | tf_op jit(solution)/shard_map/ppermute | solution.py:271
  84.2 7.4 %place_1.1.refs_1_ = bf16[1280,2048]{1,0:T(8,128)(2,1)} custom-call(bf16[4,640,512]{2,1,0:T(8,128)(2,1)} %fusion.2.pick_ref, bf16[128,2048]{1,0:T(8,128)(2,1)S(1)} %collective-permute-done.7.refs_0_, bf16[128,2048]{1,0:T(8,128)(2,1)S(1)} %collective-permute-done.8.refs_1_, bf16[128,2048]{1,0:T(8,128)(2,1)S(1)} %collective-permute-done.9.refs_2_, ...), custom_call_target="tpu_custom_call" | custom-call | flops 2684354560 | bytes 10485760 | tf_op jit(solution)/shard_map/place_1/pallas_call | solution.py:385
  91.6 37.1 %logits_and_back.1 = (bf16[128,2560]{1,0:T(8,128)(2,1)S(1)}, bf16[256,2176]{1,0:T(8,128)(2,1)}, bf16[256,2176]{1,0:T(8,128)(2,1)}, bf16[256,2176]{1,0:T(8,128)(2...) custom-call(f32[1]{0:T(128)} %bitcast.6.scale_ref, ...), custom_call_target="tpu_custom_call" | custom-call | flops 21474836480 | bytes 52428800 | tf_op jit(solution)/shard_map/logits_and_back/pallas_call | solution.py:422
  129.7 2.0 %collective-permute-done.16 = bf16[256,2176]{1,0:T(8,128)(2,1)S(1)} collective-permute-done((bf16[256,2176]{1,0:T(8,128)(2,1)}, bf16[256,2176]{1,0:T(8,128)(2,1)S(1)}, u32[]{:S(2)}, u32[]{:S(2)}) %collective-permute-start.16) | collective-permute-done | bytes 1114144 | tf_op jit(solution)/shard_map/ppermute | solution.py:462
  133.3 1.8 collective-permute-start.19
  135.4 2.9 %head_grad_0.1 = (bf16[10240,2048]{1,0:T(8,128)(2,1)}, f32[8,128]{1,0:T(8,128)}) custom-call(bf16[128,2560]{1,0:T(8,128)(2,1)S(1)} %get-tuple-element.123.grad_ref, bf16[1280,2048]{1,0:T(8,128)(2,1)S(1)} %bitcast.30, bf16[1280,2048]{1,0:T(8,128)(2,1)S(1)} %bitcast.32), custom_call_target="tpu_custom_call" | custom-call | flops 1533916928 | bytes 7489828 | tf_op jit(solution)/shard_map/head_grad_0/pallas_call | solution.py:483
  138.3 5.1 %collective-permute-done.20.refs_7_ = bf16[128,1024]{1,0:T(8,128)(2,1)S(1)} collective-permute-done((bf16[128,1024]{1,0:T(8,128)(2,1)S(1)}, bf16[128,1024]{1,0:T(8,128)(2,1)S(1)}, u32[]{:S(2)}, u32[]{:S(2)}) %collective-permute-start.20) | collective-permute-done | bytes 262176 | tf_op jit(solution)/shard_map/ppermute | solution.py:521
  145.8 4.1 %head_grad_1.1 = (bf16[10240,2048]{1,0:T(8,128)(2,1)}, f32[8,128]{1,0:T(8,128)}) custom-call(bf16[128,2560]{1,0:T(8,128)(2,1)S(1)} %get-tuple-element.123.grad_ref, bf16[1280,2048]{1,0:T(8,128)(2,1)S(1)} %bitcast.30, bf16[1280,2048]{1,0:T(8,128)(2,1)S(1)} %bitcast.32, bf16[10240,2048]{1,0:T(8,128)(2,1)} %get-tuple-element.89.refs_2_), custom_call_target="tpu_custom_call", output_to_operand_aliasing={{0}: (3, {})} | custom-call | flops 1533916928 | bytes 7489828 | tf_op jit(solution)/shard_map/head_grad_1/pallas_call | solution.py:483
  150.0 2.3 %collective-permute-done.22.refs_7_ = bf16[128,1024]{1,0:T(8,128)(2,1)S(1)} collective-permute-done((bf16[128,1024]{1,0:T(8,128)(2,1)S(1)}, bf16[128,1024]{1,0:T(8,128)(2,1)S(1)}, u32[]{:S(2)}, u32[]{:S(2)}) %collective-permute-start.22) | collective-permute-done | bytes 262176 | tf_op jit(solution)/shard_map/ppermute | solution.py:521
  154.8 4.1 %head_grad_2.1 = (bf16[10240,2048]{1,0:T(8,128)(2,1)}, f32[8,128]{1,0:T(8,128)}) custom-call(bf16[128,2560]{1,0:T(8,128)(2,1)S(1)} %get-tuple-element.123.grad_ref, bf16[1280,2048]{1,0:T(8,128)(2,1)S(1)} %bitcast.30, bf16[1280,2048]{1,0:T(8,128)(2,1)S(1)} %bitcast.32, bf16[10240,2048]{1,0:T(8,128)(2,1)} %get-tuple-element.96.refs_2_), custom_call_target="tpu_custom_call", output_to_operand_aliasing={{0}: (3, {})} | custom-call | flops 1533916928 | bytes 7489828 | tf_op jit(solution)/shard_map/head_grad_2/pallas_call | solution.py:483
  158.8 1.4 collective-permute-done.24.refs_7_
  162.7 4.1 %head_grad_3.1 = (bf16[10240,2048]{1,0:T(8,128)(2,1)}, f32[8,128]{1,0:T(8,128)}) custom-call(bf16[128,2560]{1,0:T(8,128)(2,1)S(1)} %get-tuple-element.123.grad_ref, bf16[1280,2048]{1,0:T(8,128)(2,1)S(1)} %bitcast.30, bf16[1280,2048]{1,0:T(8,128)(2,1)S(1)} %bitcast.32, bf16[10240,2048]{1,0:T(8,128)(2,1)} %get-tuple-element.103.refs_2_), custom_call_target="tpu_custom_call", output_to_operand_aliasing={{0}: (3, {})} | custom-call | flops 1533916928 | bytes 7489828 | tf_op jit(solution)/shard_map/head_grad_3/pallas_call | solution.py:483
  168.4 1.8 collective-permute-start.27
  170.5 4.1 %head_grad_4.1 = (bf16[10240,2048]{1,0:T(8,128)(2,1)}, f32[8,128]{1,0:T(8,128)}) custom-call(bf16[128,2560]{1,0:T(8,128)(2,1)S(1)} %get-tuple-element.123.grad_ref, bf16[1280,2048]{1,0:T(8,128)(2,1)S(1)} %bitcast.30, bf16[1280,2048]{1,0:T(8,128)(2,1)S(1)} %bitcast.32, bf16[10240,2048]{1,0:T(8,128)(2,1)} %get-tuple-element.110.refs_2_), custom_call_target="tpu_custom_call", output_to_operand_aliasing={{0}: (3, {})} | custom-call | flops 1533916928 | bytes 7489828 | tf_op jit(solution)/shard_map/head_grad_4/pallas_call | solution.py:483
  174.6 3.2 %collective-permute-done.28.refs_7_ = bf16[128,1024]{1,0:T(8,128)(2,1)S(1)} collective-permute-done((bf16[128,1024]{1,0:T(8,128)(2,1)S(1)}, bf16[128,1024]{1,0:T(8,128)(2,1)S(1)}, u32[]{:S(2)}, u32[]{:S(2)}) %collective-permute-start.28) | collective-permute-done | bytes 262176 | tf_op jit(solution)/shard_map/ppermute | solution.py:521
  180.3 4.1 %head_grad_5.1 = (bf16[10240,2048]{1,0:T(8,128)(2,1)}, f32[8,128]{1,0:T(8,128)}) custom-call(bf16[128,2560]{1,0:T(8,128)(2,1)S(1)} %get-tuple-element.123.grad_ref, bf16[1280,2048]{1,0:T(8,128)(2,1)S(1)} %bitcast.30, bf16[1280,2048]{1,0:T(8,128)(2,1)S(1)} %bitcast.32, bf16[10240,2048]{1,0:T(8,128)(2,1)} %get-tuple-element.117.refs_2_), custom_call_target="tpu_custom_call", output_to_operand_aliasing={{0}: (3, {})} | custom-call | flops 1533916928 | bytes 7489828 | tf_op jit(solution)/shard_map/head_grad_5/pallas_call | solution.py:483
  184.4 3.9 %collective-permute-done.30.refs_7_ = bf16[128,1024]{1,0:T(8,128)(2,1)S(1)} collective-permute-done((bf16[128,1024]{1,0:T(8,128)(2,1)S(1)}, bf16[128,1024]{1,0:T(8,128)(2,1)S(1)}, u32[]{:S(2)}, u32[]{:S(2)}) %collective-permute-start.30) | collective-permute-done | bytes 262176 | tf_op jit(solution)/shard_map/ppermute | solution.py:521
  190.8 4.2 %head_grad_6.1 = (bf16[10240,2048]{1,0:T(8,128)(2,1)}, f32[8,128]{1,0:T(8,128)}) custom-call(bf16[128,2560]{1,0:T(8,128)(2,1)S(1)} %get-tuple-element.123.grad_ref, bf16[1280,2048]{1,0:T(8,128)(2,1)S(1)} %bitcast.30, bf16[1280,2048]{1,0:T(8,128)(2,1)S(1)} %bitcast.34, bf16[10240,2048]{1,0:T(8,128)(2,1)} %get-tuple-element.124.refs_2_), custom_call_target="tpu_custom_call", output_to_operand_aliasing={{0}: (3, {})} | custom-call | flops 1533916928 | bytes 7489828 | tf_op jit(solution)/shard_map/head_grad_6/pallas_call | solution.py:483
  (134 shorter events, 34.1 us)
Async XLA Ops:
  0.6 15.2 %collective-permute-start.1 = (bf16[128,2048]{1,0:T(8,128)(2,1)}, bf16[128,2048]{1,0:T(8,128)(2,1)S(1)}, u32[]{:S(2)}, u32[]{:S(2)}) collective-permute-start(bf16[128,2048]{1,0:T(8,128)(2,1)} %refs_4_.1), channel_id=1, source_target_pairs={{0,8},{1,0},{2,1},{3,2},{11,3},{10,11},{9,10},{8,9},{4,12},{5,4},{... | collective-permute-start | bytes 1572872 | tf_op jit(solution)/shard_map/ppermute | solution.py:256
  3.6 13.6 %collective-permute-start = (bf16[128,2048]{1,0:T(8,128)(2,1)}, bf16[128,2048]{1,0:T(8,128)(2,1)S(1)}, u32[]{:S(2)}, u32[]{:S(2)}) collective-permute-start(bf16[128,2048]{1,0:T(8,128)(2,1)} %refs_4_.1), channel_id=1, source_target_pairs={{0,1},{1,2},{2,3},{3,11},{11,10},{10,9},{9,8},{8,0},{4,5},{5,6},{6... | collective-permute-start | bytes 1572872 | tf_op jit(solution)/shard_map/ppermute | solution.py:256
  17.2 28.9 %all-to-all-start = ((bf16[16,176,128]{2,1,0:T(8,128)(2,1)}), bf16[16,176,128]{2,1,0:T(8,128)(2,1)S(1)}, u32[]{:S(2)}, u32[]{:S(2)}) async-start(bf16[16,176,128]{2,1,0:T(8,128)(2,1)} %maximum_dynamic-update-slice_fusion), calls=%async_computation | async-start | bytes 1441792 | tf_op jit(solution)/shard_map/all_to_all | solution.py:346
  22.2 33.9 %collective-permute-start.5 = (bf16[128,2048]{1,0:T(8,128)(2,1)}, bf16[128,2048]{1,0:T(8,128)(2,1)}, u32[]{:S(2)}, u32[]{:S(2)}) collective-permute-start(bf16[128,2048]{1,0:T(8,128)(2,1)} %refs_4_.1), channel_id=1, source_target_pairs={{0,4},{4,0},{1,5},{5,1},{2,6},{6,2},{3,7},{7,3},{8,12},{12,8},{9,1... | collective-permute-start | bytes 1572872 | tf_op jit(solution)/shard_map/ppermute | solution.py:251
  24.7 21.4 %collective-permute-start.4 = (bf16[128,2048]{1,0:T(8,128)(2,1)S(1)}, bf16[128,2048]{1,0:T(8,128)(2,1)}, u32[]{:S(2)}, u32[]{:S(2)}) collective-permute-start(bf16[128,2048]{1,0:T(8,128)(2,1)S(1)} %collective-permute-done.refs_0_), channel_id=1, source_target_pairs={{0,1},{1,2},{2,3},{3,11},{11,10},{10,9},{9,8},{8,0},{4,5},{5,6},{6... | collective-permute-start | bytes 1572872 | tf_op jit(solution)/shard_map/ppermute | solution.py:256
  26.6 24.2 %collective-permute-start.7 = (bf16[128,2048]{1,0:T(8,128)(2,1)S(1)}, bf16[128,2048]{1,0:T(8,128)(2,1)S(1)}, u32[]{:S(2)}, u32[]{:S(2)}) collective-permute-start(bf16[128,2048]{1,0:T(8,128)(2,1)S(1)} %collective-permute-done.1.refs_1_), channel_id=1, source_target_pairs={{0,8},{1,0},{2,1},{3,2},{11,3},{10,11},{9,10},{8,9},{4,12},{5,4},{... | collective-permute-start | bytes 1572872 | tf_op jit(solution)/shard_map/ppermute | solution.py:256
  27.0 29.1 %collective-permute-start.3 = (bf16[128,2048]{1,0:T(8,128)(2,1)S(1)}, bf16[128,2048]{1,0:T(8,128)(2,1)}, u32[]{:S(2)}, u32[]{:S(2)}) collective-permute-start(bf16[128,2048]{1,0:T(8,128)(2,1)S(1)} %collective-permute-done.1.refs_1_), channel_id=1, source_target_pairs={{0,4},{4,0},{1,5},{5,1},{2,6},{6,2},{3,7},{7,3},{8,12},{12,8},{9,1... | collective-permute-start | bytes 1572872 | tf_op jit(solution)/shard_map/ppermute | solution.py:251
  27.0 29.1 %collective-permute-start.2 = (bf16[128,2048]{1,0:T(8,128)(2,1)S(1)}, bf16[128,2048]{1,0:T(8,128)(2,1)S(1)}, u32[]{:S(2)}, u32[]{:S(2)}) collective-permute-start(bf16[128,2048]{1,0:T(8,128)(2,1)S(1)} %collective-permute-done.refs_0_), channel_id=1, source_target_pairs={{0,4},{4,0},{1,5},{5,1},{2,6},{6,2},{3,7},{7,3},{8,12},{12,8},{9,1... | collective-permute-start | bytes 1572872 | tf_op jit(solution)/shard_map/ppermute | solution.py:251
  46.1 10.0 %collective-permute-start.6 = (bf16[128,2048]{1,0:T(8,128)(2,1)}, bf16[128,2048]{1,0:T(8,128)(2,1)}, u32[]{:S(2)}, u32[]{:S(2)}) collective-permute-start(bf16[128,2048]{1,0:T(8,128)(2,1)} %collective-permute-done.4.refs_5_), channel_id=1, source_target_pairs={{0,4},{4,0},{1,5},{5,1},{2,6},{6,2},{3,7},{7,3},{8,12},{12,8},{9,1... | collective-permute-start | bytes 1572872 | tf_op jit(solution)/shard_map/ppermute | solution.py:251
  50.8 17.5 %collective-permute-start.8 = (bf16[128,2048]{1,0:T(8,128)(2,1)}, bf16[128,2048]{1,0:T(8,128)(2,1)S(1)}, u32[]{:S(2)}, u32[]{:S(2)}) collective-permute-start(bf16[128,2048]{1,0:T(8,128)(2,1)} %collective-permute-done.4.refs_5_), channel_id=1, source_target_pairs={{0,1},{1,2},{2,3},{3,11},{11,10},{10,9},{9,8},{8,0},{4,5},{5,6},{6... | collective-permute-start | bytes 1572872 | tf_op jit(solution)/shard_map/ppermute | solution.py:256
  56.2 14.9 %collective-permute-start.11 = (bf16[128,2048]{1,0:T(8,128)(2,1)S(1)}, bf16[128,2048]{1,0:T(8,128)(2,1)}, u32[]{:S(2)}, u32[]{:S(2)}) collective-permute-start(bf16[128,2048]{1,0:T(8,128)(2,1)S(1)} %collective-permute-done.7.refs_0_), channel_id=1, source_target_pairs={{0,8},{1,0},{2,1},{3,2},{11,3},{10,11},{9,10},{8,9},{4,12},{5,4},{... | collective-permute-start | bytes 1572872 | tf_op jit(solution)/shard_map/ppermute | solution.py:256
  71.2 9.4 %collective-permute-start.12 = (bf16[128,2048]{1,0:T(8,128)(2,1)S(1)}, bf16[128,2048]{1,0:T(8,128)(2,1)S(1)}, u32[]{:S(2)}, u32[]{:S(2)}) collective-permute-start(bf16[128,2048]{1,0:T(8,128)(2,1)S(1)} %broadcast_select_fusion), channel_id=1, source_target_pairs={{0,1},{1,2},{2,3},{3,11},{11,10},{10,9},{9,8},{8,0},{4,12},{5,4},{... | collective-permute-start | bytes 1572872 | tf_op jit(solution)/shard_map/ppermute | solution.py:271
  73.1 11.0 %collective-permute-start.9 = (bf16[128,2048]{1,0:T(8,128)(2,1)S(1)}, bf16[128,2048]{1,0:T(8,128)(2,1)S(1)}, u32[]{:S(2)}, u32[]{:S(2)}) collective-permute-start(bf16[128,2048]{1,0:T(8,128)(2,1)S(1)} %collective-permute-done.7.refs_0_), channel_id=1, source_target_pairs={{0,4},{4,0},{1,5},{5,1},{2,6},{6,2},{3,7},{7,3},{8,12},{12,8},{9,1... | collective-permute-start | bytes 1572872 | tf_op jit(solution)/shard_map/ppermute | solution.py:251
  73.6 10.6 %collective-permute-start.10 = (bf16[128,2048]{1,0:T(8,128)(2,1)S(1)}, bf16[128,2048]{1,0:T(8,128)(2,1)}, u32[]{:S(2)}, u32[]{:S(2)}) collective-permute-start(bf16[128,2048]{1,0:T(8,128)(2,1)S(1)} %collective-permute-done.8.refs_1_), channel_id=1, source_target_pairs={{0,4},{4,0},{1,5},{5,1},{2,6},{6,2},{3,7},{7,3},{8,12},{12,8},{9,1... | collective-permute-start | bytes 1572872 | tf_op jit(solution)/shard_map/ppermute | solution.py:251
  73.6 10.5 %collective-permute-start.13 = (bf16[128,2048]{1,0:T(8,128)(2,1)}, bf16[128,2048]{1,0:T(8,128)(2,1)}, u32[]{:S(2)}, u32[]{:S(2)}) collective-permute-start(bf16[128,2048]{1,0:T(8,128)(2,1)} %collective-permute-done.11.refs_4_), channel_id=1, source_target_pairs={{0,4},{4,0},{1,5},{5,1},{2,6},{6,2},{3,7},{7,3},{8,12},{12,8},{9,1... | collective-permute-start | bytes 1572872 | tf_op jit(solution)/shard_map/ppermute | solution.py:251
  129.2 14.2 %collective-permute-start.15 = (bf16[256,2176]{1,0:T(8,128)(2,1)}, bf16[256,2176]{1,0:T(8,128)(2,1)S(1)}, u32[]{:S(2)}, u32[]{:S(2)}) collective-permute-start(bf16[256,2176]{1,0:T(8,128)(2,1)} %get-tuple-element.72), channel_id=1, source_target_pairs={{0,4},{4,0},{1,5},{5,1},{2,6},{6,2},{3,7},{7,3},{8,12},{12,8},{9,1... | collective-permute-start | bytes 3342344 | tf_op jit(solution)/shard_map/ppermute | solution.py:462
  129.2 14.1 %collective-permute-start.17 = (bf16[256,2176]{1,0:T(8,128)(2,1)}, bf16[256,2176]{1,0:T(8,128)(2,1)S(1)}, u32[]{:S(2)}, u32[]{:S(2)}) collective-permute-start(bf16[256,2176]{1,0:T(8,128)(2,1)} %get-tuple-element.76), channel_id=1, source_target_pairs={{0,4},{4,0},{1,5},{5,1},{2,6},{6,2},{3,7},{7,3},{8,12},{12,8},{9,1... | collective-permute-start | bytes 3342344 | tf_op jit(solution)/shard_map/ppermute | solution.py:462
  129.7 22.6 %collective-permute-start.18 = (bf16[256,2176]{1,0:T(8,128)(2,1)}, bf16[256,2176]{1,0:T(8,128)(2,1)S(1)}, u32[]{:S(2)}, u32[]{:S(2)}) collective-permute-start(bf16[256,2176]{1,0:T(8,128)(2,1)} %get-tuple-element.78), channel_id=1, source_target_pairs={{0,4},{4,0},{1,5},{5,1},{2,6},{6,2},{3,7},{7,3},{8,12},{12,8},{9,1... | collective-permute-start | bytes 3342344 | tf_op jit(solution)/shard_map/ppermute | solution.py:462
  133.3 10.1 %collective-permute-start.19 = (bf16[128,1152]{1,0:T(8,128)(2,1)S(1)}, bf16[128,1152]{1,0:T(8,128)(2,1)S(1)}, u32[]{:S(2)}, u32[]{:S(2)}) collective-permute-start(bf16[128,1152]{1,0:T(8,128)(2,1)S(1)} %get-tuple-element.79), channel_id=1, source_target_pairs={{0,1},{1,2},{2,3},{3,11},{11,10},{10,9},{9,8},{8,0},{4,5},{5,6},{6... | collective-permute-start | bytes 884744 | tf_op jit(solution)/shard_map/ppermute | solution.py:521
  135.1 8.3 %collective-permute-start.20 = (bf16[128,1024]{1,0:T(8,128)(2,1)S(1)}, bf16[128,1024]{1,0:T(8,128)(2,1)S(1)}, u32[]{:S(2)}, u32[]{:S(2)}) collective-permute-start(bf16[128,1024]{1,0:T(8,128)(2,1)S(1)} %get-tuple-element.81), channel_id=1, source_target_pairs={{0,8},{1,0},{2,1},{3,2},{11,3},{10,11},{9,10},{8,9},{4,12},{5,4},{... | collective-permute-start | bytes 786440 | tf_op jit(solution)/shard_map/ppermute | solution.py:521
  143.8 8.5 %collective-permute-start.21 = (bf16[128,1152]{1,0:T(8,128)(2,1)S(1)}, bf16[128,1152]{1,0:T(8,128)(2,1)S(1)}, u32[]{:S(2)}, u32[]{:S(2)}) collective-permute-start(bf16[128,1152]{1,0:T(8,128)(2,1)S(1)} %get-tuple-element.86), channel_id=1, source_target_pairs={{0,1},{1,2},{2,3},{3,11},{11,10},{10,9},{9,8},{8,0},{4,5},{5,6},{6... | collective-permute-start | bytes 884744 | tf_op jit(solution)/shard_map/ppermute | solution.py:521
  144.8 7.5 %collective-permute-start.22 = (bf16[128,1024]{1,0:T(8,128)(2,1)S(1)}, bf16[128,1024]{1,0:T(8,128)(2,1)S(1)}, u32[]{:S(2)}, u32[]{:S(2)}) collective-permute-start(bf16[128,1024]{1,0:T(8,128)(2,1)S(1)} %get-tuple-element.87), channel_id=1, source_target_pairs={{0,8},{1,0},{2,1},{3,2},{11,3},{10,11},{9,10},{8,9},{4,12},{5,4},{... | collective-permute-start | bytes 786440 | tf_op jit(solution)/shard_map/ppermute | solution.py:521
  152.7 7.6 %collective-permute-start.23 = (bf16[128,1152]{1,0:T(8,128)(2,1)S(1)}, bf16[128,1152]{1,0:T(8,128)(2,1)S(1)}, u32[]{:S(2)}, u32[]{:S(2)}) collective-permute-start(bf16[128,1152]{1,0:T(8,128)(2,1)S(1)} %get-tuple-element.93), channel_id=1, source_target_pairs={{0,1},{1,2},{2,3},{3,11},{11,10},{10,9},{9,8},{8,0},{4,5},{5,6},{6... | collective-permute-start | bytes 884744 | tf_op jit(solution)/shard_map/ppermute | solution.py:521
  153.7 6.6 %collective-permute-start.24 = (bf16[128,1024]{1,0:T(8,128)(2,1)S(1)}, bf16[128,1024]{1,0:T(8,128)(2,1)S(1)}, u32[]{:S(2)}, u32[]{:S(2)}) collective-permute-start(bf16[128,1024]{1,0:T(8,128)(2,1)S(1)} %get-tuple-element.94), channel_id=1, source_target_pairs={{0,8},{1,0},{2,1},{3,2},{11,3},{10,11},{9,10},{8,9},{4,12},{5,4},{... | collective-permute-start | bytes 786440 | tf_op jit(solution)/shard_map/ppermute | solution.py:521
  160.7 7.4 %collective-permute-start.25 = (bf16[128,1152]{1,0:T(8,128)(2,1)S(1)}, bf16[128,1152]{1,0:T(8,128)(2,1)S(1)}, u32[]{:S(2)}, u32[]{:S(2)}) collective-permute-start(bf16[128,1152]{1,0:T(8,128)(2,1)S(1)} %get-tuple-element.100), channel_id=1, source_target_pairs={{0,1},{1,2},{2,3},{3,11},{11,10},{10,9},{9,8},{8,0},{4,5},{5,6},{6... | collective-permute-start | bytes 884744 | tf_op jit(solution)/shard_map/ppermute | solution.py:521
  161.7 6.4 %collective-permute-start.26 = (bf16[128,1024]{1,0:T(8,128)(2,1)S(1)}, bf16[128,1024]{1,0:T(8,128)(2,1)S(1)}, u32[]{:S(2)}, u32[]{:S(2)}) collective-permute-start(bf16[128,1024]{1,0:T(8,128)(2,1)S(1)} %get-tuple-element.101), channel_id=1, source_target_pairs={{0,8},{1,0},{2,1},{3,2},{11,3},{10,11},{9,10},{8,9},{4,12},{5,4},{... | collective-permute-start | bytes 786440 | tf_op jit(solution)/shard_map/ppermute | solution.py:521
  168.4 9.4 %collective-permute-start.27 = (bf16[128,1152]{1,0:T(8,128)(2,1)S(1)}, bf16[128,1152]{1,0:T(8,128)(2,1)S(1)}, u32[]{:S(2)}, u32[]{:S(2)}) collective-permute-start(bf16[128,1152]{1,0:T(8,128)(2,1)S(1)} %get-tuple-element.107), channel_id=1, source_target_pairs={{0,1},{1,2},{2,3},{3,11},{11,10},{10,9},{9,8},{8,0},{4,5},{5,6},{6... | collective-permute-start | bytes 884744 | tf_op jit(solution)/shard_map/ppermute | solution.py:521
  170.2 7.6 %collective-permute-start.28 = (bf16[128,1024]{1,0:T(8,128)(2,1)S(1)}, bf16[128,1024]{1,0:T(8,128)(2,1)S(1)}, u32[]{:S(2)}, u32[]{:S(2)}) collective-permute-start(bf16[128,1024]{1,0:T(8,128)(2,1)S(1)} %get-tuple-element.108), channel_id=1, source_target_pairs={{0,8},{1,0},{2,1},{3,2},{11,3},{10,11},{9,10},{8,9},{4,12},{5,4},{... | collective-permute-start | bytes 786440 | tf_op jit(solution)/shard_map/ppermute | solution.py:521
  178.2 10.1 %collective-permute-start.29 = (bf16[128,1152]{1,0:T(8,128)(2,1)S(1)}, bf16[128,1152]{1,0:T(8,128)(2,1)S(1)}, u32[]{:S(2)}, u32[]{:S(2)}) collective-permute-start(bf16[128,1152]{1,0:T(8,128)(2,1)S(1)} %get-tuple-element.114), channel_id=1, source_target_pairs={{0,1},{1,2},{2,3},{3,11},{11,10},{10,9},{9,8},{8,0},{4,5},{5,6},{6... | collective-permute-start | bytes 884744 | tf_op jit(solution)/shard_map/ppermute | solution.py:521
  179.4 8.9 %collective-permute-start.30 = (bf16[128,1024]{1,0:T(8,128)(2,1)S(1)}, bf16[128,1024]{1,0:T(8,128)(2,1)S(1)}, u32[]{:S(2)}, u32[]{:S(2)}) collective-permute-start(bf16[128,1024]{1,0:T(8,128)(2,1)S(1)} %get-tuple-element.115), channel_id=1, source_target_pairs={{0,8},{1,0},{2,1},{3,2},{11,3},{10,11},{9,10},{8,9},{4,12},{5,4},{... | collective-permute-start | bytes 786440 | tf_op jit(solution)/shard_map/ppermute | solution.py:521
  188.8 7.5 %collective-permute-start.31 = (bf16[128,1152]{1,0:T(8,128)(2,1)S(1)}, bf16[128,1152]{1,0:T(8,128)(2,1)S(1)}, u32[]{:S(2)}, u32[]{:S(2)}) collective-permute-start(bf16[128,1152]{1,0:T(8,128)(2,1)S(1)} %get-tuple-element.121), channel_id=1, source_target_pairs={{0,1},{1,2},{2,3},{3,11},{11,10},{10,9},{9,8},{8,0},{4,5},{5,6},{6... | collective-permute-start | bytes 884744 | tf_op jit(solution)/shard_map/ppermute | solution.py:521
  189.8 6.4 %collective-permute-start.32 = (bf16[128,1024]{1,0:T(8,128)(2,1)S(1)}, bf16[128,1024]{1,0:T(8,128)(2,1)S(1)}, u32[]{:S(2)}, u32[]{:S(2)}) collective-permute-start(bf16[128,1024]{1,0:T(8,128)(2,1)S(1)} %get-tuple-element.122), channel_id=1, source_target_pairs={{0,8},{1,0},{2,1},{3,2},{11,3},{10,11},{9,10},{8,9},{4,12},{5,4},{... | collective-permute-start | bytes 786440 | tf_op jit(solution)/shard_map/ppermute | solution.py:521
  (19 other events, 306.2 us)

commit v6 on v5

--- a/solution.py
+++ b/solution.py
@@ -41,30 +41,20 @@
 
 def place_kernel(pick_ref, *refs):
     *held, out_ref = refs
-    width = out_ref.shape[1]
-    blocks = out_ref.shape[0] // (2 * ROWS)
-    for start in range(0, width, COLS):
-        quads = []
-        for quad in range(2):
-            values = [
-                ref[:, start : start + COLS] for ref in held[quad * QUAD : (quad + 1) * QUAD]
-            ]
-            rows = jnp.dot(
-                pick_ref[quad], jnp.concatenate(values, axis=0), preferred_element_type=jnp.float32
-            )
-            quads.append(rows.reshape(blocks, ROWS, COLS))
-        both = jnp.concatenate(quads, axis=1).reshape(blocks * 2 * ROWS, COLS)
-        out_ref[:, start : start + COLS] = both.astype(jnp.bfloat16)
-
-
-def in_block(shape, axis, pairs, joint):
+    for start in range(0, out_ref.shape[1], COLS):
+        columns = slice(start, start + COLS)
+        values = jnp.concatenate([ref[:, columns] for ref in held], axis=0)
+        rows = jnp.dot(pick_ref[0], values, preferred_element_type=jnp.float32)
+        out_ref[:, columns] = rows.astype(jnp.bfloat16)
+
+
+def in_block(shape, axis, quads, joint):
     slot = lax.broadcasted_iota(jnp.int32, shape, axis)
-    group = pairs * joint * 2 * ROWS
-    return slot // group * joint + slot % (joint * 2 * ROWS) // (2 * ROWS)
+    return slot // (quads * joint * ROWS) * joint + slot % (joint * ROWS) // ROWS
 
 
 def joint_rows(x_refs, first, joint, columns=slice(None)):
-    rows = slice(first * 2 * ROWS, (first + joint) * 2 * ROWS)
+    rows = slice(first * ROWS, (first + joint) * ROWS)
     return [ref[rows, columns] for ref in x_refs]
 
 
@@ -89,16 +79,16 @@
     return values + pltpu.roll(values, LANES // 2, 1)
 
 
-def main_kernel(turn, steps, pairs, sums, scale_ref, head_ref, teacher_ref, map_ref, *refs):
-    x_refs = refs[:pairs]
-    grad_ref, *loss_ref = refs[pairs:-2]
+def main_kernel(turn, steps, quads, sums, scale_ref, head_ref, teacher_ref, map_ref, *refs):
+    x_refs = refs[:quads]
+    grad_ref, *loss_ref = refs[quads:-2]
     rows_ref, slot_loss_ref = refs[-2:]
     step = pl.program_id(0)
     origin = step * turn if sums else 0
     scale = scale_ref[0]
     joint = 2 if turn % 2 == 0 else 1
-    group = pairs * joint * 2 * ROWS
-    own_block = in_block((group, BLOCK), 0, pairs, joint)
+    group = quads * joint * ROWS
+    own_block = in_block((group, BLOCK), 0, quads, joint)
     logits = []
     for first in range(0, turn, joint):
         product = lax.dot_general(
@@ -127,7 +117,7 @@
     grad = grad.astype(jnp.bfloat16)
 
     for first in range(0, turn, joint):
-        here = slice(first * pairs * 2 * ROWS, (first + joint) * pairs * 2 * ROWS)
+        here = slice(first * quads * ROWS, (first + joint) * quads * ROWS)
         lines = [
             jnp.where(own_block == k, grad[here], jnp.zeros_like(grad[here])) for k in range(joint)
         ]
@@ -136,15 +126,15 @@
             head_ref[first * BLOCK : (first + joint) * BLOCK, :],
             preferred_element_type=jnp.float32,
         )
-        for pair in range(pairs):
-            to = slice(pair * 2 * ROWS, (pair + 1) * 2 * ROWS)
+        for quad in range(quads):
+            to = slice(quad * ROWS, (quad + 1) * ROWS)
             for k in range(joint):
-                start = (pair * joint + k) * 2 * ROWS
-                rows_ref[origin + first + k, to, :] = grads[start : start + 2 * ROWS].astype(
+                start = (quad * joint + k) * ROWS
+                rows_ref[origin + first + k, to, :] = grads[start : start + ROWS].astype(
                     rows_ref.dtype
                 )
                 start += here.start
-                slot_loss_ref[origin + first + k, to, :] = loss[start : start + 2 * ROWS]
+                slot_loss_ref[origin + first + k, to, :] = loss[start : start + ROWS]
 
     if not sums:
         return
@@ -154,14 +144,14 @@
     def _():
         half = part_refs[0].shape[0]
         width = rows_ref.shape[-1]
-        for quad in range(2 * pairs):
+        for quad in range(quads):
             slots = map_ref[quad : quad + 1, :]
             token = lax.broadcasted_iota(jnp.int32, (2 * half, slots.shape[1]), 0)
             spread = jnp.where(slots == token, 1.0, 0.0).astype(jnp.bfloat16)
 
             def put(columns, total):
                 part_refs[quad][:, columns] = total[:half]
-                part_refs[2 * pairs + quad][:, columns] = total[half:]
+                part_refs[quads + quad][:, columns] = total[half:]
 
             loss = sum_quad(spread, slot_loss_ref, quad, slice(0, LANES))
             put(slice(width, width + LANES), two_parts(loss))
@@ -170,12 +160,12 @@
                 put(columns, sum_quad(spread, rows_ref, quad, columns).astype(jnp.bfloat16))
 
 
-def head_kernel(turn, splits, shift, pairs, grad_ref, *refs):
-    x_refs, (out_ref, mark_ref) = refs[:pairs], refs[-2:]
+def head_kernel(turn, splits, shift, quads, grad_ref, *refs):
+    x_refs, (out_ref, mark_ref) = refs[:quads], refs[-2:]
     joint = 2 if turn % 2 == 0 else 1
     slots = grad_ref.shape[1]
     share = turn // splits
-    place = in_block((1, slots), 1, pairs, joint) - (pl.program_id(0) + shift) % splits * share
+    place = in_block((1, slots), 1, quads, joint) - (pl.program_id(0) + shift) % splits * share
     grad = grad_ref[...]
     spaced = [grad * (place == index).astype(jnp.bfloat16) for index in range(share)]
     spaced = jnp.concatenate(spaced, axis=0)
@@ -256,7 +246,7 @@
         self.moving = [lax.ppermute(shard, CHIPS, way) for shard, way in zip(self.moving, self.ways)]
         self.got[-number], self.got[number] = (self.both(shard) for shard in self.moving)
 
-    def last(self, *behind):
+    def last(self, before, beside):
         shard = jnp.where(lax.axis_index("core") == 0, *self.moving)
         down = lax.axis_size("voc")
 
@@ -268,7 +258,8 @@
             for core in range(2)
             for source, target in self.ways[core]
         ]
-        self.got[len(self.order) // 2] = self.both(lax.ppermute(after(shard, *behind), ALL, links))
+        shard = lax.ppermute(after(shard, *before), ALL, links)
+        self.got[len(self.order) // 2] = self.both(after(shard, *beside))
 
 
 def gather_whole(hidden):
@@ -282,7 +273,7 @@
     across, down = lax.axis_size("x"), lax.axis_size("voc")
     chips = across * down
     devices = 2 * chips
-    pairs = chips // 4
+    quads = devices // QUAD
     tokens, list_width = block_ids.shape
     width = hidden.shape[1]
     blocks = head.shape[0] // BLOCK
@@ -339,22 +330,21 @@
     sent = lax.dynamic_update_slice(
         send_teacher.reshape(devices, deep, BLOCK), send_meta, (0, meta_at, 0)
     )
-    if ring:
-        sent = after(sent, *circle.moving)
-        for number in range(2, chips // 2 - 1):
-            circle.step(number)
-    got = lax.all_to_all(sent, ALL, split_axis=0, concat_axis=0, tiled=True)
-
     lanes = jnp.stack([core, 1 - core])
     pair_of = chip_of.reshape(chips // 2, 1, 2)
     source_of = (pair_of // down * 2 + lanes[None, :, None]) * down + pair_of % down
     source_of = source_of.reshape(devices)
+    if ring:
+        sent = after(sent, *circle.moving, source_of)
+        for number in range(2, chips // 2 - 1):
+            circle.step(number)
+    got = lax.all_to_all(sent, ALL, split_axis=0, concat_axis=0, tiled=True)
+
     got = got.at[source_of].get(mode="promise_in_bounds")
     meta = got[:, meta_at:].astype(jnp.int32)
     live_total = jnp.sum(meta[:, map_rows : map_rows + live_rows])
     scale = jnp.float32(tokens * devices) / live_total.astype(jnp.float32)
     slot_map = meta[:, :map_rows].reshape(devices, map_rows * BLOCK)[:, :bucket]
-    quads = devices // QUAD
     slot_map = slot_map.reshape(quads, ROWS, blocks)
     offset = jnp.arange(ROWS, dtype=jnp.int32)[None, :, None] // C * tokens - 1
     slot_map = jnp.where(slot_map > 0, slot_map + offset, -1)
@@ -366,29 +356,27 @@
         held = [circle.got[int(offset)] for offset in offsets[:-1]]
     got_teacher = got[:, :bucket].reshape(devices, C, blocks, BLOCK)
     joint = 2 if turn % 2 == 0 else 1
-    got_teacher = got_teacher.reshape(pairs, 2 * ROWS, blocks // joint, joint, BLOCK)
+    got_teacher = got_teacher.reshape(quads, ROWS, blocks // joint, joint, BLOCK)
     got_teacher = got_teacher.transpose(2, 0, 3, 1, 4).reshape(blocks * per_block, BLOCK)
 
     once = pl.Buffered(1)
-    x_rows = blocks * 2 * ROWS
+    x_rows = blocks * ROWS
     part = max(n for n in range(1, 17) if blocks % n == 0 and (n * ROWS) % 16 == 0)
     placed = []
-    for pair in range(pairs):
-        if ring and pair == pairs - 1:
-            circle.last(*placed)
+    for quad in range(quads):
+        if ring and quad == quads - 1:
+            circle.last((*placed[:-1], got_teacher, scale), placed[-1:])
             held += [circle.got[int(offset)] for offset in offsets[len(held) :]]
-        operands = []
-        for quad in range(2):
-            two = held[pair * 4 + quad * 2 : pair * 4 + quad * 2 + 2]
-            operands += [chip[lane] for lane in range(2) for chip in two]
+        two = held[quad * 2 : quad * 2 + 2]
+        operands = [chip[lane] for lane in range(2) for chip in two]
         placed.append(
             call(
                 place_kernel,
-                f"place_{pair}",
+                f"place_{quad}",
                 (blocks // part,),
-                [pl.BlockSpec((2, part * ROWS, QUAD * tokens), lambda s, p=pair: (p, s, 0))]
+                [pl.BlockSpec((1, part * ROWS, QUAD * tokens), lambda s, q=quad: (q, s, 0))]
                 + [pl.BlockSpec(o.shape, lambda s: (0, 0), pipeline_mode=once) for o in operands],
-                pl.BlockSpec((part * 2 * ROWS, width), lambda s: (s, 0)),
+                pl.BlockSpec((part * ROWS, width), lambda s: (s, 0)),
                 jax.ShapeDtypeStruct((x_rows, width), jnp.bfloat16),
                 2 * x_rows * QUAD * tokens * width,
                 2 * x_rows * width * 2,
@@ -399,7 +387,7 @@
     lane_slots = turn * per_block
     slot_spec = pl.BlockSpec((lane_slots, BLOCK), lambda s: (s, 0))
     flat_spec = pl.BlockSpec((BLOCK, lane_slots), lambda s: (0, s))
-    x_spec = pl.BlockSpec((turn * 2 * ROWS, width), lambda s: (s, 0))
+    x_spec = pl.BlockSpec((turn * ROWS, width), lambda s: (s, 0))
     flops = 2 * blocks * per_block * BLOCK * width
     if ring:
         part = (2 * tokens, width + LANES)
@@ -420,7 +408,7 @@
         ]
         scratch = []
     grad, *results = call(
-        functools.partial(main_kernel, turn, steps, pairs, ring),
+        functools.partial(main_kernel, turn, steps, quads, ring),
         "logits_and_back",
         (steps,),
         [
@@ -429,11 +417,11 @@
             slot_spec,
             pl.BlockSpec(slot_map.shape, lambda s: (0, 0), pipeline_mode=once),
         ]
-        + [x_spec] * pairs,
+        + [x_spec] * quads,
         [flat_spec] + out_specs,
         [jax.ShapeDtypeStruct((BLOCK, blocks * per_block), jnp.bfloat16)] + out_shapes,
         16 * flops,
-        head.size * 2 + pairs * x_rows * width * 2,
+        head.size * 2 + quads * x_rows * width * 2,
         52,
         scratch,
     )(
@@ -472,8 +460,8 @@
         count = cuts[number + 1] - shift
         specs = [pl.BlockSpec((BLOCK, lane_slots), lambda s, d=shift: (0, (s + d) // splits))]
         specs += [
-            pl.BlockSpec((turn * 2 * ROWS, width), lambda s, d=shift: ((s + d) // splits, 0))
-        ] * pairs
+            pl.BlockSpec((turn * ROWS, width), lambda s, d=shift: ((s + d) // splits, 0))
+        ] * quads
         operands = [grad if behind is None else after(grad, behind), *placed]
         aliases = {}
         if filled:
@@ -481,7 +469,7 @@
             aliases = {len(operands): 0}
             operands.append(filled[-1])
         out, mark = call(
-            functools.partial(head_kernel, turn, splits, shift, pairs),
+            functools.partial(head_kernel, turn, splits, shift, quads),
             f"head_grad_{number}",
             (count,),
             specs,
@@ -494,7 +482,7 @@
                 jax.ShapeDtypeStruct((8, LANES), jnp.float32),
             ],
             turn * flops // lots,
-            (head.size + pairs * x_rows * width) * 2 // lots,
+            (head.size + quads * x_rows * width) * 2 // lots,
             28,
             aliases=aliases,
         )(*operands)

time: 199 us -> 197 us (0.990)
  waiting for transfers between devices: 58 us -> 46.8 us
  Pallas kernels: 83.2 us -> 90 us
    ppermute x6, waiting for transfers between devices: 31.1 us -> 23.5 us  [step(): lax.ppermute(shard, CHIPS, way)]
    pallas_call x10 -> x12, Pallas kernels: 79.5 us -> 86.3 us  [the longest x1 36.2 us: on_device(): call(functools.partial(main_kernel, turn, steps, quads, ring), 'logits_an...]
    ppermute x1, waiting for transfers between devices: 6.49 us -> 0.72 us  [last(): shard = lax.ppermute(after(shard, *before), ALL, links)]
  transfers between devices with their start and end apart: 34 -> 34, of which waited for: 14 -> 16; matrix products, arithmetic and copies ran while one was open for 9% -> 9% of each run, Pallas kernels for 18% -> 23%
where the time goes in v6:
time: 197 us; the launch traced here: 196 us
  Pallas kernels  90 us (46%)
  waiting for transfers between devices  46.8 us (24%)
  starting transfers between devices  36.9 us (19%)
  local copies, waits for them, and re-layouts  10.5 us (5%)
  other arithmetic  7.7 us (4%)
  matrix products  2.92 us (1%)
    pallas_call x1, Pallas kernels, on_device(): call(functools.partial(main_kernel, turn, steps, quads, ring), 'logits_an...  36.2 us
    pallas_call x7, Pallas kernels, fill(): call(functools.partial(head_kernel, turn, splits, shift, quads), f'head_g...  27.5 us
    ppermute x6, waiting for transfers between devices, step(): lax.ppermute(shard, CHIPS, way)  23.5 us
    pallas_call x4, Pallas kernels, on_device(): call(place_kernel, f'place_{quad}', (blocks // part,), [pl.BlockSpec((1,...  22.6 us
    ppermute x14, waiting for transfers between devices, on_device(): moved = lax.ppermute(sums[way], CHIPS, circle.ways[way])  18.7 us
    ppermute x14, starting transfers between devices, on_device(): moved = lax.ppermute(sums[way], CHIPS, circle.ways[way])  14.8 us
    ppermute x6, starting transfers between devices, step(): lax.ppermute(shard, CHIPS, way)  10.6 us
    all_to_all x1, starting transfers between devices, on_device(): got = lax.all_to_all(sent, ALL, split_axis=0, concat_axis=0, tiled=True)  4.98 us
  transfers between devices with their start and end apart: 34, of which 16 were waited for; matrix products, arithmetic and copies ran while one was open for 9% of the time, Pallas kernels for 23%

profile of v6, /device:TPU:0, one launch (start us, length us, event | category | flops | bytes accessed | tf_op | source)
XLA Modules:
  0.0 196.4 jit_solution(12847321966065188986)
XLA Ops:
  0.6 3.0 %collective-permute-start.1 = (bf16[128,2048]{1,0:T(8,128)(2,1)}, bf16[128,2048]{1,0:T(8,128)(2,1)S(1)}, u32[]{:S(2)}, u32[]{:S(2)}) collective-permute-start(bf16[128,2048]{1,0:T(8,128)(2,1)} %refs_0_.1), channel_id=1, source_target_pairs={{0,8},{1,0},{2,1},{3,2},{11,3},{10,11},{9,10},{8,9},{4,12},{5,4},{... | collective-permute-start | bytes 1572872 | tf_op jit(solution)/shard_map/ppermute | solution.py:246
  6.1 1.6 select_reduce_fusion
  8.6 2.9 %fusion.4 = bf16[2816,128]{1,0:T(8,128)(2,1)} fusion(s32[1024]{0:T(1024)S(1)} %get-tuple-element.134, bf16[128,8,128]{2,1,0:T(8,128)(2,1)S(1)} %copy-done), kind=kOutput, calls=%fused_computation.12 | convolution fusion | flops 741441536 | bytes 987136 | tf_op jit(solution)/shard_map/dot_general | solution.py:313
  12.2 3.6 %collective-permute-done.1.refs_1_ = bf16[128,2048]{1,0:T(8,128)(2,1)S(1)} collective-permute-done((bf16[128,2048]{1,0:T(8,128)(2,1)}, bf16[128,2048]{1,0:T(8,128)(2,1)S(1)}, u32[]{:S(2)}, u32[]{:S(2)}) %collective-permute-start.1) | collective-permute-done | bytes 524320 | tf_op jit(solution)/shard_map/ppermute | solution.py:246
  17.2 5.0 %all-to-all-start = ((bf16[16,176,128]{2,1,0:T(8,128)(2,1)}), bf16[16,176,128]{2,1,0:T(8,128)(2,1)S(1)}, u32[]{:S(2)}, u32[]{:S(2)}) async-start(bf16[16,176,128]{2,1,0:T(8,128)(2,1)} %maximum_dynamic-update-slice_fusion), calls=%async_computation | async-start | bytes 1441792 | tf_op jit(solution)/shard_map/all_to_all | solution.py:341
  24.8 1.7 collective-permute-start.4
  27.6 18.5 %collective-permute-done.4.refs_1_ = bf16[128,2048]{1,0:T(8,128)(2,1)} collective-permute-done((bf16[128,2048]{1,0:T(8,128)(2,1)S(1)}, bf16[128,2048]{1,0:T(8,128)(2,1)}, u32[]{:S(2)}, u32[]{:S(2)}) %collective-permute-start.4) | collective-permute-done | bytes 524320 | tf_op jit(solution)/shard_map/ppermute | solution.py:246
  47.3 1.8 fusion.2.pick_ref
  49.1 5.3 %collective-permute-start.8 = (bf16[128,2048]{1,0:T(8,128)(2,1)}, bf16[128,2048]{1,0:T(8,128)(2,1)S(1)}, u32[]{:S(2)}, u32[]{:S(2)}) collective-permute-start(bf16[128,2048]{1,0:T(8,128)(2,1)} %collective-permute-done.4.refs_1_), channel_id=1, source_target_pairs={{0,1},{1,2},{2,3},{3,11},{11,10},{10,9},{9,8},{8,0},{4,5},{5,6},{6... | collective-permute-start | bytes 1572872 | tf_op jit(solution)/shard_map/ppermute | solution.py:246
  54.4 2.0 %slice.30 = bf16[16,160,128]{2,1,0:T(8,128)(2,1)} slice(bf16[16,176,128]{2,1,0:T(8,128)(2,1)} %copy-done.13), slice={[0:16], [0:160], [0:128]} | slice | bytes 1310720 | tf_op jit(solution)/shard_map/slice | solution.py:357
  59.4 5.6 %place_0.1.refs_0_ = bf16[640,2048]{1,0:T(8,128)(2,1)} custom-call(bf16[4,640,512]{2,1,0:T(8,128)(2,1)} %fusion.2.pick_ref, bf16[128,2048]{1,0:T(8,128)(2,1)S(1)} %collective-permute-done.refs_0_, bf16[128,2048]{1,0:T(8,128)(2,1)S(1)} %collective-permute-done.1.refs_1_, bf16[128,2048]{1,0:T(8,128)(2,1)} %collective-permute-done.2.refs_2_, ...), custom_call_target="tpu_custom_call" | custom-call | flops 1342177280 | bytes 5242880 | tf_op jit(solution)/shard_map/place_0/pallas_call | solution.py:373
  65.0 5.8 %place_1.1.refs_1_ = bf16[640,2048]{1,0:T(8,128)(2,1)} custom-call(bf16[4,640,512]{2,1,0:T(8,128)(2,1)} %fusion.2.pick_ref, bf16[128,2048]{1,0:T(8,128)(2,1)S(1)} %copy-done.11, bf16[128,2048]{1,0:T(8,128)(2,1)} %collective-permute-done.4.refs_1_, bf16[128,2048]{1,0:T(8,128)(2,1)} %collective-permute-done.5.refs_2_, ...), custom_call_target="tpu_custom_call" | custom-call | flops 1342177280 | bytes 5242880 | tf_op jit(solution)/shard_map/place_1/pallas_call | solution.py:373
  71.2 2.8 %collective-permute-start.12 = (bf16[128,2048]{1,0:T(8,128)(2,1)S(1)}, bf16[128,2048]{1,0:T(8,128)(2,1)S(1)}, u32[]{:S(2)}, u32[]{:S(2)}) collective-permute-start(bf16[128,2048]{1,0:T(8,128)(2,1)S(1)} %broadcast_select_fusion), channel_id=1, source_target_pairs={{0,1},{1,2},{2,3},{3,11},{11,10},{10,9},{9,8},{8,0},{4,12},{5,4},{... | collective-permute-start | bytes 1572872 | tf_op jit(solution)/shard_map/ppermute | solution.py:261
  75.9 5.7 %place_2.1.refs_2_ = bf16[640,2048]{1,0:T(8,128)(2,1)} custom-call(bf16[4,640,512]{2,1,0:T(8,128)(2,1)} %fusion.2.pick_ref, bf16[128,2048]{1,0:T(8,128)(2,1)} %collective-permute-done.7.refs_0_, bf16[128,2048]{1,0:T(8,128)(2,1)S(1)} %collective-permute-done.8.refs_1_, bf16[128,2048]{1,0:T(8,128)(2,1)S(1)} %collective-permute-done.9.refs_2_, ...), custom_call_target="tpu_custom_call" | custom-call | flops 1342177280 | bytes 5242880 | tf_op jit(solution)/shard_map/place_2/pallas_call | solution.py:373
  82.3 1.9 collective-permute-done.14.refs_3_
  85.0 5.4 %place_3.1.refs_3_ = bf16[640,2048]{1,0:T(8,128)(2,1)} custom-call(bf16[4,640,512]{2,1,0:T(8,128)(2,1)} %fusion.2.pick_ref, bf16[128,2048]{1,0:T(8,128)(2,1)S(1)} %collective-permute-done.11.refs_0_, bf16[128,2048]{1,0:T(8,128)(2,1)S(1)} %collective-permute-done.12.refs_1_, bf16[128,2048]{1,0:T(8,128)(2,1)S(1)} %collective-permute-done.13.refs_2_, ...), custom_call_target="tpu_custom_call" | custom-call | flops 1342177280 | bytes 5242880 | tf_op jit(solution)/shard_map/place_3/pallas_call | solution.py:373
  90.4 36.2 %logits_and_back.1 = (bf16[128,2560]{1,0:T(8,128)(2,1)S(1)}, bf16[256,2176]{1,0:T(8,128)(2,1)}, bf16[256,2176]{1,0:T(8,128)(2,1)}, bf16[256,2176]{1,0:T(8,128)(2...) custom-call(f32[1]{0:T(128)} %bitcast.6.scale_ref, ...), custom_call_target="tpu_custom_call" | custom-call | flops 21474836480 | bytes 52428800 | tf_op jit(solution)/shard_map/logits_and_back/pallas_call | solution.py:410
  127.7 1.9 collective-permute-done.16
  133.4 2.8 %head_grad_0.1 = (bf16[10240,2048]{1,0:T(8,128)(2,1)}, f32[8,128]{1,0:T(8,128)}) custom-call(bf16[128,2560]{1,0:T(8,128)(2,1)S(1)} %get-tuple-element.125.grad_ref, bf16[640,2048]{1,0:T(8,128)(2,1)S(1)} %copy-done.2, bf16[640,2048]{1,0:T(8,128)(2,1)S(1)} %copy-done.3, bf16[640,2048]{1,0:T(8,128)(2,1)S(1)} %copy-done.4, bf16[640,2048]{1,0:T(8,128)(2,1)S(1)} %copy-done.5), custom_call_target="tpu_custom_call" | custom-call | flops 1533916928 | bytes 7489828 | tf_op jit(solution)/shard_map/head_grad_0/pallas_call | solution.py:471
  136.3 4.2 %collective-permute-done.20.refs_7_ = bf16[128,1024]{1,0:T(8,128)(2,1)S(1)} collective-permute-done((bf16[128,1024]{1,0:T(8,128)(2,1)S(1)}, bf16[128,1024]{1,0:T(8,128)(2,1)S(1)}, u32[]{:S(2)}, u32[]{:S(2)}) %collective-permute-start.20) | collective-permute-done | bytes 262176 | tf_op jit(solution)/shard_map/ppermute | solution.py:509
  141.0 1.7 collective-permute-start.21
  143.3 4.1 %head_grad_1.1 = (bf16[10240,2048]{1,0:T(8,128)(2,1)}, f32[8,128]{1,0:T(8,128)}) custom-call(bf16[128,2560]{1,0:T(8,128)(2,1)S(1)} %get-tuple-element.125.grad_ref, bf16[640,2048]{1,0:T(8,128)(2,1)S(1)} %copy-done.2, bf16[640,2048]{1,0:T(8,128)(2,1)S(1)} %copy-done.3, bf16[640,2048]{1,0:T(8,128)(2,1)S(1)} %copy-done.4, ...), custom_call_target="tpu_custom_call", output_to_operand_aliasing={{0}: (5, {})} | custom-call | flops 1533916928 | bytes 7489828 | tf_op jit(solution)/shard_map/head_grad_1/pallas_call | solution.py:471
  147.4 2.2 %collective-permute-done.22.refs_7_ = bf16[128,1024]{1,0:T(8,128)(2,1)S(1)} collective-permute-done((bf16[128,1024]{1,0:T(8,128)(2,1)S(1)}, bf16[128,1024]{1,0:T(8,128)(2,1)S(1)}, u32[]{:S(2)}, u32[]{:S(2)}) %collective-permute-start.22) | collective-permute-done | bytes 262176 | tf_op jit(solution)/shard_map/ppermute | solution.py:509
  152.2 4.1 %head_grad_2.1 = (bf16[10240,2048]{1,0:T(8,128)(2,1)}, f32[8,128]{1,0:T(8,128)}) custom-call(bf16[128,2560]{1,0:T(8,128)(2,1)S(1)} %get-tuple-element.125.grad_ref, bf16[640,2048]{1,0:T(8,128)(2,1)S(1)} %copy-done.2, bf16[640,2048]{1,0:T(8,128)(2,1)S(1)} %copy-done.3, bf16[640,2048]{1,0:T(8,128)(2,1)S(1)} %copy-done.4, ...), custom_call_target="tpu_custom_call", output_to_operand_aliasing={{0}: (5, {})} | custom-call | flops 1533916928 | bytes 7489828 | tf_op jit(solution)/shard_map/head_grad_2/pallas_call | solution.py:471
  160.5 4.1 %head_grad_3.1 = (bf16[10240,2048]{1,0:T(8,128)(2,1)}, f32[8,128]{1,0:T(8,128)}) custom-call(bf16[128,2560]{1,0:T(8,128)(2,1)S(1)} %get-tuple-element.125.grad_ref, bf16[640,2048]{1,0:T(8,128)(2,1)S(1)} %copy-done.2, bf16[640,2048]{1,0:T(8,128)(2,1)S(1)} %copy-done.3, bf16[640,2048]{1,0:T(8,128)(2,1)S(1)} %copy-done.4, ...), custom_call_target="tpu_custom_call", output_to_operand_aliasing={{0}: (5, {})} | custom-call | flops 1533916928 | bytes 7489828 | tf_op jit(solution)/shard_map/head_grad_3/pallas_call | solution.py:471
  165.9 1.8 collective-permute-start.27
  168.0 4.1 %head_grad_4.1 = (bf16[10240,2048]{1,0:T(8,128)(2,1)}, f32[8,128]{1,0:T(8,128)}) custom-call(bf16[128,2560]{1,0:T(8,128)(2,1)S(1)} %get-tuple-element.125.grad_ref, bf16[640,2048]{1,0:T(8,128)(2,1)S(1)} %copy-done.2, bf16[640,2048]{1,0:T(8,128)(2,1)S(1)} %copy-done.3, bf16[640,2048]{1,0:T(8,128)(2,1)S(1)} %copy-done.4, ...), custom_call_target="tpu_custom_call", output_to_operand_aliasing={{0}: (5, {})} | custom-call | flops 1533916928 | bytes 7489828 | tf_op jit(solution)/shard_map/head_grad_4/pallas_call | solution.py:471
  172.1 3.8 %collective-permute-done.28.refs_7_ = bf16[128,1024]{1,0:T(8,128)(2,1)S(1)} collective-permute-done((bf16[128,1024]{1,0:T(8,128)(2,1)S(1)}, bf16[128,1024]{1,0:T(8,128)(2,1)S(1)}, u32[]{:S(2)}, u32[]{:S(2)}) %collective-permute-start.28) | collective-permute-done | bytes 262176 | tf_op jit(solution)/shard_map/ppermute | solution.py:509
  178.4 4.1 %head_grad_5.1 = (bf16[10240,2048]{1,0:T(8,128)(2,1)}, f32[8,128]{1,0:T(8,128)}) custom-call(bf16[128,2560]{1,0:T(8,128)(2,1)S(1)} %get-tuple-element.125.grad_ref, bf16[640,2048]{1,0:T(8,128)(2,1)S(1)} %copy-done.2, bf16[640,2048]{1,0:T(8,128)(2,1)S(1)} %copy-done.3, bf16[640,2048]{1,0:T(8,128)(2,1)S(1)} %copy-done.4, ...), custom_call_target="tpu_custom_call", output_to_operand_aliasing={{0}: (5, {})} | custom-call | flops 1533916928 | bytes 7489828 | tf_op jit(solution)/shard_map/head_grad_5/pallas_call | solution.py:471
  182.5 4.0 %collective-permute-done.30.refs_7_ = bf16[128,1024]{1,0:T(8,128)(2,1)S(1)} collective-permute-done((bf16[128,1024]{1,0:T(8,128)(2,1)S(1)}, bf16[128,1024]{1,0:T(8,128)(2,1)S(1)}, u32[]{:S(2)}, u32[]{:S(2)}) %collective-permute-start.30) | collective-permute-done | bytes 262176 | tf_op jit(solution)/shard_map/ppermute | solution.py:509
  189.0 4.1 %head_grad_6.1 = (bf16[10240,2048]{1,0:T(8,128)(2,1)}, f32[8,128]{1,0:T(8,128)}) custom-call(bf16[128,2560]{1,0:T(8,128)(2,1)S(1)} %get-tuple-element.125.grad_ref, bf16[640,2048]{1,0:T(8,128)(2,1)S(1)} %copy-done.2, bf16[640,2048]{1,0:T(8,128)(2,1)S(1)} %copy-done.3, bf16[640,2048]{1,0:T(8,128)(2,1)S(1)} %copy-done.4, ...), custom_call_target="tpu_custom_call", output_to_operand_aliasing={{0}: (5, {})} | custom-call | flops 1533916928 | bytes 7489828 | tf_op jit(solution)/shard_map/head_grad_6/pallas_call | solution.py:471
  193.1 1.5 collective-permute-done.32.refs_7_
  (133 shorter events, 36.9 us)
Async XLA Ops:
  0.6 15.2 %collective-permute-start.1 = (bf16[128,2048]{1,0:T(8,128)(2,1)}, bf16[128,2048]{1,0:T(8,128)(2,1)S(1)}, u32[]{:S(2)}, u32[]{:S(2)}) collective-permute-start(bf16[128,2048]{1,0:T(8,128)(2,1)} %refs_0_.1), channel_id=1, source_target_pairs={{0,8},{1,0},{2,1},{3,2},{11,3},{10,11},{9,10},{8,9},{4,12},{5,4},{... | collective-permute-start | bytes 1572872 | tf_op jit(solution)/shard_map/ppermute | solution.py:246
  3.6 13.6 %collective-permute-start = (bf16[128,2048]{1,0:T(8,128)(2,1)}, bf16[128,2048]{1,0:T(8,128)(2,1)S(1)}, u32[]{:S(2)}, u32[]{:S(2)}) collective-permute-start(bf16[128,2048]{1,0:T(8,128)(2,1)} %refs_0_.1), channel_id=1, source_target_pairs={{0,1},{1,2},{2,3},{3,11},{11,10},{10,9},{9,8},{8,0},{4,5},{5,6},{6... | collective-permute-start | bytes 1572872 | tf_op jit(solution)/shard_map/ppermute | solution.py:246
  17.2 28.9 %all-to-all-start = ((bf16[16,176,128]{2,1,0:T(8,128)(2,1)}), bf16[16,176,128]{2,1,0:T(8,128)(2,1)S(1)}, u32[]{:S(2)}, u32[]{:S(2)}) async-start(bf16[16,176,128]{2,1,0:T(8,128)(2,1)} %maximum_dynamic-update-slice_fusion), calls=%async_computation | async-start | bytes 1441792 | tf_op jit(solution)/shard_map/all_to_all | solution.py:341
  22.2 42.8 %collective-permute-start.5 = (bf16[128,2048]{1,0:T(8,128)(2,1)S(1)}, bf16[128,2048]{1,0:T(8,128)(2,1)}, u32[]{:S(2)}, u32[]{:S(2)}) collective-permute-start(bf16[128,2048]{1,0:T(8,128)(2,1)S(1)} %copy-done.11), channel_id=1, source_target_pairs={{0,4},{4,0},{1,5},{5,1},{2,6},{6,2},{3,7},{7,3},{8,12},{12,8},{9,1... | collective-permute-start | bytes 1572872 | tf_op jit(solution)/shard_map/ppermute | solution.py:241
  24.8 21.3 %collective-permute-start.4 = (bf16[128,2048]{1,0:T(8,128)(2,1)S(1)}, bf16[128,2048]{1,0:T(8,128)(2,1)}, u32[]{:S(2)}, u32[]{:S(2)}) collective-permute-start(bf16[128,2048]{1,0:T(8,128)(2,1)S(1)} %collective-permute-done.refs_0_), channel_id=1, source_target_pairs={{0,1},{1,2},{2,3},{3,11},{11,10},{10,9},{9,8},{8,0},{4,5},{5,6},{6... | collective-permute-start | bytes 1572872 | tf_op jit(solution)/shard_map/ppermute | solution.py:246
  26.7 22.4 %collective-permute-start.7 = (bf16[128,2048]{1,0:T(8,128)(2,1)S(1)}, bf16[128,2048]{1,0:T(8,128)(2,1)}, u32[]{:S(2)}, u32[]{:S(2)}) collective-permute-start(bf16[128,2048]{1,0:T(8,128)(2,1)S(1)} %collective-permute-done.1.refs_1_), channel_id=1, source_target_pairs={{0,8},{1,0},{2,1},{3,2},{11,3},{10,11},{9,10},{8,9},{4,12},{5,4},{... | collective-permute-start | bytes 1572872 | tf_op jit(solution)/shard_map/ppermute | solution.py:246
  27.1 27.3 %collective-permute-start.3 = (bf16[128,2048]{1,0:T(8,128)(2,1)S(1)}, bf16[128,2048]{1,0:T(8,128)(2,1)}, u32[]{:S(2)}, u32[]{:S(2)}) collective-permute-start(bf16[128,2048]{1,0:T(8,128)(2,1)S(1)} %collective-permute-done.1.refs_1_), channel_id=1, source_target_pairs={{0,4},{4,0},{1,5},{5,1},{2,6},{6,2},{3,7},{7,3},{8,12},{12,8},{9,1... | collective-permute-start | bytes 1572872 | tf_op jit(solution)/shard_map/ppermute | solution.py:241
  27.1 32.0 %collective-permute-start.2 = (bf16[128,2048]{1,0:T(8,128)(2,1)S(1)}, bf16[128,2048]{1,0:T(8,128)(2,1)}, u32[]{:S(2)}, u32[]{:S(2)}) collective-permute-start(bf16[128,2048]{1,0:T(8,128)(2,1)S(1)} %collective-permute-done.refs_0_), channel_id=1, source_target_pairs={{0,4},{4,0},{1,5},{5,1},{2,6},{6,2},{3,7},{7,3},{8,12},{12,8},{9,1... | collective-permute-start | bytes 1572872 | tf_op jit(solution)/shard_map/ppermute | solution.py:241
  46.1 18.8 %collective-permute-start.6 = (bf16[128,2048]{1,0:T(8,128)(2,1)}, bf16[128,2048]{1,0:T(8,128)(2,1)}, u32[]{:S(2)}, u32[]{:S(2)}) collective-permute-start(bf16[128,2048]{1,0:T(8,128)(2,1)} %collective-permute-done.4.refs_1_), channel_id=1, source_target_pairs={{0,4},{4,0},{1,5},{5,1},{2,6},{6,2},{3,7},{7,3},{8,12},{12,8},{9,1... | collective-permute-start | bytes 1572872 | tf_op jit(solution)/shard_map/ppermute | solution.py:241
  49.1 21.7 %collective-permute-start.8 = (bf16[128,2048]{1,0:T(8,128)(2,1)}, bf16[128,2048]{1,0:T(8,128)(2,1)S(1)}, u32[]{:S(2)}, u32[]{:S(2)}) collective-permute-start(bf16[128,2048]{1,0:T(8,128)(2,1)} %collective-permute-done.4.refs_1_), channel_id=1, source_target_pairs={{0,1},{1,2},{2,3},{3,11},{11,10},{10,9},{9,8},{8,0},{4,5},{5,6},{6... | collective-permute-start | bytes 1572872 | tf_op jit(solution)/shard_map/ppermute | solution.py:246
  54.4 16.7 %collective-permute-start.11 = (bf16[128,2048]{1,0:T(8,128)(2,1)}, bf16[128,2048]{1,0:T(8,128)(2,1)S(1)}, u32[]{:S(2)}, u32[]{:S(2)}) collective-permute-start(bf16[128,2048]{1,0:T(8,128)(2,1)} %collective-permute-done.7.refs_0_), channel_id=1, source_target_pairs={{0,8},{1,0},{2,1},{3,2},{11,3},{10,11},{9,10},{8,9},{4,12},{5,4},{... | collective-permute-start | bytes 1572872 | tf_op jit(solution)/shard_map/ppermute | solution.py:246
  59.1 16.0 %collective-permute-start.9 = (bf16[128,2048]{1,0:T(8,128)(2,1)}, bf16[128,2048]{1,0:T(8,128)(2,1)S(1)}, u32[]{:S(2)}, u32[]{:S(2)}) collective-permute-start(bf16[128,2048]{1,0:T(8,128)(2,1)} %collective-permute-done.7.refs_0_), channel_id=1, source_target_pairs={{0,4},{4,0},{1,5},{5,1},{2,6},{6,2},{3,7},{7,3},{8,12},{12,8},{9,1... | collective-permute-start | bytes 1572872 | tf_op jit(solution)/shard_map/ppermute | solution.py:241
  70.8 4.3 %collective-permute-start.10 = (bf16[128,2048]{1,0:T(8,128)(2,1)S(1)}, bf16[128,2048]{1,0:T(8,128)(2,1)S(1)}, u32[]{:S(2)}, u32[]{:S(2)}) collective-permute-start(bf16[128,2048]{1,0:T(8,128)(2,1)S(1)} %collective-permute-done.8.refs_1_), channel_id=1, source_target_pairs={{0,4},{4,0},{1,5},{5,1},{2,6},{6,2},{3,7},{7,3},{8,12},{12,8},{9,1... | collective-permute-start | bytes 1572872 | tf_op jit(solution)/shard_map/ppermute | solution.py:241
  71.2 11.1 %collective-permute-start.12 = (bf16[128,2048]{1,0:T(8,128)(2,1)S(1)}, bf16[128,2048]{1,0:T(8,128)(2,1)S(1)}, u32[]{:S(2)}, u32[]{:S(2)}) collective-permute-start(bf16[128,2048]{1,0:T(8,128)(2,1)S(1)} %broadcast_select_fusion), channel_id=1, source_target_pairs={{0,1},{1,2},{2,3},{3,11},{11,10},{10,9},{9,8},{8,0},{4,12},{5,4},{... | collective-permute-start | bytes 1572872 | tf_op jit(solution)/shard_map/ppermute | solution.py:261
  74.0 8.3 %collective-permute-start.13 = (bf16[128,2048]{1,0:T(8,128)(2,1)S(1)}, bf16[128,2048]{1,0:T(8,128)(2,1)S(1)}, u32[]{:S(2)}, u32[]{:S(2)}) collective-permute-start(bf16[128,2048]{1,0:T(8,128)(2,1)S(1)} %collective-permute-done.11.refs_0_), channel_id=1, source_target_pairs={{0,4},{4,0},{1,5},{5,1},{2,6},{6,2},{3,7},{7,3},{8,12},{12,8},{9,1... | collective-permute-start | bytes 1572872 | tf_op jit(solution)/shard_map/ppermute | solution.py:241
  126.8 13.7 %collective-permute-start.15 = (bf16[256,2176]{1,0:T(8,128)(2,1)}, bf16[256,2176]{1,0:T(8,128)(2,1)S(1)}, u32[]{:S(2)}, u32[]{:S(2)}) collective-permute-start(bf16[256,2176]{1,0:T(8,128)(2,1)} %get-tuple-element.74), channel_id=1, source_target_pairs={{0,4},{4,0},{1,5},{5,1},{2,6},{6,2},{3,7},{7,3},{8,12},{12,8},{9,1... | collective-permute-start | bytes 3342344 | tf_op jit(solution)/shard_map/ppermute | solution.py:450
  127.2 13.4 %collective-permute-start.17 = (bf16[256,2176]{1,0:T(8,128)(2,1)}, bf16[256,2176]{1,0:T(8,128)(2,1)S(1)}, u32[]{:S(2)}, u32[]{:S(2)}) collective-permute-start(bf16[256,2176]{1,0:T(8,128)(2,1)} %get-tuple-element.78), channel_id=1, source_target_pairs={{0,4},{4,0},{1,5},{5,1},{2,6},{6,2},{3,7},{7,3},{8,12},{12,8},{9,1... | collective-permute-start | bytes 3342344 | tf_op jit(solution)/shard_map/ppermute | solution.py:450
  127.3 22.4 %collective-permute-start.18 = (bf16[256,2176]{1,0:T(8,128)(2,1)}, bf16[256,2176]{1,0:T(8,128)(2,1)S(1)}, u32[]{:S(2)}, u32[]{:S(2)}) collective-permute-start(bf16[256,2176]{1,0:T(8,128)(2,1)} %get-tuple-element.80), channel_id=1, source_target_pairs={{0,4},{4,0},{1,5},{5,1},{2,6},{6,2},{3,7},{7,3},{8,12},{12,8},{9,1... | collective-permute-start | bytes 3342344 | tf_op jit(solution)/shard_map/ppermute | solution.py:450
  131.2 9.4 %collective-permute-start.19 = (bf16[128,1152]{1,0:T(8,128)(2,1)S(1)}, bf16[128,1152]{1,0:T(8,128)(2,1)S(1)}, u32[]{:S(2)}, u32[]{:S(2)}) collective-permute-start(bf16[128,1152]{1,0:T(8,128)(2,1)S(1)} %get-tuple-element.81), channel_id=1, source_target_pairs={{0,1},{1,2},{2,3},{3,11},{11,10},{10,9},{9,8},{8,0},{4,5},{5,6},{6... | collective-permute-start | bytes 884744 | tf_op jit(solution)/shard_map/ppermute | solution.py:509
  132.1 8.4 %collective-permute-start.20 = (bf16[128,1024]{1,0:T(8,128)(2,1)S(1)}, bf16[128,1024]{1,0:T(8,128)(2,1)S(1)}, u32[]{:S(2)}, u32[]{:S(2)}) collective-permute-start(bf16[128,1024]{1,0:T(8,128)(2,1)S(1)} %get-tuple-element.83), channel_id=1, source_target_pairs={{0,8},{1,0},{2,1},{3,2},{11,3},{10,11},{9,10},{8,9},{4,12},{5,4},{... | collective-permute-start | bytes 786440 | tf_op jit(solution)/shard_map/ppermute | solution.py:509
  141.0 8.8 %collective-permute-start.21 = (bf16[128,1152]{1,0:T(8,128)(2,1)S(1)}, bf16[128,1152]{1,0:T(8,128)(2,1)S(1)}, u32[]{:S(2)}, u32[]{:S(2)}) collective-permute-start(bf16[128,1152]{1,0:T(8,128)(2,1)S(1)} %get-tuple-element.88), channel_id=1, source_target_pairs={{0,1},{1,2},{2,3},{3,11},{11,10},{10,9},{9,8},{8,0},{4,5},{5,6},{6... | collective-permute-start | bytes 884744 | tf_op jit(solution)/shard_map/ppermute | solution.py:509
  142.7 6.9 %collective-permute-start.22 = (bf16[128,1024]{1,0:T(8,128)(2,1)S(1)}, bf16[128,1024]{1,0:T(8,128)(2,1)S(1)}, u32[]{:S(2)}, u32[]{:S(2)}) collective-permute-start(bf16[128,1024]{1,0:T(8,128)(2,1)S(1)} %get-tuple-element.89), channel_id=1, source_target_pairs={{0,8},{1,0},{2,1},{3,2},{11,3},{10,11},{9,10},{8,9},{4,12},{5,4},{... | collective-permute-start | bytes 786440 | tf_op jit(solution)/shard_map/ppermute | solution.py:509
  150.1 7.9 %collective-permute-start.23 = (bf16[128,1152]{1,0:T(8,128)(2,1)S(1)}, bf16[128,1152]{1,0:T(8,128)(2,1)S(1)}, u32[]{:S(2)}, u32[]{:S(2)}) collective-permute-start(bf16[128,1152]{1,0:T(8,128)(2,1)S(1)} %get-tuple-element.95), channel_id=1, source_target_pairs={{0,1},{1,2},{2,3},{3,11},{11,10},{10,9},{9,8},{8,0},{4,5},{5,6},{6... | collective-permute-start | bytes 884744 | tf_op jit(solution)/shard_map/ppermute | solution.py:509
  151.4 6.4 %collective-permute-start.24 = (bf16[128,1024]{1,0:T(8,128)(2,1)S(1)}, bf16[128,1024]{1,0:T(8,128)(2,1)S(1)}, u32[]{:S(2)}, u32[]{:S(2)}) collective-permute-start(bf16[128,1024]{1,0:T(8,128)(2,1)S(1)} %get-tuple-element.96), channel_id=1, source_target_pairs={{0,8},{1,0},{2,1},{3,2},{11,3},{10,11},{9,10},{8,9},{4,12},{5,4},{... | collective-permute-start | bytes 786440 | tf_op jit(solution)/shard_map/ppermute | solution.py:509
  158.4 7.2 %collective-permute-start.25 = (bf16[128,1152]{1,0:T(8,128)(2,1)S(1)}, bf16[128,1152]{1,0:T(8,128)(2,1)S(1)}, u32[]{:S(2)}, u32[]{:S(2)}) collective-permute-start(bf16[128,1152]{1,0:T(8,128)(2,1)S(1)} %get-tuple-element.102), channel_id=1, source_target_pairs={{0,1},{1,2},{2,3},{3,11},{11,10},{10,9},{9,8},{8,0},{4,5},{5,6},{6... | collective-permute-start | bytes 884744 | tf_op jit(solution)/shard_map/ppermute | solution.py:509
  159.2 6.4 %collective-permute-start.26 = (bf16[128,1024]{1,0:T(8,128)(2,1)S(1)}, bf16[128,1024]{1,0:T(8,128)(2,1)S(1)}, u32[]{:S(2)}, u32[]{:S(2)}) collective-permute-start(bf16[128,1024]{1,0:T(8,128)(2,1)S(1)} %get-tuple-element.103), channel_id=1, source_target_pairs={{0,8},{1,0},{2,1},{3,2},{11,3},{10,11},{9,10},{8,9},{4,12},{5,4},{... | collective-permute-start | bytes 786440 | tf_op jit(solution)/shard_map/ppermute | solution.py:509
  165.9 10.0 %collective-permute-start.27 = (bf16[128,1152]{1,0:T(8,128)(2,1)S(1)}, bf16[128,1152]{1,0:T(8,128)(2,1)S(1)}, u32[]{:S(2)}, u32[]{:S(2)}) collective-permute-start(bf16[128,1152]{1,0:T(8,128)(2,1)S(1)} %get-tuple-element.109), channel_id=1, source_target_pairs={{0,1},{1,2},{2,3},{3,11},{11,10},{10,9},{9,8},{8,0},{4,5},{5,6},{6... | collective-permute-start | bytes 884744 | tf_op jit(solution)/shard_map/ppermute | solution.py:509
  167.7 8.2 %collective-permute-start.28 = (bf16[128,1024]{1,0:T(8,128)(2,1)S(1)}, bf16[128,1024]{1,0:T(8,128)(2,1)S(1)}, u32[]{:S(2)}, u32[]{:S(2)}) collective-permute-start(bf16[128,1024]{1,0:T(8,128)(2,1)S(1)} %get-tuple-element.110), channel_id=1, source_target_pairs={{0,8},{1,0},{2,1},{3,2},{11,3},{10,11},{9,10},{8,9},{4,12},{5,4},{... | collective-permute-start | bytes 786440 | tf_op jit(solution)/shard_map/ppermute | solution.py:509
  176.3 10.2 %collective-permute-start.29 = (bf16[128,1152]{1,0:T(8,128)(2,1)S(1)}, bf16[128,1152]{1,0:T(8,128)(2,1)S(1)}, u32[]{:S(2)}, u32[]{:S(2)}) collective-permute-start(bf16[128,1152]{1,0:T(8,128)(2,1)S(1)} %get-tuple-element.116), channel_id=1, source_target_pairs={{0,1},{1,2},{2,3},{3,11},{11,10},{10,9},{9,8},{8,0},{4,5},{5,6},{6... | collective-permute-start | bytes 884744 | tf_op jit(solution)/shard_map/ppermute | solution.py:509
  177.7 8.8 %collective-permute-start.30 = (bf16[128,1024]{1,0:T(8,128)(2,1)S(1)}, bf16[128,1024]{1,0:T(8,128)(2,1)S(1)}, u32[]{:S(2)}, u32[]{:S(2)}) collective-permute-start(bf16[128,1024]{1,0:T(8,128)(2,1)S(1)} %get-tuple-element.117), channel_id=1, source_target_pairs={{0,8},{1,0},{2,1},{3,2},{11,3},{10,11},{9,10},{8,9},{4,12},{5,4},{... | collective-permute-start | bytes 786440 | tf_op jit(solution)/shard_map/ppermute | solution.py:509
  186.9 7.8 %collective-permute-start.31 = (bf16[128,1152]{1,0:T(8,128)(2,1)S(1)}, bf16[128,1152]{1,0:T(8,128)(2,1)S(1)}, u32[]{:S(2)}, u32[]{:S(2)}) collective-permute-start(bf16[128,1152]{1,0:T(8,128)(2,1)S(1)} %get-tuple-element.123), channel_id=1, source_target_pairs={{0,1},{1,2},{2,3},{3,11},{11,10},{10,9},{9,8},{8,0},{4,5},{5,6},{6... | collective-permute-start | bytes 884744 | tf_op jit(solution)/shard_map/ppermute | solution.py:509
  188.3 6.4 %collective-permute-start.32 = (bf16[128,1024]{1,0:T(8,128)(2,1)S(1)}, bf16[128,1024]{1,0:T(8,128)(2,1)S(1)}, u32[]{:S(2)}, u32[]{:S(2)}) collective-permute-start(bf16[128,1024]{1,0:T(8,128)(2,1)S(1)} %get-tuple-element.124), channel_id=1, source_target_pairs={{0,8},{1,0},{2,1},{3,2},{11,3},{10,11},{9,10},{8,9},{4,12},{5,4},{... | collective-permute-start | bytes 786440 | tf_op jit(solution)/shard_map/ppermute | solution.py:509
  (19 other events, 187.4 us)

commit v7 on v6

--- a/solution.py
+++ b/solution.py
@@ -40,12 +40,16 @@
 
 
 def place_kernel(pick_ref, *refs):
-    *held, out_ref = refs
-    for start in range(0, out_ref.shape[1], COLS):
+    count = pick_ref.shape[0]
+    held, outs = refs[: count * QUAD], refs[count * QUAD :]
+    for start in range(0, outs[0].shape[1], COLS):
         columns = slice(start, start + COLS)
-        values = jnp.concatenate([ref[:, columns] for ref in held], axis=0)
-        rows = jnp.dot(pick_ref[0], values, preferred_element_type=jnp.float32)
-        out_ref[:, columns] = rows.astype(jnp.bfloat16)
+        for quad, out_ref in enumerate(outs):
+            values = [ref[:, columns] for ref in held[quad * QUAD : (quad + 1) * QUAD]]
+            rows = jnp.dot(
+                pick_ref[quad], jnp.concatenate(values, axis=0), preferred_element_type=jnp.float32
+            )
+            out_ref[:, columns] = rows.astype(jnp.bfloat16)
 
 
 def in_block(shape, axis, quads, joint):
@@ -290,9 +294,12 @@
         circle = Ring(hidden, order)
         circle.step(1)
         offsets = np.array(arrivals(chips))
-        places = np.argsort(np.array(order))
-        spot = jnp.asarray(places, jnp.int32)[lax.axis_index(CHIPS)]
-        chip_of = jnp.asarray(np.array(order), jnp.int32)[(spot + offsets) % chips]
+
+        def turned(place):
+            line, spot = place // down, place % down
+            return line * down + jnp.where(line % 2 == 0, spot, down - 1 - spot)
+
+        chip_of = turned((turned(lax.axis_index(CHIPS)) + offsets + chips) % chips)
     else:
         held = gather_whole(hidden)
         offsets = np.arange(chips)
@@ -363,26 +370,35 @@
     x_rows = blocks * ROWS
     part = max(n for n in range(1, 17) if blocks % n == 0 and (n * ROWS) % 16 == 0)
     placed = []
-    for quad in range(quads):
-        if ring and quad == quads - 1:
-            circle.last((*placed[:-1], got_teacher, scale), placed[-1:])
+    runs = [[quad] for quad in range(quads)]
+    if ring and quads > 2:
+        runs = [list(range(quads - 2)), [quads - 2], [quads - 1]]
+    for run in runs:
+        if ring and run[-1] == quads - 1:
+            circle.last(placed[: len(runs[0])], (*placed[len(runs[0]) :], got_teacher, scale))
             held += [circle.got[int(offset)] for offset in offsets[len(held) :]]
-        two = held[quad * 2 : quad * 2 + 2]
-        operands = [chip[lane] for lane in range(2) for chip in two]
-        placed.append(
-            call(
-                place_kernel,
-                f"place_{quad}",
-                (blocks // part,),
-                [pl.BlockSpec((1, part * ROWS, QUAD * tokens), lambda s, q=quad: (q, s, 0))]
-                + [pl.BlockSpec(o.shape, lambda s: (0, 0), pipeline_mode=once) for o in operands],
-                pl.BlockSpec((part * ROWS, width), lambda s: (s, 0)),
-                jax.ShapeDtypeStruct((x_rows, width), jnp.bfloat16),
-                2 * x_rows * QUAD * tokens * width,
-                2 * x_rows * width * 2,
-                52,
-            )(pick, *operands)
-        )
+        operands = []
+        for quad in run:
+            two = held[quad * 2 : quad * 2 + 2]
+            operands += [chip[lane] for lane in range(2) for chip in two]
+        size = len(run)
+        placed += call(
+            place_kernel,
+            f"place_{run[0]}",
+            (blocks // part,),
+            [
+                pl.BlockSpec(
+                    (size, part * ROWS, QUAD * tokens),
+                    lambda s, q=run[0] // size: (q, s, 0),
+                )
+            ]
+            + [pl.BlockSpec(o.shape, lambda s: (0, 0), pipeline_mode=once) for o in operands],
+            [pl.BlockSpec((part * ROWS, width), lambda s: (s, 0))] * size,
+            [jax.ShapeDtypeStruct((x_rows, width), jnp.bfloat16)] * size,
+            2 * size * x_rows * QUAD * tokens * width,
+            2 * size * x_rows * width * 2,
+            52,
+        )(pick, *operands)
 
     lane_slots = turn * per_block
     slot_spec = pl.BlockSpec((lane_slots, BLOCK), lambda s: (s, 0))

time: 197 us -> 197 us (level)
  waiting for transfers between devices: 46.8 us -> 54.4 us
  Pallas kernels: 90 us -> 85.9 us
  local copies, waits for them, and re-layouts: 10.5 us -> 8.29 us
  starting transfers between devices: 36.9 us -> 34.7 us
    ppermute x6, waiting for transfers between devices: 23.5 us -> 32.5 us  [step(): lax.ppermute(shard, CHIPS, way)]
    pallas_call x4 -> x3, Pallas kernels: 22.6 us -> 18.5 us  [on_device(): call(place_kernel, f'place_{run[0]}', (blocks // part,), [pl.BlockSpec((s...]
  transfers between devices with their start and end apart: 34 -> 34, of which waited for: 16 -> 16; matrix products, arithmetic and copies ran while one was open for 9% -> 9% of each run, Pallas kernels for 23% -> 21%
where the time goes in v7:
time: 197 us; the launch traced here: 196 us
  Pallas kernels  85.9 us (44%)
  waiting for transfers between devices  54.4 us (28%)
  starting transfers between devices  34.7 us (18%)
  other arithmetic  8.7 us (4%)
  local copies, waits for them, and re-layouts  8.29 us (4%)
  matrix products  2.92 us (1%)
    pallas_call x1, Pallas kernels, on_device(): call(functools.partial(main_kernel, turn, steps, quads, ring), 'logits_an...  36.2 us
    ppermute x6, waiting for transfers between devices, step(): lax.ppermute(shard, CHIPS, way)  32.5 us
    pallas_call x7, Pallas kernels, fill(): call(functools.partial(head_kernel, turn, splits, shift, quads), f'head_g...  27.5 us
    ppermute x14, waiting for transfers between devices, on_device(): moved = lax.ppermute(sums[way], CHIPS, circle.ways[way])  18.5 us
    pallas_call x3, Pallas kernels, on_device(): call(place_kernel, f'place_{run[0]}', (blocks // part,), [pl.BlockSpec((s...  18.5 us
    ppermute x14, starting transfers between devices, on_device(): moved = lax.ppermute(sums[way], CHIPS, circle.ways[way])  14.6 us
    ppermute x6, starting transfers between devices, step(): lax.ppermute(shard, CHIPS, way)  10.6 us
    all_to_all x1, starting transfers between devices, on_device(): got = lax.all_to_all(sent, ALL, split_axis=0, concat_axis=0, tiled=True)  4.98 us
  transfers between devices with their start and end apart: 34, of which 16 were waited for; matrix products, arithmetic and copies ran while one was open for 9% of the time, Pallas kernels for 21%

profile of v7, /device:TPU:0, one launch (start us, length us, event | category | flops | bytes accessed | tf_op | source)
XLA Modules:
  0.0 196.5 jit_solution(5295157134536540961)
XLA Ops:
  0.6 3.0 %collective-permute-start.1 = (bf16[128,2048]{1,0:T(8,128)(2,1)}, bf16[128,2048]{1,0:T(8,128)(2,1)S(1)}, u32[]{:S(2)}, u32[]{:S(2)}) collective-permute-start(bf16[128,2048]{1,0:T(8,128)(2,1)} %refs_4_.1), channel_id=1, source_target_pairs={{0,8},{1,0},{2,1},{3,2},{11,3},{10,11},{9,10},{8,9},{4,12},{5,4},{... | collective-permute-start | bytes 1572872 | tf_op jit(solution)/shard_map/ppermute | solution.py:250
  6.1 1.6 select_reduce_fusion
  8.6 2.9 %fusion.4 = bf16[2816,128]{1,0:T(8,128)(2,1)} fusion(s32[1024]{0:T(1024)S(1)} %get-tuple-element.138, bf16[128,8,128]{2,1,0:T(8,128)(2,1)S(1)} %copy-done), kind=kOutput, calls=%fused_computation.11 | convolution fusion | flops 741441536 | bytes 987136 | tf_op jit(solution)/shard_map/dot_general | solution.py:320
  12.2 3.7 %collective-permute-done.1.refs_1_ = bf16[128,2048]{1,0:T(8,128)(2,1)S(1)} collective-permute-done((bf16[128,2048]{1,0:T(8,128)(2,1)}, bf16[128,2048]{1,0:T(8,128)(2,1)S(1)}, u32[]{:S(2)}, u32[]{:S(2)}) %collective-permute-start.1) | collective-permute-done | bytes 524320 | tf_op jit(solution)/shard_map/ppermute | solution.py:250
  17.2 5.0 %all-to-all-start = ((bf16[16,176,128]{2,1,0:T(8,128)(2,1)}), bf16[16,176,128]{2,1,0:T(8,128)(2,1)S(1)}, u32[]{:S(2)}, u32[]{:S(2)}) async-start(bf16[16,176,128]{2,1,0:T(8,128)(2,1)} %maximum_dynamic-update-slice_fusion), calls=%async_computation | async-start | bytes 1441792 | tf_op jit(solution)/shard_map/all_to_all | solution.py:348
  22.8 1.7 collective-permute-start.4
  25.7 20.5 %collective-permute-done.4.refs_5_ = bf16[128,2048]{1,0:T(8,128)(2,1)} collective-permute-done((bf16[128,2048]{1,0:T(8,128)(2,1)S(1)}, bf16[128,2048]{1,0:T(8,128)(2,1)}, u32[]{:S(2)}, u32[]{:S(2)}) %collective-permute-start.4) | collective-permute-done | bytes 524320 | tf_op jit(solution)/shard_map/ppermute | solution.py:250
  48.9 1.8 fusion.2.pick_ref
  50.7 5.3 %collective-permute-start.8 = (bf16[128,2048]{1,0:T(8,128)(2,1)}, bf16[128,2048]{1,0:T(8,128)(2,1)S(1)}, u32[]{:S(2)}, u32[]{:S(2)}) collective-permute-start(bf16[128,2048]{1,0:T(8,128)(2,1)} %collective-permute-done.4.refs_5_), channel_id=1, source_target_pairs={{0,1},{1,2},{2,3},{3,11},{11,10},{10,9},{9,8},{8,0},{4,5},{5,6},{6... | collective-permute-start | bytes 1572872 | tf_op jit(solution)/shard_map/ppermute | solution.py:250
  56.3 7.6 %place_0.1 = (bf16[640,2048]{1,0:T(8,128)(2,1)}, bf16[640,2048]{1,0:T(8,128)(2,1)}) custom-call(bf16[4,640,512]{2,1,0:T(8,128)(2,1)} %fusion.2.pick_ref, bf16[128,2048]{1,0:T(8,128)(2,1)S(1)} %collective-permute-done.refs_0_, bf16[128,2048]{1,0:T(8,128)(2,1)S(1)} %collective-permute-done.1.refs_1_, bf16[128,2048]{1,0:T(8,128)(2,1)} %collective-permute-done.2.refs_2_, ...), custom_call_target="tpu_custom_call" | custom-call | flops 2684354560 | bytes 10485760 | tf_op jit(solution)/shard_map/place_0/pallas_call | solution.py:385
  63.9 4.3 %collective-permute-done.8.refs_1_ = bf16[128,2048]{1,0:T(8,128)(2,1)S(1)} collective-permute-done((bf16[128,2048]{1,0:T(8,128)(2,1)}, bf16[128,2048]{1,0:T(8,128)(2,1)S(1)}, u32[]{:S(2)}, u32[]{:S(2)}) %collective-permute-start.8) | collective-permute-done | bytes 524320 | tf_op jit(solution)/shard_map/ppermute | solution.py:250
  68.2 2.7 %collective-permute-done.11.refs_0_ = bf16[128,2048]{1,0:T(8,128)(2,1)S(1)} collective-permute-done((bf16[128,2048]{1,0:T(8,128)(2,1)S(1)}, bf16[128,2048]{1,0:T(8,128)(2,1)S(1)}, u32[]{:S(2)}, u32[]{:S(2)}) %collective-permute-start.11) | collective-permute-done | bytes 524320 | tf_op jit(solution)/shard_map/ppermute | solution.py:250
  71.8 1.7 collective-permute-start.12
  77.3 5.5 %place_2.1.refs_2_ = bf16[640,2048]{1,0:T(8,128)(2,1)} custom-call(bf16[4,640,512]{2,1,0:T(8,128)(2,1)} %fusion.2.pick_ref, bf16[128,2048]{1,0:T(8,128)(2,1)S(1)} %collective-permute-done.7.refs_0_, bf16[128,2048]{1,0:T(8,128)(2,1)S(1)} %collective-permute-done.8.refs_1_, bf16[128,2048]{1,0:T(8,128)(2,1)S(1)} %collective-permute-done.9.refs_2_, ...), custom_call_target="tpu_custom_call" | custom-call | flops 1342177280 | bytes 5242880 | tf_op jit(solution)/shard_map/place_2/pallas_call | solution.py:385
  85.5 5.4 %place_3.1.refs_3_ = bf16[640,2048]{1,0:T(8,128)(2,1)} custom-call(bf16[4,640,512]{2,1,0:T(8,128)(2,1)} %fusion.2.pick_ref, bf16[128,2048]{1,0:T(8,128)(2,1)S(1)} %collective-permute-done.11.refs_0_, bf16[128,2048]{1,0:T(8,128)(2,1)S(1)} %collective-permute-done.12.refs_1_, bf16[128,2048]{1,0:T(8,128)(2,1)S(1)} %collective-permute-done.13.refs_2_, ...), custom_call_target="tpu_custom_call" | custom-call | flops 1342177280 | bytes 5242880 | tf_op jit(solution)/shard_map/place_3/pallas_call | solution.py:385
  90.9 36.2 %logits_and_back.1 = (bf16[128,2560]{1,0:T(8,128)(2,1)S(1)}, bf16[256,2176]{1,0:T(8,128)(2,1)}, bf16[256,2176]{1,0:T(8,128)(2,1)}, bf16[256,2176]{1,0:T(8,128)(2...) custom-call(f32[1]{0:T(128)} %bitcast.5.scale_ref, ...), custom_call_target="tpu_custom_call" | custom-call | flops 21474836480 | bytes 52428800 | tf_op jit(solution)/shard_map/logits_and_back/pallas_call | solution.py:426
  128.2 1.9 collective-permute-done.16
  133.9 2.8 %head_grad_0.1 = (bf16[10240,2048]{1,0:T(8,128)(2,1)}, f32[8,128]{1,0:T(8,128)}) custom-call(bf16[128,2560]{1,0:T(8,128)(2,1)S(1)} %get-tuple-element.129.grad_ref, bf16[640,2048]{1,0:T(8,128)(2,1)S(1)} %copy-done.4, bf16[640,2048]{1,0:T(8,128)(2,1)S(1)} %copy-done.5, bf16[640,2048]{1,0:T(8,128)(2,1)S(1)} %copy-done.2, bf16[640,2048]{1,0:T(8,128)(2,1)S(1)} %copy-done.3), custom_call_target="tpu_custom_call" | custom-call | flops 1533916928 | bytes 7489828 | tf_op jit(solution)/shard_map/head_grad_0/pallas_call | solution.py:487
  136.7 3.7 %collective-permute-done.20.refs_7_ = bf16[128,1024]{1,0:T(8,128)(2,1)S(1)} collective-permute-done((bf16[128,1024]{1,0:T(8,128)(2,1)S(1)}, bf16[128,1024]{1,0:T(8,128)(2,1)S(1)}, u32[]{:S(2)}, u32[]{:S(2)}) %collective-permute-start.20) | collective-permute-done | bytes 262176 | tf_op jit(solution)/shard_map/ppermute | solution.py:525
  143.5 4.1 %head_grad_1.1 = (bf16[10240,2048]{1,0:T(8,128)(2,1)}, f32[8,128]{1,0:T(8,128)}) custom-call(bf16[128,2560]{1,0:T(8,128)(2,1)S(1)} %get-tuple-element.129.grad_ref, bf16[640,2048]{1,0:T(8,128)(2,1)S(1)} %copy-done.4, bf16[640,2048]{1,0:T(8,128)(2,1)S(1)} %copy-done.5, bf16[640,2048]{1,0:T(8,128)(2,1)S(1)} %copy-done.2, ...), custom_call_target="tpu_custom_call", output_to_operand_aliasing={{0}: (5, {})} | custom-call | flops 1533916928 | bytes 7489828 | tf_op jit(solution)/shard_map/head_grad_1/pallas_call | solution.py:487
  147.6 2.0 %collective-permute-done.22.refs_7_ = bf16[128,1024]{1,0:T(8,128)(2,1)S(1)} collective-permute-done((bf16[128,1024]{1,0:T(8,128)(2,1)S(1)}, bf16[128,1024]{1,0:T(8,128)(2,1)S(1)}, u32[]{:S(2)}, u32[]{:S(2)}) %collective-permute-start.22) | collective-permute-done | bytes 262176 | tf_op jit(solution)/shard_map/ppermute | solution.py:525
  152.4 4.1 %head_grad_2.1 = (bf16[10240,2048]{1,0:T(8,128)(2,1)}, f32[8,128]{1,0:T(8,128)}) custom-call(bf16[128,2560]{1,0:T(8,128)(2,1)S(1)} %get-tuple-element.129.grad_ref, bf16[640,2048]{1,0:T(8,128)(2,1)S(1)} %copy-done.4, bf16[640,2048]{1,0:T(8,128)(2,1)S(1)} %copy-done.5, bf16[640,2048]{1,0:T(8,128)(2,1)S(1)} %copy-done.2, ...), custom_call_target="tpu_custom_call", output_to_operand_aliasing={{0}: (5, {})} | custom-call | flops 1533916928 | bytes 7489828 | tf_op jit(solution)/shard_map/head_grad_2/pallas_call | solution.py:487
  158.3 1.8 collective-permute-start.25
  160.4 4.1 %head_grad_3.1 = (bf16[10240,2048]{1,0:T(8,128)(2,1)}, f32[8,128]{1,0:T(8,128)}) custom-call(bf16[128,2560]{1,0:T(8,128)(2,1)S(1)} %get-tuple-element.129.grad_ref, bf16[640,2048]{1,0:T(8,128)(2,1)S(1)} %copy-done.4, bf16[640,2048]{1,0:T(8,128)(2,1)S(1)} %copy-done.5, bf16[640,2048]{1,0:T(8,128)(2,1)S(1)} %copy-done.2, ...), custom_call_target="tpu_custom_call", output_to_operand_aliasing={{0}: (5, {})} | custom-call | flops 1533916928 | bytes 7489828 | tf_op jit(solution)/shard_map/head_grad_3/pallas_call | solution.py:487
  164.5 1.9 collective-permute-done.26.refs_7_
  168.9 4.1 %head_grad_4.1 = (bf16[10240,2048]{1,0:T(8,128)(2,1)}, f32[8,128]{1,0:T(8,128)}) custom-call(bf16[128,2560]{1,0:T(8,128)(2,1)S(1)} %get-tuple-element.129.grad_ref, bf16[640,2048]{1,0:T(8,128)(2,1)S(1)} %copy-done.4, bf16[640,2048]{1,0:T(8,128)(2,1)S(1)} %copy-done.5, bf16[640,2048]{1,0:T(8,128)(2,1)S(1)} %copy-done.2, ...), custom_call_target="tpu_custom_call", output_to_operand_aliasing={{0}: (5, {})} | custom-call | flops 1533916928 | bytes 7489828 | tf_op jit(solution)/shard_map/head_grad_4/pallas_call | solution.py:487
  173.0 2.7 %collective-permute-done.28.refs_7_ = bf16[128,1024]{1,0:T(8,128)(2,1)S(1)} collective-permute-done((bf16[128,1024]{1,0:T(8,128)(2,1)S(1)}, bf16[128,1024]{1,0:T(8,128)(2,1)S(1)}, u32[]{:S(2)}, u32[]{:S(2)}) %collective-permute-start.28) | collective-permute-done | bytes 262176 | tf_op jit(solution)/shard_map/ppermute | solution.py:525
  178.1 4.1 %head_grad_5.1 = (bf16[10240,2048]{1,0:T(8,128)(2,1)}, f32[8,128]{1,0:T(8,128)}) custom-call(bf16[128,2560]{1,0:T(8,128)(2,1)S(1)} %get-tuple-element.129.grad_ref, bf16[640,2048]{1,0:T(8,128)(2,1)S(1)} %copy-done.4, bf16[640,2048]{1,0:T(8,128)(2,1)S(1)} %copy-done.5, bf16[640,2048]{1,0:T(8,128)(2,1)S(1)} %copy-done.2, ...), custom_call_target="tpu_custom_call", output_to_operand_aliasing={{0}: (5, {})} | custom-call | flops 1533916928 | bytes 7489828 | tf_op jit(solution)/shard_map/head_grad_5/pallas_call | solution.py:487
  182.2 3.8 %collective-permute-done.30.refs_7_ = bf16[128,1024]{1,0:T(8,128)(2,1)S(1)} collective-permute-done((bf16[128,1024]{1,0:T(8,128)(2,1)S(1)}, bf16[128,1024]{1,0:T(8,128)(2,1)S(1)}, u32[]{:S(2)}, u32[]{:S(2)}) %collective-permute-start.30) | collective-permute-done | bytes 262176 | tf_op jit(solution)/shard_map/ppermute | solution.py:525
  186.4 2.0 collective-permute-start.31
  188.5 4.1 %head_grad_6.1 = (bf16[10240,2048]{1,0:T(8,128)(2,1)}, f32[8,128]{1,0:T(8,128)}) custom-call(bf16[128,2560]{1,0:T(8,128)(2,1)S(1)} %get-tuple-element.129.grad_ref, bf16[640,2048]{1,0:T(8,128)(2,1)S(1)} %copy-done.4, bf16[640,2048]{1,0:T(8,128)(2,1)S(1)} %copy-done.5, bf16[640,2048]{1,0:T(8,128)(2,1)S(1)} %copy-done.2, ...), custom_call_target="tpu_custom_call", output_to_operand_aliasing={{0}: (5, {})} | custom-call | flops 1533916928 | bytes 7489828 | tf_op jit(solution)/shard_map/head_grad_6/pallas_call | solution.py:487
  192.6 2.1 %collective-permute-done.32.refs_7_ = bf16[128,1024]{1,0:T(8,128)(2,1)S(1)} collective-permute-done((bf16[128,1024]{1,0:T(8,128)(2,1)S(1)}, bf16[128,1024]{1,0:T(8,128)(2,1)S(1)}, u32[]{:S(2)}, u32[]{:S(2)}) %collective-permute-start.32) | collective-permute-done | bytes 262176 | tf_op jit(solution)/shard_map/ppermute | solution.py:525
  (123 shorter events, 36.6 us)
Async XLA Ops:
  0.6 15.2 %collective-permute-start.1 = (bf16[128,2048]{1,0:T(8,128)(2,1)}, bf16[128,2048]{1,0:T(8,128)(2,1)S(1)}, u32[]{:S(2)}, u32[]{:S(2)}) collective-permute-start(bf16[128,2048]{1,0:T(8,128)(2,1)} %refs_4_.1), channel_id=1, source_target_pairs={{0,8},{1,0},{2,1},{3,2},{11,3},{10,11},{9,10},{8,9},{4,12},{5,4},{... | collective-permute-start | bytes 1572872 | tf_op jit(solution)/shard_map/ppermute | solution.py:250
  3.6 13.6 %collective-permute-start = (bf16[128,2048]{1,0:T(8,128)(2,1)}, bf16[128,2048]{1,0:T(8,128)(2,1)S(1)}, u32[]{:S(2)}, u32[]{:S(2)}) collective-permute-start(bf16[128,2048]{1,0:T(8,128)(2,1)} %refs_4_.1), channel_id=1, source_target_pairs={{0,1},{1,2},{2,3},{3,11},{11,10},{10,9},{9,8},{8,0},{4,5},{5,6},{6... | collective-permute-start | bytes 1572872 | tf_op jit(solution)/shard_map/ppermute | solution.py:250
  17.2 28.9 %all-to-all-start = ((bf16[16,176,128]{2,1,0:T(8,128)(2,1)}), bf16[16,176,128]{2,1,0:T(8,128)(2,1)S(1)}, u32[]{:S(2)}, u32[]{:S(2)}) async-start(bf16[16,176,128]{2,1,0:T(8,128)(2,1)} %maximum_dynamic-update-slice_fusion), calls=%async_computation | async-start | bytes 1441792 | tf_op jit(solution)/shard_map/all_to_all | solution.py:348
  22.2 33.9 %collective-permute-start.5 = (bf16[128,2048]{1,0:T(8,128)(2,1)}, bf16[128,2048]{1,0:T(8,128)(2,1)}, u32[]{:S(2)}, u32[]{:S(2)}) collective-permute-start(bf16[128,2048]{1,0:T(8,128)(2,1)} %refs_4_.1), channel_id=1, source_target_pairs={{0,4},{4,0},{1,5},{5,1},{2,6},{6,2},{3,7},{7,3},{8,12},{12,8},{9,1... | collective-permute-start | bytes 1572872 | tf_op jit(solution)/shard_map/ppermute | solution.py:245
  22.8 23.3 %collective-permute-start.4 = (bf16[128,2048]{1,0:T(8,128)(2,1)S(1)}, bf16[128,2048]{1,0:T(8,128)(2,1)}, u32[]{:S(2)}, u32[]{:S(2)}) collective-permute-start(bf16[128,2048]{1,0:T(8,128)(2,1)S(1)} %collective-permute-done.refs_0_), channel_id=1, source_target_pairs={{0,1},{1,2},{2,3},{3,11},{11,10},{10,9},{9,8},{8,0},{4,5},{5,6},{6... | collective-permute-start | bytes 1572872 | tf_op jit(solution)/shard_map/ppermute | solution.py:250
  24.8 26.0 %collective-permute-start.7 = (bf16[128,2048]{1,0:T(8,128)(2,1)S(1)}, bf16[128,2048]{1,0:T(8,128)(2,1)S(1)}, u32[]{:S(2)}, u32[]{:S(2)}) collective-permute-start(bf16[128,2048]{1,0:T(8,128)(2,1)S(1)} %collective-permute-done.1.refs_1_), channel_id=1, source_target_pairs={{0,8},{1,0},{2,1},{3,2},{11,3},{10,11},{9,10},{8,9},{4,12},{5,4},{... | collective-permute-start | bytes 1572872 | tf_op jit(solution)/shard_map/ppermute | solution.py:250
  25.2 30.9 %collective-permute-start.3 = (bf16[128,2048]{1,0:T(8,128)(2,1)S(1)}, bf16[128,2048]{1,0:T(8,128)(2,1)}, u32[]{:S(2)}, u32[]{:S(2)}) collective-permute-start(bf16[128,2048]{1,0:T(8,128)(2,1)S(1)} %collective-permute-done.1.refs_1_), channel_id=1, source_target_pairs={{0,4},{4,0},{1,5},{5,1},{2,6},{6,2},{3,7},{7,3},{8,12},{12,8},{9,1... | collective-permute-start | bytes 1572872 | tf_op jit(solution)/shard_map/ppermute | solution.py:245
  25.2 31.2 %collective-permute-start.2 = (bf16[128,2048]{1,0:T(8,128)(2,1)S(1)}, bf16[128,2048]{1,0:T(8,128)(2,1)}, u32[]{:S(2)}, u32[]{:S(2)}) collective-permute-start(bf16[128,2048]{1,0:T(8,128)(2,1)S(1)} %collective-permute-done.refs_0_), channel_id=1, source_target_pairs={{0,4},{4,0},{1,5},{5,1},{2,6},{6,2},{3,7},{7,3},{8,12},{12,8},{9,1... | collective-permute-start | bytes 1572872 | tf_op jit(solution)/shard_map/ppermute | solution.py:245
  46.1 10.2 %collective-permute-start.6 = (bf16[128,2048]{1,0:T(8,128)(2,1)}, bf16[128,2048]{1,0:T(8,128)(2,1)}, u32[]{:S(2)}, u32[]{:S(2)}) collective-permute-start(bf16[128,2048]{1,0:T(8,128)(2,1)} %collective-permute-done.4.refs_5_), channel_id=1, source_target_pairs={{0,4},{4,0},{1,5},{5,1},{2,6},{6,2},{3,7},{7,3},{8,12},{12,8},{9,1... | collective-permute-start | bytes 1572872 | tf_op jit(solution)/shard_map/ppermute | solution.py:245
  50.7 17.5 %collective-permute-start.8 = (bf16[128,2048]{1,0:T(8,128)(2,1)}, bf16[128,2048]{1,0:T(8,128)(2,1)S(1)}, u32[]{:S(2)}, u32[]{:S(2)}) collective-permute-start(bf16[128,2048]{1,0:T(8,128)(2,1)} %collective-permute-done.4.refs_5_), channel_id=1, source_target_pairs={{0,1},{1,2},{2,3},{3,11},{11,10},{10,9},{9,8},{8,0},{4,5},{5,6},{6... | collective-permute-start | bytes 1572872 | tf_op jit(solution)/shard_map/ppermute | solution.py:250
  56.1 14.8 %collective-permute-start.11 = (bf16[128,2048]{1,0:T(8,128)(2,1)S(1)}, bf16[128,2048]{1,0:T(8,128)(2,1)S(1)}, u32[]{:S(2)}, u32[]{:S(2)}) collective-permute-start(bf16[128,2048]{1,0:T(8,128)(2,1)S(1)} %collective-permute-done.7.refs_0_), channel_id=1, source_target_pairs={{0,8},{1,0},{2,1},{3,2},{11,3},{10,11},{9,10},{8,9},{4,12},{5,4},{... | collective-permute-start | bytes 1572872 | tf_op jit(solution)/shard_map/ppermute | solution.py:250
  56.1 21.2 %collective-permute-start.9 = (bf16[128,2048]{1,0:T(8,128)(2,1)S(1)}, bf16[128,2048]{1,0:T(8,128)(2,1)S(1)}, u32[]{:S(2)}, u32[]{:S(2)}) collective-permute-start(bf16[128,2048]{1,0:T(8,128)(2,1)S(1)} %collective-permute-done.7.refs_0_), channel_id=1, source_target_pairs={{0,4},{4,0},{1,5},{5,1},{2,6},{6,2},{3,7},{7,3},{8,12},{12,8},{9,1... | collective-permute-start | bytes 1572872 | tf_op jit(solution)/shard_map/ppermute | solution.py:245
  68.2 9.1 %collective-permute-start.10 = (bf16[128,2048]{1,0:T(8,128)(2,1)S(1)}, bf16[128,2048]{1,0:T(8,128)(2,1)}, u32[]{:S(2)}, u32[]{:S(2)}) collective-permute-start(bf16[128,2048]{1,0:T(8,128)(2,1)S(1)} %collective-permute-done.8.refs_1_), channel_id=1, source_target_pairs={{0,4},{4,0},{1,5},{5,1},{2,6},{6,2},{3,7},{7,3},{8,12},{12,8},{9,1... | collective-permute-start | bytes 1572872 | tf_op jit(solution)/shard_map/ppermute | solution.py:245
  71.8 11.0 %collective-permute-start.12 = (bf16[128,2048]{1,0:T(8,128)(2,1)}, bf16[128,2048]{1,0:T(8,128)(2,1)S(1)}, u32[]{:S(2)}, u32[]{:S(2)}) collective-permute-start(bf16[128,2048]{1,0:T(8,128)(2,1)} %broadcast_select_fusion), channel_id=1, source_target_pairs={{0,1},{1,2},{2,3},{3,11},{11,10},{10,9},{9,8},{8,0},{4,12},{5,4},{... | collective-permute-start | bytes 1572872 | tf_op jit(solution)/shard_map/ppermute | solution.py:265
  77.1 6.1 %collective-permute-start.13 = (bf16[128,2048]{1,0:T(8,128)(2,1)S(1)}, bf16[128,2048]{1,0:T(8,128)(2,1)S(1)}, u32[]{:S(2)}, u32[]{:S(2)}) collective-permute-start(bf16[128,2048]{1,0:T(8,128)(2,1)S(1)} %collective-permute-done.11.refs_0_), channel_id=1, source_target_pairs={{0,4},{4,0},{1,5},{5,1},{2,6},{6,2},{3,7},{7,3},{8,12},{12,8},{9,1... | collective-permute-start | bytes 1572872 | tf_op jit(solution)/shard_map/ppermute | solution.py:245
  127.5 13.5 %collective-permute-start.15 = (bf16[256,2176]{1,0:T(8,128)(2,1)}, bf16[256,2176]{1,0:T(8,128)(2,1)S(1)}, u32[]{:S(2)}, u32[]{:S(2)}) collective-permute-start(bf16[256,2176]{1,0:T(8,128)(2,1)} %get-tuple-element.78), channel_id=1, source_target_pairs={{0,4},{4,0},{1,5},{5,1},{2,6},{6,2},{3,7},{7,3},{8,12},{12,8},{9,1... | collective-permute-start | bytes 3342344 | tf_op jit(solution)/shard_map/ppermute | solution.py:466
  127.7 13.3 %collective-permute-start.17 = (bf16[256,2176]{1,0:T(8,128)(2,1)}, bf16[256,2176]{1,0:T(8,128)(2,1)S(1)}, u32[]{:S(2)}, u32[]{:S(2)}) collective-permute-start(bf16[256,2176]{1,0:T(8,128)(2,1)} %get-tuple-element.82), channel_id=1, source_target_pairs={{0,4},{4,0},{1,5},{5,1},{2,6},{6,2},{3,7},{7,3},{8,12},{12,8},{9,1... | collective-permute-start | bytes 3342344 | tf_op jit(solution)/shard_map/ppermute | solution.py:466
  128.0 21.9 %collective-permute-start.18 = (bf16[256,2176]{1,0:T(8,128)(2,1)}, bf16[256,2176]{1,0:T(8,128)(2,1)S(1)}, u32[]{:S(2)}, u32[]{:S(2)}) collective-permute-start(bf16[256,2176]{1,0:T(8,128)(2,1)} %get-tuple-element.84), channel_id=1, source_target_pairs={{0,4},{4,0},{1,5},{5,1},{2,6},{6,2},{3,7},{7,3},{8,12},{12,8},{9,1... | collective-permute-start | bytes 3342344 | tf_op jit(solution)/shard_map/ppermute | solution.py:466
  131.6 9.3 %collective-permute-start.19 = (bf16[128,1152]{1,0:T(8,128)(2,1)S(1)}, bf16[128,1152]{1,0:T(8,128)(2,1)S(1)}, u32[]{:S(2)}, u32[]{:S(2)}) collective-permute-start(bf16[128,1152]{1,0:T(8,128)(2,1)S(1)} %get-tuple-element.85), channel_id=1, source_target_pairs={{0,1},{1,2},{2,3},{3,11},{11,10},{10,9},{9,8},{8,0},{4,5},{5,6},{6... | collective-permute-start | bytes 884744 | tf_op jit(solution)/shard_map/ppermute | solution.py:525
  132.2 8.3 %collective-permute-start.20 = (bf16[128,1024]{1,0:T(8,128)(2,1)S(1)}, bf16[128,1024]{1,0:T(8,128)(2,1)S(1)}, u32[]{:S(2)}, u32[]{:S(2)}) collective-permute-start(bf16[128,1024]{1,0:T(8,128)(2,1)S(1)} %get-tuple-element.87), channel_id=1, source_target_pairs={{0,8},{1,0},{2,1},{3,2},{11,3},{10,11},{9,10},{8,9},{4,12},{5,4},{... | collective-permute-start | bytes 786440 | tf_op jit(solution)/shard_map/ppermute | solution.py:525
  141.4 8.5 %collective-permute-start.21 = (bf16[128,1152]{1,0:T(8,128)(2,1)S(1)}, bf16[128,1152]{1,0:T(8,128)(2,1)S(1)}, u32[]{:S(2)}, u32[]{:S(2)}) collective-permute-start(bf16[128,1152]{1,0:T(8,128)(2,1)S(1)} %get-tuple-element.92), channel_id=1, source_target_pairs={{0,1},{1,2},{2,3},{3,11},{11,10},{10,9},{9,8},{8,0},{4,5},{5,6},{6... | collective-permute-start | bytes 884744 | tf_op jit(solution)/shard_map/ppermute | solution.py:525
  142.1 7.5 %collective-permute-start.22 = (bf16[128,1024]{1,0:T(8,128)(2,1)S(1)}, bf16[128,1024]{1,0:T(8,128)(2,1)S(1)}, u32[]{:S(2)}, u32[]{:S(2)}) collective-permute-start(bf16[128,1024]{1,0:T(8,128)(2,1)S(1)} %get-tuple-element.93), channel_id=1, source_target_pairs={{0,8},{1,0},{2,1},{3,2},{11,3},{10,11},{9,10},{8,9},{4,12},{5,4},{... | collective-permute-start | bytes 786440 | tf_op jit(solution)/shard_map/ppermute | solution.py:525
  150.3 7.6 %collective-permute-start.23 = (bf16[128,1152]{1,0:T(8,128)(2,1)S(1)}, bf16[128,1152]{1,0:T(8,128)(2,1)S(1)}, u32[]{:S(2)}, u32[]{:S(2)}) collective-permute-start(bf16[128,1152]{1,0:T(8,128)(2,1)S(1)} %get-tuple-element.99), channel_id=1, source_target_pairs={{0,1},{1,2},{2,3},{3,11},{11,10},{10,9},{9,8},{8,0},{4,5},{5,6},{6... | collective-permute-start | bytes 884744 | tf_op jit(solution)/shard_map/ppermute | solution.py:525
  151.5 6.4 %collective-permute-start.24 = (bf16[128,1024]{1,0:T(8,128)(2,1)S(1)}, bf16[128,1024]{1,0:T(8,128)(2,1)S(1)}, u32[]{:S(2)}, u32[]{:S(2)}) collective-permute-start(bf16[128,1024]{1,0:T(8,128)(2,1)S(1)} %get-tuple-element.100), channel_id=1, source_target_pairs={{0,8},{1,0},{2,1},{3,2},{11,3},{10,11},{9,10},{8,9},{4,12},{5,4},{... | collective-permute-start | bytes 786440 | tf_op jit(solution)/shard_map/ppermute | solution.py:525
  158.3 8.1 %collective-permute-start.25 = (bf16[128,1152]{1,0:T(8,128)(2,1)S(1)}, bf16[128,1152]{1,0:T(8,128)(2,1)S(1)}, u32[]{:S(2)}, u32[]{:S(2)}) collective-permute-start(bf16[128,1152]{1,0:T(8,128)(2,1)S(1)} %get-tuple-element.106), channel_id=1, source_target_pairs={{0,1},{1,2},{2,3},{3,11},{11,10},{10,9},{9,8},{8,0},{4,5},{5,6},{6... | collective-permute-start | bytes 884744 | tf_op jit(solution)/shard_map/ppermute | solution.py:525
  160.0 6.4 %collective-permute-start.26 = (bf16[128,1024]{1,0:T(8,128)(2,1)S(1)}, bf16[128,1024]{1,0:T(8,128)(2,1)S(1)}, u32[]{:S(2)}, u32[]{:S(2)}) collective-permute-start(bf16[128,1024]{1,0:T(8,128)(2,1)S(1)} %get-tuple-element.107), channel_id=1, source_target_pairs={{0,8},{1,0},{2,1},{3,2},{11,3},{10,11},{9,10},{8,9},{4,12},{5,4},{... | collective-permute-start | bytes 786440 | tf_op jit(solution)/shard_map/ppermute | solution.py:525
  166.8 8.8 %collective-permute-start.27 = (bf16[128,1152]{1,0:T(8,128)(2,1)S(1)}, bf16[128,1152]{1,0:T(8,128)(2,1)S(1)}, u32[]{:S(2)}, u32[]{:S(2)}) collective-permute-start(bf16[128,1152]{1,0:T(8,128)(2,1)S(1)} %get-tuple-element.113), channel_id=1, source_target_pairs={{0,1},{1,2},{2,3},{3,11},{11,10},{10,9},{9,8},{8,0},{4,5},{5,6},{6... | collective-permute-start | bytes 884744 | tf_op jit(solution)/shard_map/ppermute | solution.py:525
  168.1 7.5 %collective-permute-start.28 = (bf16[128,1024]{1,0:T(8,128)(2,1)S(1)}, bf16[128,1024]{1,0:T(8,128)(2,1)S(1)}, u32[]{:S(2)}, u32[]{:S(2)}) collective-permute-start(bf16[128,1024]{1,0:T(8,128)(2,1)S(1)} %get-tuple-element.114), channel_id=1, source_target_pairs={{0,8},{1,0},{2,1},{3,2},{11,3},{10,11},{9,10},{8,9},{4,12},{5,4},{... | collective-permute-start | bytes 786440 | tf_op jit(solution)/shard_map/ppermute | solution.py:525
  176.0 10.0 %collective-permute-start.29 = (bf16[128,1152]{1,0:T(8,128)(2,1)S(1)}, bf16[128,1152]{1,0:T(8,128)(2,1)S(1)}, u32[]{:S(2)}, u32[]{:S(2)}) collective-permute-start(bf16[128,1152]{1,0:T(8,128)(2,1)S(1)} %get-tuple-element.120), channel_id=1, source_target_pairs={{0,1},{1,2},{2,3},{3,11},{11,10},{10,9},{9,8},{8,0},{4,5},{5,6},{6... | collective-permute-start | bytes 884744 | tf_op jit(solution)/shard_map/ppermute | solution.py:525
  177.2 8.8 %collective-permute-start.30 = (bf16[128,1024]{1,0:T(8,128)(2,1)S(1)}, bf16[128,1024]{1,0:T(8,128)(2,1)S(1)}, u32[]{:S(2)}, u32[]{:S(2)}) collective-permute-start(bf16[128,1024]{1,0:T(8,128)(2,1)S(1)} %get-tuple-element.121), channel_id=1, source_target_pairs={{0,8},{1,0},{2,1},{3,2},{11,3},{10,11},{9,10},{8,9},{4,12},{5,4},{... | collective-permute-start | bytes 786440 | tf_op jit(solution)/shard_map/ppermute | solution.py:525
  186.4 8.3 %collective-permute-start.31 = (bf16[128,1152]{1,0:T(8,128)(2,1)S(1)}, bf16[128,1152]{1,0:T(8,128)(2,1)S(1)}, u32[]{:S(2)}, u32[]{:S(2)}) collective-permute-start(bf16[128,1152]{1,0:T(8,128)(2,1)S(1)} %get-tuple-element.127), channel_id=1, source_target_pairs={{0,1},{1,2},{2,3},{3,11},{11,10},{10,9},{9,8},{8,0},{4,5},{5,6},{6... | collective-permute-start | bytes 884744 | tf_op jit(solution)/shard_map/ppermute | solution.py:525
  188.4 6.4 %collective-permute-start.32 = (bf16[128,1024]{1,0:T(8,128)(2,1)S(1)}, bf16[128,1024]{1,0:T(8,128)(2,1)S(1)}, u32[]{:S(2)}, u32[]{:S(2)}) collective-permute-start(bf16[128,1024]{1,0:T(8,128)(2,1)S(1)} %get-tuple-element.128), channel_id=1, source_target_pairs={{0,8},{1,0},{2,1},{3,2},{11,3},{10,11},{9,10},{8,9},{4,12},{5,4},{... | collective-permute-start | bytes 786440 | tf_op jit(solution)/shard_map/ppermute | solution.py:525
  (16 other events, 173.5 us)

commit v8 on v7

--- a/solution.py
+++ b/solution.py
@@ -375,7 +375,8 @@
         runs = [list(range(quads - 2)), [quads - 2], [quads - 1]]
     for run in runs:
         if ring and run[-1] == quads - 1:
-            circle.last(placed[: len(runs[0])], (*placed[len(runs[0]) :], got_teacher, scale))
+            first = len(runs[0])
+            circle.last((*placed[:first], got_teacher, scale), placed[first:])
             held += [circle.got[int(offset)] for offset in offsets[len(held) :]]
         operands = []
         for quad in run:

time: 197 us -> 193 us (0.980)
  waiting for transfers between devices: 54.4 us -> 51 us
    ppermute x6, waiting for transfers between devices: 32.5 us -> 27.3 us  [step(): lax.ppermute(shard, CHIPS, way)]
  transfers between devices with their start and end apart: 34 -> 34, of which waited for: 16 -> 14; matrix products, arithmetic and copies ran while one was open for 9% -> 8% of each run, Pallas kernels for 21% -> 21%
where the time goes in v8:
time: 193 us
  Pallas kernels  86 us (45%)
  waiting for transfers between devices  51 us (26%)
  starting transfers between devices  34.8 us (18%)
  local copies, waits for them, and re-layouts  9.35 us (5%)
  other arithmetic  7.06 us (4%)
  matrix products  2.92 us (2%)
    pallas_call x1, Pallas kernels, on_device(): call(functools.partial(main_kernel, turn, steps, quads, ring), 'logits_an...  36.2 us
    pallas_call x7, Pallas kernels, fill(): call(functools.partial(head_kernel, turn, splits, shift, quads), f'head_g...  27.6 us
    ppermute x6, waiting for transfers between devices, step(): lax.ppermute(shard, CHIPS, way)  27.3 us
    ppermute x14, waiting for transfers between devices, on_device(): moved = lax.ppermute(sums[way], CHIPS, circle.ways[way])  18.7 us
    pallas_call x3, Pallas kernels, on_device(): call(place_kernel, f'place_{run[0]}', (blocks // part,), [pl.BlockSpec((s...  18.5 us
    ppermute x14, starting transfers between devices, on_device(): moved = lax.ppermute(sums[way], CHIPS, circle.ways[way])  14.5 us
    ppermute x6, starting transfers between devices, step(): lax.ppermute(shard, CHIPS, way)  10.6 us
    all_to_all x1, starting transfers between devices, on_device(): got = lax.all_to_all(sent, ALL, split_axis=0, concat_axis=0, tiled=True)  4.98 us
  transfers between devices with their start and end apart: 34, of which 14 were waited for; matrix products, arithmetic and copies ran while one was open for 8% of the time, Pallas kernels for 21%

profile of v8, /device:TPU:0, one launch (start us, length us, event | category | flops | bytes accessed | tf_op | source)
XLA Modules:
  0.0 192.7 jit_solution(8711507796398595325)
XLA Ops:
  0.6 3.0 %collective-permute-start.1 = (bf16[128,2048]{1,0:T(8,128)(2,1)}, bf16[128,2048]{1,0:T(8,128)(2,1)S(1)}, u32[]{:S(2)}, u32[]{:S(2)}) collective-permute-start(bf16[128,2048]{1,0:T(8,128)(2,1)} %refs_4_.1), channel_id=1, source_target_pairs={{0,8},{1,0},{2,1},{3,2},{11,3},{10,11},{9,10},{8,9},{4,12},{5,4},{... | collective-permute-start | bytes 1572872 | tf_op jit(solution)/shard_map/ppermute | solution.py:250
  6.1 1.6 select_reduce_fusion
  8.6 2.9 %fusion.4 = bf16[2816,128]{1,0:T(8,128)(2,1)} fusion(s32[1024]{0:T(1024)S(1)} %get-tuple-element.138, bf16[128,8,128]{2,1,0:T(8,128)(2,1)S(1)} %copy-done), kind=kOutput, calls=%fused_computation.11 | convolution fusion | flops 741441536 | bytes 987136 | tf_op jit(solution)/shard_map/dot_general | solution.py:320
  12.2 3.7 %collective-permute-done.1.refs_1_ = bf16[128,2048]{1,0:T(8,128)(2,1)S(1)} collective-permute-done((bf16[128,2048]{1,0:T(8,128)(2,1)}, bf16[128,2048]{1,0:T(8,128)(2,1)S(1)}, u32[]{:S(2)}, u32[]{:S(2)}) %collective-permute-start.1) | collective-permute-done | bytes 524320 | tf_op jit(solution)/shard_map/ppermute | solution.py:250
  17.2 5.0 %all-to-all-start = ((bf16[16,176,128]{2,1,0:T(8,128)(2,1)}), bf16[16,176,128]{2,1,0:T(8,128)(2,1)S(1)}, u32[]{:S(2)}, u32[]{:S(2)}) async-start(bf16[16,176,128]{2,1,0:T(8,128)(2,1)} %maximum_dynamic-update-slice_fusion), calls=%async_computation | async-start | bytes 1441792 | tf_op jit(solution)/shard_map/all_to_all | solution.py:348
  22.8 1.7 collective-permute-start.4
  25.7 20.5 %collective-permute-done.4.refs_5_ = bf16[128,2048]{1,0:T(8,128)(2,1)} collective-permute-done((bf16[128,2048]{1,0:T(8,128)(2,1)S(1)}, bf16[128,2048]{1,0:T(8,128)(2,1)}, u32[]{:S(2)}, u32[]{:S(2)}) %collective-permute-start.4) | collective-permute-done | bytes 524320 | tf_op jit(solution)/shard_map/ppermute | solution.py:250
  47.3 1.8 fusion.2.pick_ref
  49.1 5.3 %collective-permute-start.8 = (bf16[128,2048]{1,0:T(8,128)(2,1)}, bf16[128,2048]{1,0:T(8,128)(2,1)S(1)}, u32[]{:S(2)}, u32[]{:S(2)}) collective-permute-start(bf16[128,2048]{1,0:T(8,128)(2,1)} %collective-permute-done.4.refs_5_), channel_id=1, source_target_pairs={{0,1},{1,2},{2,3},{3,11},{11,10},{10,9},{9,8},{8,0},{4,5},{5,6},{6... | collective-permute-start | bytes 1572872 | tf_op jit(solution)/shard_map/ppermute | solution.py:250
  54.4 2.0 %slice.28 = bf16[16,160,128]{2,1,0:T(8,128)(2,1)} slice(bf16[16,176,128]{2,1,0:T(8,128)(2,1)} %copy-done.11), slice={[0:16], [0:160], [0:128]} | slice | bytes 1310720 | tf_op jit(solution)/shard_map/slice | solution.py:364
  59.4 7.7 %place_0.1 = (bf16[640,2048]{1,0:T(8,128)(2,1)}, bf16[640,2048]{1,0:T(8,128)(2,1)}) custom-call(bf16[4,640,512]{2,1,0:T(8,128)(2,1)} %fusion.2.pick_ref, bf16[128,2048]{1,0:T(8,128)(2,1)S(1)} %collective-permute-done.refs_0_, bf16[128,2048]{1,0:T(8,128)(2,1)S(1)} %collective-permute-done.1.refs_1_, bf16[128,2048]{1,0:T(8,128)(2,1)} %collective-permute-done.2.refs_2_, ...), custom_call_target="tpu_custom_call" | custom-call | flops 2684354560 | bytes 10485760 | tf_op jit(solution)/shard_map/place_0/pallas_call | solution.py:386
  67.4 1.8 collective-permute-done.11.refs_0_
  69.3 2.0 %collective-permute-start.12 = (bf16[128,2048]{1,0:T(8,128)(2,1)S(1)}, bf16[128,2048]{1,0:T(8,128)(2,1)S(1)}, u32[]{:S(2)}, u32[]{:S(2)}) collective-permute-start(bf16[128,2048]{1,0:T(8,128)(2,1)S(1)} %broadcast_select_fusion), channel_id=1, source_target_pairs={{0,1},{1,2},{2,3},{3,11},{11,10},{10,9},{9,8},{8,0},{4,12},{5,4},{... | collective-permute-start | bytes 1572872 | tf_op jit(solution)/shard_map/ppermute | solution.py:265
  72.2 5.5 %place_2.1.refs_2_ = bf16[640,2048]{1,0:T(8,128)(2,1)} custom-call(bf16[4,640,512]{2,1,0:T(8,128)(2,1)} %fusion.2.pick_ref, bf16[128,2048]{1,0:T(8,128)(2,1)S(1)} %collective-permute-done.7.refs_0_, bf16[128,2048]{1,0:T(8,128)(2,1)S(1)} %collective-permute-done.8.refs_1_, bf16[128,2048]{1,0:T(8,128)(2,1)S(1)} %collective-permute-done.9.refs_2_, ...), custom_call_target="tpu_custom_call" | custom-call | flops 1342177280 | bytes 5242880 | tf_op jit(solution)/shard_map/place_2/pallas_call | solution.py:386
  78.8 1.9 collective-permute-done.14.refs_3_
  81.5 5.4 %place_3.1.refs_3_ = bf16[640,2048]{1,0:T(8,128)(2,1)} custom-call(bf16[4,640,512]{2,1,0:T(8,128)(2,1)} %fusion.2.pick_ref, bf16[128,2048]{1,0:T(8,128)(2,1)S(1)} %collective-permute-done.11.refs_0_, bf16[128,2048]{1,0:T(8,128)(2,1)S(1)} %collective-permute-done.12.refs_1_, bf16[128,2048]{1,0:T(8,128)(2,1)S(1)} %collective-permute-done.13.refs_2_, ...), custom_call_target="tpu_custom_call" | custom-call | flops 1342177280 | bytes 5242880 | tf_op jit(solution)/shard_map/place_3/pallas_call | solution.py:386
  86.9 36.2 %logits_and_back.1 = (bf16[128,2560]{1,0:T(8,128)(2,1)S(1)}, bf16[256,2176]{1,0:T(8,128)(2,1)}, bf16[256,2176]{1,0:T(8,128)(2,1)}, bf16[256,2176]{1,0:T(8,128)(2...) custom-call(f32[1]{0:T(128)} %bitcast.5.scale_ref, ...), custom_call_target="tpu_custom_call" | custom-call | flops 21474836480 | bytes 52428800 | tf_op jit(solution)/shard_map/logits_and_back/pallas_call | solution.py:427
  124.1 1.9 %collective-permute-done.16 = bf16[256,2176]{1,0:T(8,128)(2,1)S(1)} collective-permute-done((bf16[256,2176]{1,0:T(8,128)(2,1)}, bf16[256,2176]{1,0:T(8,128)(2,1)S(1)}, u32[]{:S(2)}, u32[]{:S(2)}) %collective-permute-start.16) | collective-permute-done | bytes 1114144 | tf_op jit(solution)/shard_map/ppermute | solution.py:467
  127.6 1.8 collective-permute-start.19
  129.9 2.8 %head_grad_0.1 = (bf16[10240,2048]{1,0:T(8,128)(2,1)}, f32[8,128]{1,0:T(8,128)}) custom-call(bf16[128,2560]{1,0:T(8,128)(2,1)S(1)} %get-tuple-element.129.grad_ref, bf16[640,2048]{1,0:T(8,128)(2,1)S(1)} %copy-done.4, bf16[640,2048]{1,0:T(8,128)(2,1)S(1)} %copy-done.5, bf16[640,2048]{1,0:T(8,128)(2,1)S(1)} %copy-done.2, bf16[640,2048]{1,0:T(8,128)(2,1)S(1)} %copy-done.3), custom_call_target="tpu_custom_call" | custom-call | flops 1533916928 | bytes 7489828 | tf_op jit(solution)/shard_map/head_grad_0/pallas_call | solution.py:488
  132.7 4.8 %collective-permute-done.20.refs_7_ = bf16[128,1024]{1,0:T(8,128)(2,1)S(1)} collective-permute-done((bf16[128,1024]{1,0:T(8,128)(2,1)S(1)}, bf16[128,1024]{1,0:T(8,128)(2,1)S(1)}, u32[]{:S(2)}, u32[]{:S(2)}) %collective-permute-start.20) | collective-permute-done | bytes 262176 | tf_op jit(solution)/shard_map/ppermute | solution.py:526
  140.0 4.1 %head_grad_1.1 = (bf16[10240,2048]{1,0:T(8,128)(2,1)}, f32[8,128]{1,0:T(8,128)}) custom-call(bf16[128,2560]{1,0:T(8,128)(2,1)S(1)} %get-tuple-element.129.grad_ref, bf16[640,2048]{1,0:T(8,128)(2,1)S(1)} %copy-done.4, bf16[640,2048]{1,0:T(8,128)(2,1)S(1)} %copy-done.5, bf16[640,2048]{1,0:T(8,128)(2,1)S(1)} %copy-done.2, ...), custom_call_target="tpu_custom_call", output_to_operand_aliasing={{0}: (5, {})} | custom-call | flops 1533916928 | bytes 7489828 | tf_op jit(solution)/shard_map/head_grad_1/pallas_call | solution.py:488
  144.1 2.1 %collective-permute-done.22.refs_7_ = bf16[128,1024]{1,0:T(8,128)(2,1)S(1)} collective-permute-done((bf16[128,1024]{1,0:T(8,128)(2,1)S(1)}, bf16[128,1024]{1,0:T(8,128)(2,1)S(1)}, u32[]{:S(2)}, u32[]{:S(2)}) %collective-permute-start.22) | collective-permute-done | bytes 262176 | tf_op jit(solution)/shard_map/ppermute | solution.py:526
  148.7 4.1 %head_grad_2.1 = (bf16[10240,2048]{1,0:T(8,128)(2,1)}, f32[8,128]{1,0:T(8,128)}) custom-call(bf16[128,2560]{1,0:T(8,128)(2,1)S(1)} %get-tuple-element.129.grad_ref, bf16[640,2048]{1,0:T(8,128)(2,1)S(1)} %copy-done.4, bf16[640,2048]{1,0:T(8,128)(2,1)S(1)} %copy-done.5, bf16[640,2048]{1,0:T(8,128)(2,1)S(1)} %copy-done.2, ...), custom_call_target="tpu_custom_call", output_to_operand_aliasing={{0}: (5, {})} | custom-call | flops 1533916928 | bytes 7489828 | tf_op jit(solution)/shard_map/head_grad_2/pallas_call | solution.py:488
  156.5 4.1 %head_grad_3.1 = (bf16[10240,2048]{1,0:T(8,128)(2,1)}, f32[8,128]{1,0:T(8,128)}) custom-call(bf16[128,2560]{1,0:T(8,128)(2,1)S(1)} %get-tuple-element.129.grad_ref, bf16[640,2048]{1,0:T(8,128)(2,1)S(1)} %copy-done.4, bf16[640,2048]{1,0:T(8,128)(2,1)S(1)} %copy-done.5, bf16[640,2048]{1,0:T(8,128)(2,1)S(1)} %copy-done.2, ...), custom_call_target="tpu_custom_call", output_to_operand_aliasing={{0}: (5, {})} | custom-call | flops 1533916928 | bytes 7489828 | tf_op jit(solution)/shard_map/head_grad_3/pallas_call | solution.py:488
  160.6 1.5 collective-permute-done.26.refs_7_
  162.5 1.9 %collective-permute-start.27 = (bf16[128,1152]{1,0:T(8,128)(2,1)S(1)}, bf16[128,1152]{1,0:T(8,128)(2,1)S(1)}, u32[]{:S(2)}, u32[]{:S(2)}) collective-permute-start(bf16[128,1152]{1,0:T(8,128)(2,1)S(1)} %get-tuple-element.113), channel_id=1, source_target_pairs={{0,1},{1,2},{2,3},{3,11},{11,10},{10,9},{9,8},{8,0},{4,5},{5,6},{6... | collective-permute-start | bytes 884744 | tf_op jit(solution)/shard_map/ppermute | solution.py:526
  164.6 4.1 %head_grad_4.1 = (bf16[10240,2048]{1,0:T(8,128)(2,1)}, f32[8,128]{1,0:T(8,128)}) custom-call(bf16[128,2560]{1,0:T(8,128)(2,1)S(1)} %get-tuple-element.129.grad_ref, bf16[640,2048]{1,0:T(8,128)(2,1)S(1)} %copy-done.4, bf16[640,2048]{1,0:T(8,128)(2,1)S(1)} %copy-done.5, bf16[640,2048]{1,0:T(8,128)(2,1)S(1)} %copy-done.2, ...), custom_call_target="tpu_custom_call", output_to_operand_aliasing={{0}: (5, {})} | custom-call | flops 1533916928 | bytes 7489828 | tf_op jit(solution)/shard_map/head_grad_4/pallas_call | solution.py:488
  168.7 3.9 %collective-permute-done.28.refs_7_ = bf16[128,1024]{1,0:T(8,128)(2,1)S(1)} collective-permute-done((bf16[128,1024]{1,0:T(8,128)(2,1)S(1)}, bf16[128,1024]{1,0:T(8,128)(2,1)S(1)}, u32[]{:S(2)}, u32[]{:S(2)}) %collective-permute-start.28) | collective-permute-done | bytes 262176 | tf_op jit(solution)/shard_map/ppermute | solution.py:526
  175.1 4.1 %head_grad_5.1 = (bf16[10240,2048]{1,0:T(8,128)(2,1)}, f32[8,128]{1,0:T(8,128)}) custom-call(bf16[128,2560]{1,0:T(8,128)(2,1)S(1)} %get-tuple-element.129.grad_ref, bf16[640,2048]{1,0:T(8,128)(2,1)S(1)} %copy-done.4, bf16[640,2048]{1,0:T(8,128)(2,1)S(1)} %copy-done.5, bf16[640,2048]{1,0:T(8,128)(2,1)S(1)} %copy-done.2, ...), custom_call_target="tpu_custom_call", output_to_operand_aliasing={{0}: (5, {})} | custom-call | flops 1533916928 | bytes 7489828 | tf_op jit(solution)/shard_map/head_grad_5/pallas_call | solution.py:488
  179.2 4.0 %collective-permute-done.30.refs_7_ = bf16[128,1024]{1,0:T(8,128)(2,1)S(1)} collective-permute-done((bf16[128,1024]{1,0:T(8,128)(2,1)S(1)}, bf16[128,1024]{1,0:T(8,128)(2,1)S(1)}, u32[]{:S(2)}, u32[]{:S(2)}) %collective-permute-start.30) | collective-permute-done | bytes 262176 | tf_op jit(solution)/shard_map/ppermute | solution.py:526
  185.6 4.1 %head_grad_6.1 = (bf16[10240,2048]{1,0:T(8,128)(2,1)}, f32[8,128]{1,0:T(8,128)}) custom-call(bf16[128,2560]{1,0:T(8,128)(2,1)S(1)} %get-tuple-element.129.grad_ref, bf16[640,2048]{1,0:T(8,128)(2,1)S(1)} %copy-done.4, bf16[640,2048]{1,0:T(8,128)(2,1)S(1)} %copy-done.5, bf16[640,2048]{1,0:T(8,128)(2,1)S(1)} %copy-done.2, ...), custom_call_target="tpu_custom_call", output_to_operand_aliasing={{0}: (5, {})} | custom-call | flops 1533916928 | bytes 7489828 | tf_op jit(solution)/shard_map/head_grad_6/pallas_call | solution.py:488
  (125 shorter events, 33.7 us)
Async XLA Ops:
  0.6 15.2 %collective-permute-start.1 = (bf16[128,2048]{1,0:T(8,128)(2,1)}, bf16[128,2048]{1,0:T(8,128)(2,1)S(1)}, u32[]{:S(2)}, u32[]{:S(2)}) collective-permute-start(bf16[128,2048]{1,0:T(8,128)(2,1)} %refs_4_.1), channel_id=1, source_target_pairs={{0,8},{1,0},{2,1},{3,2},{11,3},{10,11},{9,10},{8,9},{4,12},{5,4},{... | collective-permute-start | bytes 1572872 | tf_op jit(solution)/shard_map/ppermute | solution.py:250
  3.6 13.6 %collective-permute-start = (bf16[128,2048]{1,0:T(8,128)(2,1)}, bf16[128,2048]{1,0:T(8,128)(2,1)S(1)}, u32[]{:S(2)}, u32[]{:S(2)}) collective-permute-start(bf16[128,2048]{1,0:T(8,128)(2,1)} %refs_4_.1), channel_id=1, source_target_pairs={{0,1},{1,2},{2,3},{3,11},{11,10},{10,9},{9,8},{8,0},{4,5},{5,6},{6... | collective-permute-start | bytes 1572872 | tf_op jit(solution)/shard_map/ppermute | solution.py:250
  17.2 28.9 %all-to-all-start = ((bf16[16,176,128]{2,1,0:T(8,128)(2,1)}), bf16[16,176,128]{2,1,0:T(8,128)(2,1)S(1)}, u32[]{:S(2)}, u32[]{:S(2)}) async-start(bf16[16,176,128]{2,1,0:T(8,128)(2,1)} %maximum_dynamic-update-slice_fusion), calls=%async_computation | async-start | bytes 1441792 | tf_op jit(solution)/shard_map/all_to_all | solution.py:348
  22.2 32.2 %collective-permute-start.5 = (bf16[128,2048]{1,0:T(8,128)(2,1)}, bf16[128,2048]{1,0:T(8,128)(2,1)}, u32[]{:S(2)}, u32[]{:S(2)}) collective-permute-start(bf16[128,2048]{1,0:T(8,128)(2,1)} %refs_4_.1), channel_id=1, source_target_pairs={{0,4},{4,0},{1,5},{5,1},{2,6},{6,2},{3,7},{7,3},{8,12},{12,8},{9,1... | collective-permute-start | bytes 1572872 | tf_op jit(solution)/shard_map/ppermute | solution.py:245
  22.8 23.3 %collective-permute-start.4 = (bf16[128,2048]{1,0:T(8,128)(2,1)S(1)}, bf16[128,2048]{1,0:T(8,128)(2,1)}, u32[]{:S(2)}, u32[]{:S(2)}) collective-permute-start(bf16[128,2048]{1,0:T(8,128)(2,1)S(1)} %collective-permute-done.refs_0_), channel_id=1, source_target_pairs={{0,1},{1,2},{2,3},{3,11},{11,10},{10,9},{9,8},{8,0},{4,5},{5,6},{6... | collective-permute-start | bytes 1572872 | tf_op jit(solution)/shard_map/ppermute | solution.py:250
  24.8 24.3 %collective-permute-start.7 = (bf16[128,2048]{1,0:T(8,128)(2,1)S(1)}, bf16[128,2048]{1,0:T(8,128)(2,1)S(1)}, u32[]{:S(2)}, u32[]{:S(2)}) collective-permute-start(bf16[128,2048]{1,0:T(8,128)(2,1)S(1)} %collective-permute-done.1.refs_1_), channel_id=1, source_target_pairs={{0,8},{1,0},{2,1},{3,2},{11,3},{10,11},{9,10},{8,9},{4,12},{5,4},{... | collective-permute-start | bytes 1572872 | tf_op jit(solution)/shard_map/ppermute | solution.py:250
  25.2 33.9 %collective-permute-start.3 = (bf16[128,2048]{1,0:T(8,128)(2,1)S(1)}, bf16[128,2048]{1,0:T(8,128)(2,1)}, u32[]{:S(2)}, u32[]{:S(2)}) collective-permute-start(bf16[128,2048]{1,0:T(8,128)(2,1)S(1)} %collective-permute-done.1.refs_1_), channel_id=1, source_target_pairs={{0,4},{4,0},{1,5},{5,1},{2,6},{6,2},{3,7},{7,3},{8,12},{12,8},{9,1... | collective-permute-start | bytes 1572872 | tf_op jit(solution)/shard_map/ppermute | solution.py:245
  25.2 34.2 %collective-permute-start.2 = (bf16[128,2048]{1,0:T(8,128)(2,1)S(1)}, bf16[128,2048]{1,0:T(8,128)(2,1)}, u32[]{:S(2)}, u32[]{:S(2)}) collective-permute-start(bf16[128,2048]{1,0:T(8,128)(2,1)S(1)} %collective-permute-done.refs_0_), channel_id=1, source_target_pairs={{0,4},{4,0},{1,5},{5,1},{2,6},{6,2},{3,7},{7,3},{8,12},{12,8},{9,1... | collective-permute-start | bytes 1572872 | tf_op jit(solution)/shard_map/ppermute | solution.py:245
  46.1 13.2 %collective-permute-start.6 = (bf16[128,2048]{1,0:T(8,128)(2,1)}, bf16[128,2048]{1,0:T(8,128)(2,1)}, u32[]{:S(2)}, u32[]{:S(2)}) collective-permute-start(bf16[128,2048]{1,0:T(8,128)(2,1)} %collective-permute-done.4.refs_5_), channel_id=1, source_target_pairs={{0,4},{4,0},{1,5},{5,1},{2,6},{6,2},{3,7},{7,3},{8,12},{12,8},{9,1... | collective-permute-start | bytes 1572872 | tf_op jit(solution)/shard_map/ppermute | solution.py:245
  49.1 17.9 %collective-permute-start.8 = (bf16[128,2048]{1,0:T(8,128)(2,1)}, bf16[128,2048]{1,0:T(8,128)(2,1)S(1)}, u32[]{:S(2)}, u32[]{:S(2)}) collective-permute-start(bf16[128,2048]{1,0:T(8,128)(2,1)} %collective-permute-done.4.refs_5_), channel_id=1, source_target_pairs={{0,1},{1,2},{2,3},{3,11},{11,10},{10,9},{9,8},{8,0},{4,5},{5,6},{6... | collective-permute-start | bytes 1572872 | tf_op jit(solution)/shard_map/ppermute | solution.py:250
  54.4 14.8 %collective-permute-start.11 = (bf16[128,2048]{1,0:T(8,128)(2,1)S(1)}, bf16[128,2048]{1,0:T(8,128)(2,1)S(1)}, u32[]{:S(2)}, u32[]{:S(2)}) collective-permute-start(bf16[128,2048]{1,0:T(8,128)(2,1)S(1)} %collective-permute-done.7.refs_0_), channel_id=1, source_target_pairs={{0,8},{1,0},{2,1},{3,2},{11,3},{10,11},{9,10},{8,9},{4,12},{5,4},{... | collective-permute-start | bytes 1572872 | tf_op jit(solution)/shard_map/ppermute | solution.py:250
  59.1 12.3 %collective-permute-start.9 = (bf16[128,2048]{1,0:T(8,128)(2,1)S(1)}, bf16[128,2048]{1,0:T(8,128)(2,1)S(1)}, u32[]{:S(2)}, u32[]{:S(2)}) collective-permute-start(bf16[128,2048]{1,0:T(8,128)(2,1)S(1)} %collective-permute-done.7.refs_0_), channel_id=1, source_target_pairs={{0,4},{4,0},{1,5},{5,1},{2,6},{6,2},{3,7},{7,3},{8,12},{12,8},{9,1... | collective-permute-start | bytes 1572872 | tf_op jit(solution)/shard_map/ppermute | solution.py:245
  67.0 4.4 %collective-permute-start.10 = (bf16[128,2048]{1,0:T(8,128)(2,1)S(1)}, bf16[128,2048]{1,0:T(8,128)(2,1)S(1)}, u32[]{:S(2)}, u32[]{:S(2)}) collective-permute-start(bf16[128,2048]{1,0:T(8,128)(2,1)S(1)} %collective-permute-done.8.refs_1_), channel_id=1, source_target_pairs={{0,4},{4,0},{1,5},{5,1},{2,6},{6,2},{3,7},{7,3},{8,12},{12,8},{9,1... | collective-permute-start | bytes 1572872 | tf_op jit(solution)/shard_map/ppermute | solution.py:245
  69.3 9.4 %collective-permute-start.12 = (bf16[128,2048]{1,0:T(8,128)(2,1)S(1)}, bf16[128,2048]{1,0:T(8,128)(2,1)S(1)}, u32[]{:S(2)}, u32[]{:S(2)}) collective-permute-start(bf16[128,2048]{1,0:T(8,128)(2,1)S(1)} %broadcast_select_fusion), channel_id=1, source_target_pairs={{0,1},{1,2},{2,3},{3,11},{11,10},{10,9},{9,8},{8,0},{4,12},{5,4},{... | collective-permute-start | bytes 1572872 | tf_op jit(solution)/shard_map/ppermute | solution.py:265
  71.3 7.4 %collective-permute-start.13 = (bf16[128,2048]{1,0:T(8,128)(2,1)S(1)}, bf16[128,2048]{1,0:T(8,128)(2,1)S(1)}, u32[]{:S(2)}, u32[]{:S(2)}) collective-permute-start(bf16[128,2048]{1,0:T(8,128)(2,1)S(1)} %collective-permute-done.11.refs_0_), channel_id=1, source_target_pairs={{0,4},{4,0},{1,5},{5,1},{2,6},{6,2},{3,7},{7,3},{8,12},{12,8},{9,1... | collective-permute-start | bytes 1572872 | tf_op jit(solution)/shard_map/ppermute | solution.py:245
  123.3 14.2 %collective-permute-start.15 = (bf16[256,2176]{1,0:T(8,128)(2,1)}, bf16[256,2176]{1,0:T(8,128)(2,1)S(1)}, u32[]{:S(2)}, u32[]{:S(2)}) collective-permute-start(bf16[256,2176]{1,0:T(8,128)(2,1)} %get-tuple-element.78), channel_id=1, source_target_pairs={{0,4},{4,0},{1,5},{5,1},{2,6},{6,2},{3,7},{7,3},{8,12},{12,8},{9,1... | collective-permute-start | bytes 3342344 | tf_op jit(solution)/shard_map/ppermute | solution.py:467
  123.6 13.9 %collective-permute-start.17 = (bf16[256,2176]{1,0:T(8,128)(2,1)}, bf16[256,2176]{1,0:T(8,128)(2,1)S(1)}, u32[]{:S(2)}, u32[]{:S(2)}) collective-permute-start(bf16[256,2176]{1,0:T(8,128)(2,1)} %get-tuple-element.82), channel_id=1, source_target_pairs={{0,4},{4,0},{1,5},{5,1},{2,6},{6,2},{3,7},{7,3},{8,12},{12,8},{9,1... | collective-permute-start | bytes 3342344 | tf_op jit(solution)/shard_map/ppermute | solution.py:467
  123.8 22.4 %collective-permute-start.18 = (bf16[256,2176]{1,0:T(8,128)(2,1)}, bf16[256,2176]{1,0:T(8,128)(2,1)S(1)}, u32[]{:S(2)}, u32[]{:S(2)}) collective-permute-start(bf16[256,2176]{1,0:T(8,128)(2,1)} %get-tuple-element.84), channel_id=1, source_target_pairs={{0,4},{4,0},{1,5},{5,1},{2,6},{6,2},{3,7},{7,3},{8,12},{12,8},{9,1... | collective-permute-start | bytes 3342344 | tf_op jit(solution)/shard_map/ppermute | solution.py:467
  127.6 9.9 %collective-permute-start.19 = (bf16[128,1152]{1,0:T(8,128)(2,1)S(1)}, bf16[128,1152]{1,0:T(8,128)(2,1)S(1)}, u32[]{:S(2)}, u32[]{:S(2)}) collective-permute-start(bf16[128,1152]{1,0:T(8,128)(2,1)S(1)} %get-tuple-element.85), channel_id=1, source_target_pairs={{0,1},{1,2},{2,3},{3,11},{11,10},{10,9},{9,8},{8,0},{4,5},{5,6},{6... | collective-permute-start | bytes 884744 | tf_op jit(solution)/shard_map/ppermute | solution.py:526
  129.4 8.1 %collective-permute-start.20 = (bf16[128,1024]{1,0:T(8,128)(2,1)S(1)}, bf16[128,1024]{1,0:T(8,128)(2,1)S(1)}, u32[]{:S(2)}, u32[]{:S(2)}) collective-permute-start(bf16[128,1024]{1,0:T(8,128)(2,1)S(1)} %get-tuple-element.87), channel_id=1, source_target_pairs={{0,8},{1,0},{2,1},{3,2},{11,3},{10,11},{9,10},{8,9},{4,12},{5,4},{... | collective-permute-start | bytes 786440 | tf_op jit(solution)/shard_map/ppermute | solution.py:526
  137.9 8.3 %collective-permute-start.21 = (bf16[128,1152]{1,0:T(8,128)(2,1)S(1)}, bf16[128,1152]{1,0:T(8,128)(2,1)S(1)}, u32[]{:S(2)}, u32[]{:S(2)}) collective-permute-start(bf16[128,1152]{1,0:T(8,128)(2,1)S(1)} %get-tuple-element.92), channel_id=1, source_target_pairs={{0,1},{1,2},{2,3},{3,11},{11,10},{10,9},{9,8},{8,0},{4,5},{5,6},{6... | collective-permute-start | bytes 884744 | tf_op jit(solution)/shard_map/ppermute | solution.py:526
  139.0 7.2 %collective-permute-start.22 = (bf16[128,1024]{1,0:T(8,128)(2,1)S(1)}, bf16[128,1024]{1,0:T(8,128)(2,1)S(1)}, u32[]{:S(2)}, u32[]{:S(2)}) collective-permute-start(bf16[128,1024]{1,0:T(8,128)(2,1)S(1)} %get-tuple-element.93), channel_id=1, source_target_pairs={{0,8},{1,0},{2,1},{3,2},{11,3},{10,11},{9,10},{8,9},{4,12},{5,4},{... | collective-permute-start | bytes 786440 | tf_op jit(solution)/shard_map/ppermute | solution.py:526
  146.6 7.4 %collective-permute-start.23 = (bf16[128,1152]{1,0:T(8,128)(2,1)S(1)}, bf16[128,1152]{1,0:T(8,128)(2,1)S(1)}, u32[]{:S(2)}, u32[]{:S(2)}) collective-permute-start(bf16[128,1152]{1,0:T(8,128)(2,1)S(1)} %get-tuple-element.99), channel_id=1, source_target_pairs={{0,1},{1,2},{2,3},{3,11},{11,10},{10,9},{9,8},{8,0},{4,5},{5,6},{6... | collective-permute-start | bytes 884744 | tf_op jit(solution)/shard_map/ppermute | solution.py:526
  147.6 6.4 %collective-permute-start.24 = (bf16[128,1024]{1,0:T(8,128)(2,1)S(1)}, bf16[128,1024]{1,0:T(8,128)(2,1)S(1)}, u32[]{:S(2)}, u32[]{:S(2)}) collective-permute-start(bf16[128,1024]{1,0:T(8,128)(2,1)S(1)} %get-tuple-element.100), channel_id=1, source_target_pairs={{0,8},{1,0},{2,1},{3,2},{11,3},{10,11},{9,10},{8,9},{4,12},{5,4},{... | collective-permute-start | bytes 786440 | tf_op jit(solution)/shard_map/ppermute | solution.py:526
  154.4 7.7 %collective-permute-start.25 = (bf16[128,1152]{1,0:T(8,128)(2,1)S(1)}, bf16[128,1152]{1,0:T(8,128)(2,1)S(1)}, u32[]{:S(2)}, u32[]{:S(2)}) collective-permute-start(bf16[128,1152]{1,0:T(8,128)(2,1)S(1)} %get-tuple-element.106), channel_id=1, source_target_pairs={{0,1},{1,2},{2,3},{3,11},{11,10},{10,9},{9,8},{8,0},{4,5},{5,6},{6... | collective-permute-start | bytes 884744 | tf_op jit(solution)/shard_map/ppermute | solution.py:526
  155.5 6.6 %collective-permute-start.26 = (bf16[128,1024]{1,0:T(8,128)(2,1)S(1)}, bf16[128,1024]{1,0:T(8,128)(2,1)S(1)}, u32[]{:S(2)}, u32[]{:S(2)}) collective-permute-start(bf16[128,1024]{1,0:T(8,128)(2,1)S(1)} %get-tuple-element.107), channel_id=1, source_target_pairs={{0,8},{1,0},{2,1},{3,2},{11,3},{10,11},{9,10},{8,9},{4,12},{5,4},{... | collective-permute-start | bytes 786440 | tf_op jit(solution)/shard_map/ppermute | solution.py:526
  162.5 10.1 %collective-permute-start.27 = (bf16[128,1152]{1,0:T(8,128)(2,1)S(1)}, bf16[128,1152]{1,0:T(8,128)(2,1)S(1)}, u32[]{:S(2)}, u32[]{:S(2)}) collective-permute-start(bf16[128,1152]{1,0:T(8,128)(2,1)S(1)} %get-tuple-element.113), channel_id=1, source_target_pairs={{0,1},{1,2},{2,3},{3,11},{11,10},{10,9},{9,8},{8,0},{4,5},{5,6},{6... | collective-permute-start | bytes 884744 | tf_op jit(solution)/shard_map/ppermute | solution.py:526
  164.4 8.1 %collective-permute-start.28 = (bf16[128,1024]{1,0:T(8,128)(2,1)S(1)}, bf16[128,1024]{1,0:T(8,128)(2,1)S(1)}, u32[]{:S(2)}, u32[]{:S(2)}) collective-permute-start(bf16[128,1024]{1,0:T(8,128)(2,1)S(1)} %get-tuple-element.114), channel_id=1, source_target_pairs={{0,8},{1,0},{2,1},{3,2},{11,3},{10,11},{9,10},{8,9},{4,12},{5,4},{... | collective-permute-start | bytes 786440 | tf_op jit(solution)/shard_map/ppermute | solution.py:526
  173.0 10.2 %collective-permute-start.29 = (bf16[128,1152]{1,0:T(8,128)(2,1)S(1)}, bf16[128,1152]{1,0:T(8,128)(2,1)S(1)}, u32[]{:S(2)}, u32[]{:S(2)}) collective-permute-start(bf16[128,1152]{1,0:T(8,128)(2,1)S(1)} %get-tuple-element.120), channel_id=1, source_target_pairs={{0,1},{1,2},{2,3},{3,11},{11,10},{10,9},{9,8},{8,0},{4,5},{5,6},{6... | collective-permute-start | bytes 884744 | tf_op jit(solution)/shard_map/ppermute | solution.py:526
  174.4 8.7 %collective-permute-start.30 = (bf16[128,1024]{1,0:T(8,128)(2,1)S(1)}, bf16[128,1024]{1,0:T(8,128)(2,1)S(1)}, u32[]{:S(2)}, u32[]{:S(2)}) collective-permute-start(bf16[128,1024]{1,0:T(8,128)(2,1)S(1)} %get-tuple-element.121), channel_id=1, source_target_pairs={{0,8},{1,0},{2,1},{3,2},{11,3},{10,11},{9,10},{8,9},{4,12},{5,4},{... | collective-permute-start | bytes 786440 | tf_op jit(solution)/shard_map/ppermute | solution.py:526
  183.5 7.4 %collective-permute-start.31 = (bf16[128,1152]{1,0:T(8,128)(2,1)S(1)}, bf16[128,1152]{1,0:T(8,128)(2,1)S(1)}, u32[]{:S(2)}, u32[]{:S(2)}) collective-permute-start(bf16[128,1152]{1,0:T(8,128)(2,1)S(1)} %get-tuple-element.127), channel_id=1, source_target_pairs={{0,1},{1,2},{2,3},{3,11},{11,10},{10,9},{9,8},{8,0},{4,5},{5,6},{6... | collective-permute-start | bytes 884744 | tf_op jit(solution)/shard_map/ppermute | solution.py:526
  184.6 6.4 %collective-permute-start.32 = (bf16[128,1024]{1,0:T(8,128)(2,1)S(1)}, bf16[128,1024]{1,0:T(8,128)(2,1)S(1)}, u32[]{:S(2)}, u32[]{:S(2)}) collective-permute-start(bf16[128,1024]{1,0:T(8,128)(2,1)S(1)} %get-tuple-element.128), channel_id=1, source_target_pairs={{0,8},{1,0},{2,1},{3,2},{11,3},{10,11},{9,10},{8,9},{4,12},{5,4},{... | collective-permute-start | bytes 786440 | tf_op jit(solution)/shard_map/ppermute | solution.py:526
  (17 other events, 159.1 us)
